TPU v7x, 32 devices: a whole 2x2x4 slice. The times are simulated.
32 devices in a mesh: freq: 4 (over y, x), mx: 2 (over core), my: 4 (over z).
Axes of the slice: x: 2, y: 2, z: 4, core: 2. Of those that a mesh axis runs over, the one named last changes fastest.
Arguments:
- adjoint_rhs: float32 [4, 2, 3, 128, 1024], P('freq', None, None, 'mx', 'my'), may hold values from -4 to 6
- state: bfloat16 [4, 2, 3, 128, 1024], P('freq', None, None, 'mx', 'my'), may hold values from -1.5 to 1.5
- density: float32 [128, 1024], P('mx', 'my'), may hold values from 0.85 to 1
- stiffness: float32 [128, 1024], P('mx', 'my'), may hold values from 1.5 to 4
- mass: float32 [128, 1024], P('mx', 'my'), may hold values from 0.2 to 1
- omega: float32 [4], P('freq'), may hold values from 0.15 to 0.45
- send_rows: int32 [8, 256], P(('mx', 'my')), may hold values from 0 to 16383, as said below
- recv_rows: int32 [8, 256], P(('mx', 'my')), may hold values from 0 to 16383, as said below
- mortar_weight: float32 [8, 256], P(('mx', 'my')), may hold values from 0 to 1.5, as said below
Outputs:
- adjoint: float32 [4, 2, 3, 128, 1024], P('freq', None, None, 'mx', 'my')
- filtered_sensitivity: float32 [128, 1024], P('mx', 'my')
Inputs may be any that keep to these rules, and one draw needn't show every extreme that they name: `send_rows`: a local cell of the sending device; slots past the live count of a device pair hold 0. `recv_rows`: a local cell of the receiving device; empty slots hold 0. Live slots of a pair come first, up to 32 of them. `mortar_weight`: zero exactly in empty slots, at least 0.5 in live ones; every receiving device has a source device with all 32 slots live.
All inputs are finite; a program needn't handle non-finite values.
Results may differ from a plain program's by a relative error of at most 0.0003.
Values may be sent and summed in bfloat16 or wider, within the bound.
No kernel may reach another device: no remote copies, remote signals or barrier semaphores. Data moves between devices by JAX's collectives and lax.ppermute only.
A program may use at most 64 MiB of HBM per device.

v0:
```python
import jax
import jax.numpy as jnp
from jax import lax
from jax.sharding import PartitionSpec as P

ITERS = 20


def extended(x, sides, width):
    for axis, dim in sides:
        size, length = (lax.axis_size(axis), x.shape[dim])
        up = [(i, (i + 1) % size) for i in range(size - 1)]
        down = [(j, i) for i, j in up]
        last = lax.slice_in_dim(x, length - width, length, axis=dim)
        first = lax.slice_in_dim(x, 0, width, axis=dim)
        before = lax.ppermute(last, axis, up)
        after = lax.ppermute(first, axis, down)
        x = jnp.concatenate([before, x, after], axis=dim)
    return x


def on_device(
    adjoint_rhs, state, density, stiffness, mass, omega, send_rows, recv_rows, mortar_weight
):
    rows_x, rows_y = density.shape
    cells = rows_x * rows_y
    w = omega[0]
    stiff = density**3 * stiffness
    dstiff = 3.0 * density**2 * stiffness
    rmass = density * mass
    sources = send_rows[0]
    targets = recv_rows[0]
    weights = mortar_weight[0]
    mdiag = jnp.zeros((cells,), jnp.float32).at[targets].add(weights).reshape(rows_x, rows_y)
    real_d = 4.4 * stiff + 0.3 + mdiag - w * w * rmass
    imag_d = 0.2 * w * (stiff + rmass)
    den = real_d * real_d + imag_d * imag_d
    rhs = adjoint_rhs.reshape(6, rows_x, rows_y)

    def mortar(field):
        sent = field.reshape(6, cells)[:, sources]
        got = lax.all_to_all(sent, ("mx", "my"), split_axis=1, concat_axis=1, tiled=True)
        added = jnp.zeros((6, cells), jnp.float32).at[:, targets].add(got * weights)
        return added.reshape(6, rows_x, rows_y)

    def sweep(step, field):
        padded = extended(field, (("mx", 1), ("my", 2)), 1)
        beside = (
            padded[:, 2:, 1:-1] + padded[:, :-2, 1:-1] + padded[:, 1:-1, 2:] + padded[:, 1:-1, :-2]
        )
        h = rhs + stiff * beside + mortar(field)
        new_re = (h[:3] * real_d + h[3:] * imag_d) / den
        new_im = (h[3:] * real_d - h[:3] * imag_d) / den
        return jnp.concatenate([new_re, new_im], axis=0)

    field = lax.fori_loop(0, ITERS, sweep, jnp.zeros((6, rows_x, rows_y), jnp.float32))
    state_six = state.reshape(6, rows_x, rows_y)
    state_pad = extended(state_six, (("mx", 1), ("my", 2)), 1).astype(jnp.float32)
    u = state_six.astype(jnp.float32)
    nb = (
        state_pad[:, 2:, 1:-1]
        + state_pad[:, :-2, 1:-1]
        + state_pad[:, 1:-1, 2:]
        + state_pad[:, 1:-1, :-2]
    )
    da = 4.4 * dstiff - w * w * mass
    db = 0.2 * w * (dstiff + mass)
    t_re = da * u[:3] - db * u[3:] - dstiff * nb[:3]
    t_im = da * u[3:] + db * u[:3] - dstiff * nb[3:]
    sens = -jnp.sum(field[:3] * t_re - field[3:] * t_im, axis=0)
    total = lax.psum(sens, "freq")
    weighted = extended(density * total, (("mx", 0), ("my", 1)), 1)
    filt = weighted[1:-1, 1:-1]
    filt = filt + 0.5 * (
        weighted[2:, 1:-1] + weighted[:-2, 1:-1] + weighted[1:-1, 2:] + weighted[1:-1, :-2]
    )
    filt = filt + 0.25 * (
        weighted[2:, 2:] + weighted[:-2, :-2] + weighted[2:, :-2] + weighted[:-2, 2:]
    )
    return (field.reshape(1, 2, 3, rows_x, rows_y), filt / (4.0 * density))


def solution(mesh):
    return jax.shard_map(
        on_device,
        mesh=mesh,
        in_specs=(
            P("freq", None, None, "mx", "my"),
            P("freq", None, None, "mx", "my"),
            P("mx", "my"),
            P("mx", "my"),
            P("mx", "my"),
            P("freq"),
            P(("mx", "my"), None),
            P(("mx", "my"), None),
            P(("mx", "my"), None),
        ),
        out_specs=(P("freq", None, None, "mx", "my"), P("mx", "my")),
        check_vma=False,
    )
```

profile of v0, /device:TPU:8, one launch (start us, length us, event | category | flops | bytes accessed | tf_op | source)
XLA Modules:
  0.0 868.6 jit_solution(16920527046503184683)
XLA Ops:
  29.1 773.2 %while.10 = (s32[]{:T(128)}, f32[6,64,256]{2,1,0:T(8,128)S(1)}, f32[64,256]{1,0:T(8,128)S(1)}, f32[6,64,256]{2,1,0:T(8,128)}, s32[256]{0:T(256)}, /*index=5*/s32...) while((s32[]{:T(128)}, f32[6,64,256]{2,1,0:T(8,128)S(1)}, ...), condition=%wide.region_3.0_spmd, body=%wide.region_1.0_spmd.sunk | while | flops 2076162 | bytes 8023133 | solution.py:56
  38.8 5.8 all-to-all-start
  57.3 5.3 scatter_custom_fusion.7
  62.6 5.3 copy.35
  68.4 4.7 copy.31
  78.1 5.1 all-to-all-start
  95.9 5.3 scatter_custom_fusion.7
  101.2 5.3 copy.35
  116.7 5.1 all-to-all-start
  134.5 5.3 scatter_custom_fusion.7
  139.8 5.3 copy.35
  145.7 4.7 copy.31
  155.3 5.1 all-to-all-start
  173.1 5.3 scatter_custom_fusion.7
  178.4 5.3 copy.35
  194.0 5.1 all-to-all-start
  211.8 5.3 scatter_custom_fusion.7
  217.1 5.3 copy.35
  232.6 5.1 all-to-all-start
  250.4 5.3 scatter_custom_fusion.7
  255.7 5.3 copy.35
  271.2 5.1 all-to-all-start
  289.0 5.3 scatter_custom_fusion.7
  294.3 5.3 copy.35
  309.8 5.1 all-to-all-start
  327.6 5.3 scatter_custom_fusion.7
  332.9 5.3 copy.35
  348.5 5.1 all-to-all-start
  366.3 5.3 scatter_custom_fusion.7
  371.6 5.3 copy.35
  387.1 5.1 all-to-all-start
  404.9 5.3 scatter_custom_fusion.7
  410.2 5.3 copy.35
  425.7 5.1 all-to-all-start
  443.5 5.3 scatter_custom_fusion.7
  448.8 5.3 copy.35
  464.3 5.1 all-to-all-start
  482.1 5.3 scatter_custom_fusion.7
  487.4 5.3 copy.35
  503.0 5.1 all-to-all-start
  520.8 5.3 scatter_custom_fusion.7
  526.0 5.3 copy.35
  541.6 5.1 all-to-all-start
  559.4 5.3 scatter_custom_fusion.7
  564.7 5.3 copy.35
  580.2 5.1 all-to-all-start
  598.0 5.3 scatter_custom_fusion.7
  603.3 5.3 copy.35
  618.8 5.1 all-to-all-start
  636.6 5.3 scatter_custom_fusion.7
  641.9 5.3 copy.35
  657.5 5.1 all-to-all-start
  675.2 5.3 scatter_custom_fusion.7
  680.5 5.3 copy.35
  696.1 5.1 all-to-all-start
  713.9 5.3 scatter_custom_fusion.7
  719.2 5.3 copy.35
  734.7 5.1 all-to-all-start
  752.5 5.3 scatter_custom_fusion.7
  757.8 5.3 copy.35
  773.3 5.1 all-to-all-start
  791.1 5.3 scatter_custom_fusion.7
  796.4 5.3 copy.35
  803.0 42.5 %all-reduce.2.cloned.1.call-done = f32[64,256]{1,0:T(8,128)} async-done(((f32[64,256]{1,0:T(8,128)}), f32[64,256]{1,0:T(8,128)}) %all-reduce.2.cloned.1.call-update) | async-done | bytes 65552 | tf_op jit(solution)/shard_map/psum | solution.py:71
  (780 shorter events, 484.1 us)
Async XLA Ops:
  7.2 838.4 %all-reduce.2.cloned.1.call-start = ((), (), s32[]{:S(2)}) async-start(), calls=%async_computation.1 | async-start | bytes 131072 | tf_op jit(solution)/shard_map/psum | solution.py:71
  8.0 9.8 %collective-permute-start.5 = (bf16[6,1,256]{2,1,0:T(2,128)(2,1)S(1)}, bf16[6,1,256]{2,1,0:T(2,128)(2,1)S(1)}, u32[]{:S(2)}, u32[]{:S(2)}) collective-permute-start(bf16[6,1,256]{2,1,0:T(2,128)(2,1)S(1)} %get-tuple-element.104), channel_id=1, source_target_pairs={{4,0},{5,1},{6,2},{7,3},{12,8},{13,9},{14,10},{15,11},{20,16},{21,... | collective-permute-start | bytes 9224 | tf_op jit(solution)/shard_map/ppermute | solution.py:17
  9.3 8.5 collective-permute-start.4
  18.9 6.7 collective-permute-start.7
  38.8 17.0 %all-to-all-start = ((f32[8,1,192]{2,1,0:T(1,128)}), f32[8,1,192]{2,1,0:T(1,128)S(1)}, u32[]{:S(2)}, u32[]{:S(2)}) async-start(f32[8,1,192]{2,1,0:T(1,128)} %reshape.136), calls=%async_computation | async-start | bytes 16384 | tf_op jit(solution)/shard_map/while/body/eval_jaxpr/all_to_all | solution.py:42
  49.9 18.0 %collective-permute-start.2 = (f32[6,66,1]{2,1,0:T(8,128)S(1)}, f32[6,66,1]{2,1,0:T(8,128)S(1)}, u32[]{:S(2)}, u32[]{:S(2)}) collective-permute-start(f32[6,66,1]{2,1,0:T(8,128)S(1)} %get-tuple-element.180), channel_id=1, source_target_pairs={{0,1},{1,2},{2,3},{4,5},{5,6},{6,7},{8,9},{9,10},{10,11},{12,13},{... | collective-permute-start | bytes 4760 | tf_op jit(solution)/shard_map/while/body/eval_jaxpr/ppermute | solution.py:16
  53.3 14.6 %collective-permute-start.3 = (f32[6,66,1]{2,1,0:T(8,128)S(1)}, f32[6,66,1]{2,1,0:T(8,128)S(1)}, u32[]{:S(2)}, u32[]{:S(2)}) collective-permute-start(f32[6,66,1]{2,1,0:T(8,128)S(1)} %get-tuple-element.181), channel_id=1, source_target_pairs={{1,0},{2,1},{3,2},{5,4},{6,5},{7,6},{9,8},{10,9},{11,10},{13,12},{... | collective-permute-start | bytes 4760 | tf_op jit(solution)/shard_map/while/body/eval_jaxpr/ppermute | solution.py:17
  78.1 16.3 %all-to-all-start = ((f32[8,1,192]{2,1,0:T(1,128)}), f32[8,1,192]{2,1,0:T(1,128)S(1)}, u32[]{:S(2)}, u32[]{:S(2)}) async-start(f32[8,1,192]{2,1,0:T(1,128)} %reshape.136), calls=%async_computation | async-start | bytes 16384 | tf_op jit(solution)/shard_map/while/body/eval_jaxpr/all_to_all | solution.py:42
  88.5 18.0 %collective-permute-start.2 = (f32[6,66,1]{2,1,0:T(8,128)S(1)}, f32[6,66,1]{2,1,0:T(8,128)S(1)}, u32[]{:S(2)}, u32[]{:S(2)}) collective-permute-start(f32[6,66,1]{2,1,0:T(8,128)S(1)} %get-tuple-element.180), channel_id=1, source_target_pairs={{0,1},{1,2},{2,3},{4,5},{5,6},{6,7},{8,9},{9,10},{10,11},{12,13},{... | collective-permute-start | bytes 4760 | tf_op jit(solution)/shard_map/while/body/eval_jaxpr/ppermute | solution.py:16
  91.9 14.6 %collective-permute-start.3 = (f32[6,66,1]{2,1,0:T(8,128)S(1)}, f32[6,66,1]{2,1,0:T(8,128)S(1)}, u32[]{:S(2)}, u32[]{:S(2)}) collective-permute-start(f32[6,66,1]{2,1,0:T(8,128)S(1)} %get-tuple-element.181), channel_id=1, source_target_pairs={{1,0},{2,1},{3,2},{5,4},{6,5},{7,6},{9,8},{10,9},{11,10},{13,12},{... | collective-permute-start | bytes 4760 | tf_op jit(solution)/shard_map/while/body/eval_jaxpr/ppermute | solution.py:17
  116.7 16.3 %all-to-all-start = ((f32[8,1,192]{2,1,0:T(1,128)}), f32[8,1,192]{2,1,0:T(1,128)S(1)}, u32[]{:S(2)}, u32[]{:S(2)}) async-start(f32[8,1,192]{2,1,0:T(1,128)} %reshape.136), calls=%async_computation | async-start | bytes 16384 | tf_op jit(solution)/shard_map/while/body/eval_jaxpr/all_to_all | solution.py:42
  127.1 18.0 %collective-permute-start.2 = (f32[6,66,1]{2,1,0:T(8,128)S(1)}, f32[6,66,1]{2,1,0:T(8,128)S(1)}, u32[]{:S(2)}, u32[]{:S(2)}) collective-permute-start(f32[6,66,1]{2,1,0:T(8,128)S(1)} %get-tuple-element.180), channel_id=1, source_target_pairs={{0,1},{1,2},{2,3},{4,5},{5,6},{6,7},{8,9},{9,10},{10,11},{12,13},{... | collective-permute-start | bytes 4760 | tf_op jit(solution)/shard_map/while/body/eval_jaxpr/ppermute | solution.py:16
  130.5 14.6 %collective-permute-start.3 = (f32[6,66,1]{2,1,0:T(8,128)S(1)}, f32[6,66,1]{2,1,0:T(8,128)S(1)}, u32[]{:S(2)}, u32[]{:S(2)}) collective-permute-start(f32[6,66,1]{2,1,0:T(8,128)S(1)} %get-tuple-element.181), channel_id=1, source_target_pairs={{1,0},{2,1},{3,2},{5,4},{6,5},{7,6},{9,8},{10,9},{11,10},{13,12},{... | collective-permute-start | bytes 4760 | tf_op jit(solution)/shard_map/while/body/eval_jaxpr/ppermute | solution.py:17
  155.3 16.3 %all-to-all-start = ((f32[8,1,192]{2,1,0:T(1,128)}), f32[8,1,192]{2,1,0:T(1,128)S(1)}, u32[]{:S(2)}, u32[]{:S(2)}) async-start(f32[8,1,192]{2,1,0:T(1,128)} %reshape.136), calls=%async_computation | async-start | bytes 16384 | tf_op jit(solution)/shard_map/while/body/eval_jaxpr/all_to_all | solution.py:42
  165.7 18.0 %collective-permute-start.2 = (f32[6,66,1]{2,1,0:T(8,128)S(1)}, f32[6,66,1]{2,1,0:T(8,128)S(1)}, u32[]{:S(2)}, u32[]{:S(2)}) collective-permute-start(f32[6,66,1]{2,1,0:T(8,128)S(1)} %get-tuple-element.180), channel_id=1, source_target_pairs={{0,1},{1,2},{2,3},{4,5},{5,6},{6,7},{8,9},{9,10},{10,11},{12,13},{... | collective-permute-start | bytes 4760 | tf_op jit(solution)/shard_map/while/body/eval_jaxpr/ppermute | solution.py:16
  169.1 14.6 %collective-permute-start.3 = (f32[6,66,1]{2,1,0:T(8,128)S(1)}, f32[6,66,1]{2,1,0:T(8,128)S(1)}, u32[]{:S(2)}, u32[]{:S(2)}) collective-permute-start(f32[6,66,1]{2,1,0:T(8,128)S(1)} %get-tuple-element.181), channel_id=1, source_target_pairs={{1,0},{2,1},{3,2},{5,4},{6,5},{7,6},{9,8},{10,9},{11,10},{13,12},{... | collective-permute-start | bytes 4760 | tf_op jit(solution)/shard_map/while/body/eval_jaxpr/ppermute | solution.py:17
  194.0 16.3 %all-to-all-start = ((f32[8,1,192]{2,1,0:T(1,128)}), f32[8,1,192]{2,1,0:T(1,128)S(1)}, u32[]{:S(2)}, u32[]{:S(2)}) async-start(f32[8,1,192]{2,1,0:T(1,128)} %reshape.136), calls=%async_computation | async-start | bytes 16384 | tf_op jit(solution)/shard_map/while/body/eval_jaxpr/all_to_all | solution.py:42
  204.4 18.0 %collective-permute-start.2 = (f32[6,66,1]{2,1,0:T(8,128)S(1)}, f32[6,66,1]{2,1,0:T(8,128)S(1)}, u32[]{:S(2)}, u32[]{:S(2)}) collective-permute-start(f32[6,66,1]{2,1,0:T(8,128)S(1)} %get-tuple-element.180), channel_id=1, source_target_pairs={{0,1},{1,2},{2,3},{4,5},{5,6},{6,7},{8,9},{9,10},{10,11},{12,13},{... | collective-permute-start | bytes 4760 | tf_op jit(solution)/shard_map/while/body/eval_jaxpr/ppermute | solution.py:16
  207.7 14.6 %collective-permute-start.3 = (f32[6,66,1]{2,1,0:T(8,128)S(1)}, f32[6,66,1]{2,1,0:T(8,128)S(1)}, u32[]{:S(2)}, u32[]{:S(2)}) collective-permute-start(f32[6,66,1]{2,1,0:T(8,128)S(1)} %get-tuple-element.181), channel_id=1, source_target_pairs={{1,0},{2,1},{3,2},{5,4},{6,5},{7,6},{9,8},{10,9},{11,10},{13,12},{... | collective-permute-start | bytes 4760 | tf_op jit(solution)/shard_map/while/body/eval_jaxpr/ppermute | solution.py:17
  232.6 16.3 %all-to-all-start = ((f32[8,1,192]{2,1,0:T(1,128)}), f32[8,1,192]{2,1,0:T(1,128)S(1)}, u32[]{:S(2)}, u32[]{:S(2)}) async-start(f32[8,1,192]{2,1,0:T(1,128)} %reshape.136), calls=%async_computation | async-start | bytes 16384 | tf_op jit(solution)/shard_map/while/body/eval_jaxpr/all_to_all | solution.py:42
  243.0 18.0 %collective-permute-start.2 = (f32[6,66,1]{2,1,0:T(8,128)S(1)}, f32[6,66,1]{2,1,0:T(8,128)S(1)}, u32[]{:S(2)}, u32[]{:S(2)}) collective-permute-start(f32[6,66,1]{2,1,0:T(8,128)S(1)} %get-tuple-element.180), channel_id=1, source_target_pairs={{0,1},{1,2},{2,3},{4,5},{5,6},{6,7},{8,9},{9,10},{10,11},{12,13},{... | collective-permute-start | bytes 4760 | tf_op jit(solution)/shard_map/while/body/eval_jaxpr/ppermute | solution.py:16
  246.4 14.6 %collective-permute-start.3 = (f32[6,66,1]{2,1,0:T(8,128)S(1)}, f32[6,66,1]{2,1,0:T(8,128)S(1)}, u32[]{:S(2)}, u32[]{:S(2)}) collective-permute-start(f32[6,66,1]{2,1,0:T(8,128)S(1)} %get-tuple-element.181), channel_id=1, source_target_pairs={{1,0},{2,1},{3,2},{5,4},{6,5},{7,6},{9,8},{10,9},{11,10},{13,12},{... | collective-permute-start | bytes 4760 | tf_op jit(solution)/shard_map/while/body/eval_jaxpr/ppermute | solution.py:17
  271.2 16.3 %all-to-all-start = ((f32[8,1,192]{2,1,0:T(1,128)}), f32[8,1,192]{2,1,0:T(1,128)S(1)}, u32[]{:S(2)}, u32[]{:S(2)}) async-start(f32[8,1,192]{2,1,0:T(1,128)} %reshape.136), calls=%async_computation | async-start | bytes 16384 | tf_op jit(solution)/shard_map/while/body/eval_jaxpr/all_to_all | solution.py:42
  281.6 18.0 %collective-permute-start.2 = (f32[6,66,1]{2,1,0:T(8,128)S(1)}, f32[6,66,1]{2,1,0:T(8,128)S(1)}, u32[]{:S(2)}, u32[]{:S(2)}) collective-permute-start(f32[6,66,1]{2,1,0:T(8,128)S(1)} %get-tuple-element.180), channel_id=1, source_target_pairs={{0,1},{1,2},{2,3},{4,5},{5,6},{6,7},{8,9},{9,10},{10,11},{12,13},{... | collective-permute-start | bytes 4760 | tf_op jit(solution)/shard_map/while/body/eval_jaxpr/ppermute | solution.py:16
  285.0 14.6 %collective-permute-start.3 = (f32[6,66,1]{2,1,0:T(8,128)S(1)}, f32[6,66,1]{2,1,0:T(8,128)S(1)}, u32[]{:S(2)}, u32[]{:S(2)}) collective-permute-start(f32[6,66,1]{2,1,0:T(8,128)S(1)} %get-tuple-element.181), channel_id=1, source_target_pairs={{1,0},{2,1},{3,2},{5,4},{6,5},{7,6},{9,8},{10,9},{11,10},{13,12},{... | collective-permute-start | bytes 4760 | tf_op jit(solution)/shard_map/while/body/eval_jaxpr/ppermute | solution.py:17
  309.8 16.3 %all-to-all-start = ((f32[8,1,192]{2,1,0:T(1,128)}), f32[8,1,192]{2,1,0:T(1,128)S(1)}, u32[]{:S(2)}, u32[]{:S(2)}) async-start(f32[8,1,192]{2,1,0:T(1,128)} %reshape.136), calls=%async_computation | async-start | bytes 16384 | tf_op jit(solution)/shard_map/while/body/eval_jaxpr/all_to_all | solution.py:42
  320.2 18.0 %collective-permute-start.2 = (f32[6,66,1]{2,1,0:T(8,128)S(1)}, f32[6,66,1]{2,1,0:T(8,128)S(1)}, u32[]{:S(2)}, u32[]{:S(2)}) collective-permute-start(f32[6,66,1]{2,1,0:T(8,128)S(1)} %get-tuple-element.180), channel_id=1, source_target_pairs={{0,1},{1,2},{2,3},{4,5},{5,6},{6,7},{8,9},{9,10},{10,11},{12,13},{... | collective-permute-start | bytes 4760 | tf_op jit(solution)/shard_map/while/body/eval_jaxpr/ppermute | solution.py:16
  323.6 14.6 %collective-permute-start.3 = (f32[6,66,1]{2,1,0:T(8,128)S(1)}, f32[6,66,1]{2,1,0:T(8,128)S(1)}, u32[]{:S(2)}, u32[]{:S(2)}) collective-permute-start(f32[6,66,1]{2,1,0:T(8,128)S(1)} %get-tuple-element.181), channel_id=1, source_target_pairs={{1,0},{2,1},{3,2},{5,4},{6,5},{7,6},{9,8},{10,9},{11,10},{13,12},{... | collective-permute-start | bytes 4760 | tf_op jit(solution)/shard_map/while/body/eval_jaxpr/ppermute | solution.py:17
  348.5 16.3 %all-to-all-start = ((f32[8,1,192]{2,1,0:T(1,128)}), f32[8,1,192]{2,1,0:T(1,128)S(1)}, u32[]{:S(2)}, u32[]{:S(2)}) async-start(f32[8,1,192]{2,1,0:T(1,128)} %reshape.136), calls=%async_computation | async-start | bytes 16384 | tf_op jit(solution)/shard_map/while/body/eval_jaxpr/all_to_all | solution.py:42
  358.9 18.0 %collective-permute-start.2 = (f32[6,66,1]{2,1,0:T(8,128)S(1)}, f32[6,66,1]{2,1,0:T(8,128)S(1)}, u32[]{:S(2)}, u32[]{:S(2)}) collective-permute-start(f32[6,66,1]{2,1,0:T(8,128)S(1)} %get-tuple-element.180), channel_id=1, source_target_pairs={{0,1},{1,2},{2,3},{4,5},{5,6},{6,7},{8,9},{9,10},{10,11},{12,13},{... | collective-permute-start | bytes 4760 | tf_op jit(solution)/shard_map/while/body/eval_jaxpr/ppermute | solution.py:16
  362.2 14.6 %collective-permute-start.3 = (f32[6,66,1]{2,1,0:T(8,128)S(1)}, f32[6,66,1]{2,1,0:T(8,128)S(1)}, u32[]{:S(2)}, u32[]{:S(2)}) collective-permute-start(f32[6,66,1]{2,1,0:T(8,128)S(1)} %get-tuple-element.181), channel_id=1, source_target_pairs={{1,0},{2,1},{3,2},{5,4},{6,5},{7,6},{9,8},{10,9},{11,10},{13,12},{... | collective-permute-start | bytes 4760 | tf_op jit(solution)/shard_map/while/body/eval_jaxpr/ppermute | solution.py:17
  387.1 16.3 %all-to-all-start = ((f32[8,1,192]{2,1,0:T(1,128)}), f32[8,1,192]{2,1,0:T(1,128)S(1)}, u32[]{:S(2)}, u32[]{:S(2)}) async-start(f32[8,1,192]{2,1,0:T(1,128)} %reshape.136), calls=%async_computation | async-start | bytes 16384 | tf_op jit(solution)/shard_map/while/body/eval_jaxpr/all_to_all | solution.py:42
  397.5 18.0 %collective-permute-start.2 = (f32[6,66,1]{2,1,0:T(8,128)S(1)}, f32[6,66,1]{2,1,0:T(8,128)S(1)}, u32[]{:S(2)}, u32[]{:S(2)}) collective-permute-start(f32[6,66,1]{2,1,0:T(8,128)S(1)} %get-tuple-element.180), channel_id=1, source_target_pairs={{0,1},{1,2},{2,3},{4,5},{5,6},{6,7},{8,9},{9,10},{10,11},{12,13},{... | collective-permute-start | bytes 4760 | tf_op jit(solution)/shard_map/while/body/eval_jaxpr/ppermute | solution.py:16
  400.9 14.6 %collective-permute-start.3 = (f32[6,66,1]{2,1,0:T(8,128)S(1)}, f32[6,66,1]{2,1,0:T(8,128)S(1)}, u32[]{:S(2)}, u32[]{:S(2)}) collective-permute-start(f32[6,66,1]{2,1,0:T(8,128)S(1)} %get-tuple-element.181), channel_id=1, source_target_pairs={{1,0},{2,1},{3,2},{5,4},{6,5},{7,6},{9,8},{10,9},{11,10},{13,12},{... | collective-permute-start | bytes 4760 | tf_op jit(solution)/shard_map/while/body/eval_jaxpr/ppermute | solution.py:17
  425.7 16.3 %all-to-all-start = ((f32[8,1,192]{2,1,0:T(1,128)}), f32[8,1,192]{2,1,0:T(1,128)S(1)}, u32[]{:S(2)}, u32[]{:S(2)}) async-start(f32[8,1,192]{2,1,0:T(1,128)} %reshape.136), calls=%async_computation | async-start | bytes 16384 | tf_op jit(solution)/shard_map/while/body/eval_jaxpr/all_to_all | solution.py:42
  436.1 18.0 %collective-permute-start.2 = (f32[6,66,1]{2,1,0:T(8,128)S(1)}, f32[6,66,1]{2,1,0:T(8,128)S(1)}, u32[]{:S(2)}, u32[]{:S(2)}) collective-permute-start(f32[6,66,1]{2,1,0:T(8,128)S(1)} %get-tuple-element.180), channel_id=1, source_target_pairs={{0,1},{1,2},{2,3},{4,5},{5,6},{6,7},{8,9},{9,10},{10,11},{12,13},{... | collective-permute-start | bytes 4760 | tf_op jit(solution)/shard_map/while/body/eval_jaxpr/ppermute | solution.py:16
  439.5 14.6 %collective-permute-start.3 = (f32[6,66,1]{2,1,0:T(8,128)S(1)}, f32[6,66,1]{2,1,0:T(8,128)S(1)}, u32[]{:S(2)}, u32[]{:S(2)}) collective-permute-start(f32[6,66,1]{2,1,0:T(8,128)S(1)} %get-tuple-element.181), channel_id=1, source_target_pairs={{1,0},{2,1},{3,2},{5,4},{6,5},{7,6},{9,8},{10,9},{11,10},{13,12},{... | collective-permute-start | bytes 4760 | tf_op jit(solution)/shard_map/while/body/eval_jaxpr/ppermute | solution.py:17
  464.3 16.3 %all-to-all-start = ((f32[8,1,192]{2,1,0:T(1,128)}), f32[8,1,192]{2,1,0:T(1,128)S(1)}, u32[]{:S(2)}, u32[]{:S(2)}) async-start(f32[8,1,192]{2,1,0:T(1,128)} %reshape.136), calls=%async_computation | async-start | bytes 16384 | tf_op jit(solution)/shard_map/while/body/eval_jaxpr/all_to_all | solution.py:42
  474.7 18.0 %collective-permute-start.2 = (f32[6,66,1]{2,1,0:T(8,128)S(1)}, f32[6,66,1]{2,1,0:T(8,128)S(1)}, u32[]{:S(2)}, u32[]{:S(2)}) collective-permute-start(f32[6,66,1]{2,1,0:T(8,128)S(1)} %get-tuple-element.180), channel_id=1, source_target_pairs={{0,1},{1,2},{2,3},{4,5},{5,6},{6,7},{8,9},{9,10},{10,11},{12,13},{... | collective-permute-start | bytes 4760 | tf_op jit(solution)/shard_map/while/body/eval_jaxpr/ppermute | solution.py:16
  478.1 14.6 %collective-permute-start.3 = (f32[6,66,1]{2,1,0:T(8,128)S(1)}, f32[6,66,1]{2,1,0:T(8,128)S(1)}, u32[]{:S(2)}, u32[]{:S(2)}) collective-permute-start(f32[6,66,1]{2,1,0:T(8,128)S(1)} %get-tuple-element.181), channel_id=1, source_target_pairs={{1,0},{2,1},{3,2},{5,4},{6,5},{7,6},{9,8},{10,9},{11,10},{13,12},{... | collective-permute-start | bytes 4760 | tf_op jit(solution)/shard_map/while/body/eval_jaxpr/ppermute | solution.py:17
  503.0 16.3 %all-to-all-start = ((f32[8,1,192]{2,1,0:T(1,128)}), f32[8,1,192]{2,1,0:T(1,128)S(1)}, u32[]{:S(2)}, u32[]{:S(2)}) async-start(f32[8,1,192]{2,1,0:T(1,128)} %reshape.136), calls=%async_computation | async-start | bytes 16384 | tf_op jit(solution)/shard_map/while/body/eval_jaxpr/all_to_all | solution.py:42
  513.4 18.0 %collective-permute-start.2 = (f32[6,66,1]{2,1,0:T(8,128)S(1)}, f32[6,66,1]{2,1,0:T(8,128)S(1)}, u32[]{:S(2)}, u32[]{:S(2)}) collective-permute-start(f32[6,66,1]{2,1,0:T(8,128)S(1)} %get-tuple-element.180), channel_id=1, source_target_pairs={{0,1},{1,2},{2,3},{4,5},{5,6},{6,7},{8,9},{9,10},{10,11},{12,13},{... | collective-permute-start | bytes 4760 | tf_op jit(solution)/shard_map/while/body/eval_jaxpr/ppermute | solution.py:16
  516.7 14.6 %collective-permute-start.3 = (f32[6,66,1]{2,1,0:T(8,128)S(1)}, f32[6,66,1]{2,1,0:T(8,128)S(1)}, u32[]{:S(2)}, u32[]{:S(2)}) collective-permute-start(f32[6,66,1]{2,1,0:T(8,128)S(1)} %get-tuple-element.181), channel_id=1, source_target_pairs={{1,0},{2,1},{3,2},{5,4},{6,5},{7,6},{9,8},{10,9},{11,10},{13,12},{... | collective-permute-start | bytes 4760 | tf_op jit(solution)/shard_map/while/body/eval_jaxpr/ppermute | solution.py:17
  541.6 16.3 %all-to-all-start = ((f32[8,1,192]{2,1,0:T(1,128)}), f32[8,1,192]{2,1,0:T(1,128)S(1)}, u32[]{:S(2)}, u32[]{:S(2)}) async-start(f32[8,1,192]{2,1,0:T(1,128)} %reshape.136), calls=%async_computation | async-start | bytes 16384 | tf_op jit(solution)/shard_map/while/body/eval_jaxpr/all_to_all | solution.py:42
  552.0 18.0 %collective-permute-start.2 = (f32[6,66,1]{2,1,0:T(8,128)S(1)}, f32[6,66,1]{2,1,0:T(8,128)S(1)}, u32[]{:S(2)}, u32[]{:S(2)}) collective-permute-start(f32[6,66,1]{2,1,0:T(8,128)S(1)} %get-tuple-element.180), channel_id=1, source_target_pairs={{0,1},{1,2},{2,3},{4,5},{5,6},{6,7},{8,9},{9,10},{10,11},{12,13},{... | collective-permute-start | bytes 4760 | tf_op jit(solution)/shard_map/while/body/eval_jaxpr/ppermute | solution.py:16
  555.4 14.6 %collective-permute-start.3 = (f32[6,66,1]{2,1,0:T(8,128)S(1)}, f32[6,66,1]{2,1,0:T(8,128)S(1)}, u32[]{:S(2)}, u32[]{:S(2)}) collective-permute-start(f32[6,66,1]{2,1,0:T(8,128)S(1)} %get-tuple-element.181), channel_id=1, source_target_pairs={{1,0},{2,1},{3,2},{5,4},{6,5},{7,6},{9,8},{10,9},{11,10},{13,12},{... | collective-permute-start | bytes 4760 | tf_op jit(solution)/shard_map/while/body/eval_jaxpr/ppermute | solution.py:17
  580.2 16.3 %all-to-all-start = ((f32[8,1,192]{2,1,0:T(1,128)}), f32[8,1,192]{2,1,0:T(1,128)S(1)}, u32[]{:S(2)}, u32[]{:S(2)}) async-start(f32[8,1,192]{2,1,0:T(1,128)} %reshape.136), calls=%async_computation | async-start | bytes 16384 | tf_op jit(solution)/shard_map/while/body/eval_jaxpr/all_to_all | solution.py:42
  590.6 18.0 %collective-permute-start.2 = (f32[6,66,1]{2,1,0:T(8,128)S(1)}, f32[6,66,1]{2,1,0:T(8,128)S(1)}, u32[]{:S(2)}, u32[]{:S(2)}) collective-permute-start(f32[6,66,1]{2,1,0:T(8,128)S(1)} %get-tuple-element.180), channel_id=1, source_target_pairs={{0,1},{1,2},{2,3},{4,5},{5,6},{6,7},{8,9},{9,10},{10,11},{12,13},{... | collective-permute-start | bytes 4760 | tf_op jit(solution)/shard_map/while/body/eval_jaxpr/ppermute | solution.py:16
  594.0 14.6 %collective-permute-start.3 = (f32[6,66,1]{2,1,0:T(8,128)S(1)}, f32[6,66,1]{2,1,0:T(8,128)S(1)}, u32[]{:S(2)}, u32[]{:S(2)}) collective-permute-start(f32[6,66,1]{2,1,0:T(8,128)S(1)} %get-tuple-element.181), channel_id=1, source_target_pairs={{1,0},{2,1},{3,2},{5,4},{6,5},{7,6},{9,8},{10,9},{11,10},{13,12},{... | collective-permute-start | bytes 4760 | tf_op jit(solution)/shard_map/while/body/eval_jaxpr/ppermute | solution.py:17
  618.8 16.3 %all-to-all-start = ((f32[8,1,192]{2,1,0:T(1,128)}), f32[8,1,192]{2,1,0:T(1,128)S(1)}, u32[]{:S(2)}, u32[]{:S(2)}) async-start(f32[8,1,192]{2,1,0:T(1,128)} %reshape.136), calls=%async_computation | async-start | bytes 16384 | tf_op jit(solution)/shard_map/while/body/eval_jaxpr/all_to_all | solution.py:42
  629.2 18.0 %collective-permute-start.2 = (f32[6,66,1]{2,1,0:T(8,128)S(1)}, f32[6,66,1]{2,1,0:T(8,128)S(1)}, u32[]{:S(2)}, u32[]{:S(2)}) collective-permute-start(f32[6,66,1]{2,1,0:T(8,128)S(1)} %get-tuple-element.180), channel_id=1, source_target_pairs={{0,1},{1,2},{2,3},{4,5},{5,6},{6,7},{8,9},{9,10},{10,11},{12,13},{... | collective-permute-start | bytes 4760 | tf_op jit(solution)/shard_map/while/body/eval_jaxpr/ppermute | solution.py:16
  632.6 14.6 %collective-permute-start.3 = (f32[6,66,1]{2,1,0:T(8,128)S(1)}, f32[6,66,1]{2,1,0:T(8,128)S(1)}, u32[]{:S(2)}, u32[]{:S(2)}) collective-permute-start(f32[6,66,1]{2,1,0:T(8,128)S(1)} %get-tuple-element.181), channel_id=1, source_target_pairs={{1,0},{2,1},{3,2},{5,4},{6,5},{7,6},{9,8},{10,9},{11,10},{13,12},{... | collective-permute-start | bytes 4760 | tf_op jit(solution)/shard_map/while/body/eval_jaxpr/ppermute | solution.py:17
  657.5 16.3 %all-to-all-start = ((f32[8,1,192]{2,1,0:T(1,128)}), f32[8,1,192]{2,1,0:T(1,128)S(1)}, u32[]{:S(2)}, u32[]{:S(2)}) async-start(f32[8,1,192]{2,1,0:T(1,128)} %reshape.136), calls=%async_computation | async-start | bytes 16384 | tf_op jit(solution)/shard_map/while/body/eval_jaxpr/all_to_all | solution.py:42
  667.9 18.0 %collective-permute-start.2 = (f32[6,66,1]{2,1,0:T(8,128)S(1)}, f32[6,66,1]{2,1,0:T(8,128)S(1)}, u32[]{:S(2)}, u32[]{:S(2)}) collective-permute-start(f32[6,66,1]{2,1,0:T(8,128)S(1)} %get-tuple-element.180), channel_id=1, source_target_pairs={{0,1},{1,2},{2,3},{4,5},{5,6},{6,7},{8,9},{9,10},{10,11},{12,13},{... | collective-permute-start | bytes 4760 | tf_op jit(solution)/shard_map/while/body/eval_jaxpr/ppermute | solution.py:16
  671.2 14.6 %collective-permute-start.3 = (f32[6,66,1]{2,1,0:T(8,128)S(1)}, f32[6,66,1]{2,1,0:T(8,128)S(1)}, u32[]{:S(2)}, u32[]{:S(2)}) collective-permute-start(f32[6,66,1]{2,1,0:T(8,128)S(1)} %get-tuple-element.181), channel_id=1, source_target_pairs={{1,0},{2,1},{3,2},{5,4},{6,5},{7,6},{9,8},{10,9},{11,10},{13,12},{... | collective-permute-start | bytes 4760 | tf_op jit(solution)/shard_map/while/body/eval_jaxpr/ppermute | solution.py:17
  696.1 16.3 %all-to-all-start = ((f32[8,1,192]{2,1,0:T(1,128)}), f32[8,1,192]{2,1,0:T(1,128)S(1)}, u32[]{:S(2)}, u32[]{:S(2)}) async-start(f32[8,1,192]{2,1,0:T(1,128)} %reshape.136), calls=%async_computation | async-start | bytes 16384 | tf_op jit(solution)/shard_map/while/body/eval_jaxpr/all_to_all | solution.py:42
  706.5 18.0 %collective-permute-start.2 = (f32[6,66,1]{2,1,0:T(8,128)S(1)}, f32[6,66,1]{2,1,0:T(8,128)S(1)}, u32[]{:S(2)}, u32[]{:S(2)}) collective-permute-start(f32[6,66,1]{2,1,0:T(8,128)S(1)} %get-tuple-element.180), channel_id=1, source_target_pairs={{0,1},{1,2},{2,3},{4,5},{5,6},{6,7},{8,9},{9,10},{10,11},{12,13},{... | collective-permute-start | bytes 4760 | tf_op jit(solution)/shard_map/while/body/eval_jaxpr/ppermute | solution.py:16
  709.9 14.6 %collective-permute-start.3 = (f32[6,66,1]{2,1,0:T(8,128)S(1)}, f32[6,66,1]{2,1,0:T(8,128)S(1)}, u32[]{:S(2)}, u32[]{:S(2)}) collective-permute-start(f32[6,66,1]{2,1,0:T(8,128)S(1)} %get-tuple-element.181), channel_id=1, source_target_pairs={{1,0},{2,1},{3,2},{5,4},{6,5},{7,6},{9,8},{10,9},{11,10},{13,12},{... | collective-permute-start | bytes 4760 | tf_op jit(solution)/shard_map/while/body/eval_jaxpr/ppermute | solution.py:17
  734.7 16.3 %all-to-all-start = ((f32[8,1,192]{2,1,0:T(1,128)}), f32[8,1,192]{2,1,0:T(1,128)S(1)}, u32[]{:S(2)}, u32[]{:S(2)}) async-start(f32[8,1,192]{2,1,0:T(1,128)} %reshape.136), calls=%async_computation | async-start | bytes 16384 | tf_op jit(solution)/shard_map/while/body/eval_jaxpr/all_to_all | solution.py:42
  745.1 18.0 %collective-permute-start.2 = (f32[6,66,1]{2,1,0:T(8,128)S(1)}, f32[6,66,1]{2,1,0:T(8,128)S(1)}, u32[]{:S(2)}, u32[]{:S(2)}) collective-permute-start(f32[6,66,1]{2,1,0:T(8,128)S(1)} %get-tuple-element.180), channel_id=1, source_target_pairs={{0,1},{1,2},{2,3},{4,5},{5,6},{6,7},{8,9},{9,10},{10,11},{12,13},{... | collective-permute-start | bytes 4760 | tf_op jit(solution)/shard_map/while/body/eval_jaxpr/ppermute | solution.py:16
  748.5 14.6 %collective-permute-start.3 = (f32[6,66,1]{2,1,0:T(8,128)S(1)}, f32[6,66,1]{2,1,0:T(8,128)S(1)}, u32[]{:S(2)}, u32[]{:S(2)}) collective-permute-start(f32[6,66,1]{2,1,0:T(8,128)S(1)} %get-tuple-element.181), channel_id=1, source_target_pairs={{1,0},{2,1},{3,2},{5,4},{6,5},{7,6},{9,8},{10,9},{11,10},{13,12},{... | collective-permute-start | bytes 4760 | tf_op jit(solution)/shard_map/while/body/eval_jaxpr/ppermute | solution.py:17
  773.3 16.3 %all-to-all-start = ((f32[8,1,192]{2,1,0:T(1,128)}), f32[8,1,192]{2,1,0:T(1,128)S(1)}, u32[]{:S(2)}, u32[]{:S(2)}) async-start(f32[8,1,192]{2,1,0:T(1,128)} %reshape.136), calls=%async_computation | async-start | bytes 16384 | tf_op jit(solution)/shard_map/while/body/eval_jaxpr/all_to_all | solution.py:42
  783.7 18.0 %collective-permute-start.2 = (f32[6,66,1]{2,1,0:T(8,128)S(1)}, f32[6,66,1]{2,1,0:T(8,128)S(1)}, u32[]{:S(2)}, u32[]{:S(2)}) collective-permute-start(f32[6,66,1]{2,1,0:T(8,128)S(1)} %get-tuple-element.180), channel_id=1, source_target_pairs={{0,1},{1,2},{2,3},{4,5},{5,6},{6,7},{8,9},{9,10},{10,11},{12,13},{... | collective-permute-start | bytes 4760 | tf_op jit(solution)/shard_map/while/body/eval_jaxpr/ppermute | solution.py:16
  787.1 14.6 %collective-permute-start.3 = (f32[6,66,1]{2,1,0:T(8,128)S(1)}, f32[6,66,1]{2,1,0:T(8,128)S(1)}, u32[]{:S(2)}, u32[]{:S(2)}) collective-permute-start(f32[6,66,1]{2,1,0:T(8,128)S(1)} %get-tuple-element.181), channel_id=1, source_target_pairs={{1,0},{2,1},{3,2},{5,4},{6,5},{7,6},{9,8},{10,9},{11,10},{13,12},{... | collective-permute-start | bytes 4760 | tf_op jit(solution)/shard_map/while/body/eval_jaxpr/ppermute | solution.py:17
  (127 other events, 2303.5 us)
Sparse Core Ops, SparseCore 0:
  803.2 42.3 all-reduce.1
where the time goes:
time: 875 us; the launch traced here: 869 us
  starting transfers between devices  326 us (37%)
  local copies, waits for them, and re-layouts  319 us (36%)
  other arithmetic  141 us (16%)
  waiting for transfers between devices  64.3 us (7%)
  between operations  14.9 us (2%)
    ppermute x44, starting transfers between devices, extended(): before = lax.ppermute(last, axis, up)  141 us
    scatter-add x20, other arithmetic, mortar(): added = jnp.zeros((6, cells), jnp.float32).at[:, targets].add(got * weights)  106 us
    reshape x20, local copies, waits for them, and re-layouts, mortar(): return added.reshape(6, rows_x, rows_y)  106 us
    all_to_all x20, starting transfers between devices, mortar(): lax.all_to_all(sent, ('mx', 'my'), split_axis=1, concat_axis=1, tiled=True)  102 us
    another operation x20, local copies, waits for them, and re-layouts  94.5 us
    ppermute x44, starting transfers between devices, extended(): after = lax.ppermute(first, axis, down)  82.4 us
    gather x20, local copies, waits for them, and re-layouts, mortar(): sent = field.reshape(6, cells)[:, sources]  82 us
    psum x1, waiting for transfers between devices, on_device(): total = lax.psum(sens, 'freq')  42.5 us
  transfers between devices with their start and end apart: 109, of which 24 were waited for; matrix products, arithmetic and copies ran while one was open for 29% of the time, Pallas kernels for 0%

commit v1 on v0

--- a/solution.py
+++ b/solution.py
@@ -1,9 +1,17 @@
+import functools
+
 import jax
 import jax.numpy as jnp
 from jax import lax
+from jax.experimental import pallas as pl
+from jax.experimental.pallas import tpu as pltpu
 from jax.sharding import PartitionSpec as P
 
 ITERS = 20
+PARTS = 3
+LANES = 128
+F32 = jnp.float32
+BF16 = jnp.bfloat16
 
 
 def extended(x, sides, width):
@@ -19,14 +27,256 @@
     return x
 
 
-def on_device(
-    adjoint_rhs, state, density, stiffness, mass, omega, send_rows, recv_rows, mortar_weight
-):
+def pack_kernel(comps, rhs, density, stiffness, mass, send, recv, weight, *outs):
+    *outs, pages = outs
+    rows = density.shape[0]
+    tiles = rows // 8
+    cy = density.shape[1]
+    info = []
+    for ref in (send, recv):
+        cell = ref[...]
+        x, y = cell // cy, cell % cy
+        row = (x % tiles) * 8 + x // tiles + (y // LANES) * rows
+        info += [row.astype(F32), (y % LANES).astype(F32)]
+    info += [weight[...]]
+    slot = 0
+
+    def interleaved(value):
+        nonlocal slot
+        halves = []
+        for u in range(cy // LANES):
+            page = pages.at[slot % pages.shape[0]]
+            slot += 1
+            page[...] = value[:, u * LANES : (u + 1) * LANES]
+            halves.append(jnp.concatenate([page[pl.ds(t, 8, stride=tiles), :] for t in range(tiles)], axis=0))
+        return jnp.concatenate(halves, axis=1)
+
+    rho = density[...]
+    stiff = interleaved(rho * rho * rho * stiffness[...])
+    rmass = interleaved(rho * mass[...])
+    for s, out in enumerate(outs):
+        c = comps[s]
+        out[:rows, :] = interleaved(rhs[c])
+        out[rows : 2 * rows, :] = interleaved(rhs[PARTS + c])
+        out[2 * rows : 3 * rows, :] = stiff
+        out[3 * rows : 4 * rows, :] = rmass
+    for out in outs:
+        for k, line in enumerate(info):
+            out[pl.ds(4 * rows + k, 1), :] = line
+        out[pl.ds(4 * rows + 5, 3), :] = jnp.zeros((3, cy), F32)
+
+
+def split(v):
+    high = v.astype(BF16)
+    return high, (v - high.astype(F32)).astype(BF16)
+
+
+def sweep_kernel(n_i, n_j, cap, pos, omega, *refs):
+    blocks = n_i * n_j
+    msgs, refs = refs[: blocks], refs[blocks:]
+    outs, refs = refs[:n_j], refs[n_j:]
+    field, rhs, stiff, gain, lag, info, take, lane_of, put, weights, picked, pages = refs
+    rows = rhs.shape[2] // 2
+    slots = blocks * cap
+    me_i, me_j = pos[0], pos[1]
+    w = omega[0]
+
+    def both(x):
+        return x[:, :LANES], x[:, LANES:]
+
+    order = [(a, s) for a in range(n_i) for s in range(n_j)]
+    index = [lax.rem(me_i + a, n_i) * n_j + lax.rem(me_j + n_j - s, n_j) for a, s in order]
+    for msg, b in zip(msgs, index):
+        info[b] = msg[4 * rows :, :]
+    lines = jnp.concatenate([info[b] for b in range(blocks)], axis=0)
+    columns = jnp.transpose(lines)
+    lane = lax.broadcasted_iota(jnp.int32, (slots, LANES), 1)
+    depth = lax.broadcasted_iota(jnp.int32, (2 * rows, slots), 0)
+
+    def column(b, kind):
+        return jnp.broadcast_to(columns[:, b * 8 + kind : b * 8 + kind + 1], (slots, LANES))
+
+    for b in range(blocks):
+        pick = (column(b, 0).astype(jnp.int32) == lane).astype(F32).astype(BF16)
+        take[b] = jnp.concatenate([pick, pick], axis=1)
+        lane_of[b] = column(b, 1).astype(jnp.int32)
+        target = info[b, 2:3, :].astype(jnp.int32)
+        spread = (jnp.broadcast_to(target, depth.shape) == depth).astype(F32).astype(BF16)
+        put[b] = jnp.concatenate([spread, spread], axis=1)
+        weighted = jnp.where(column(b, 3).astype(jnp.int32) == lane, column(b, 4), 0.0)
+        for p in range(blocks):
+            weights[p, b * cap : (b + 1) * cap, :] = weighted[p * cap : (p + 1) * cap, :]
+        high, low = split(weighted)
+        gain[b] = jnp.dot(put[b], jnp.concatenate([high, low], axis=0), preferred_element_type=F32)
+
+    for msg, b in zip(msgs, index):
+        for u in range(2):
+            at = slice(u * rows, (u + 1) * rows)
+            lanes = slice(u * LANES, (u + 1) * LANES)
+            rhs_re, rhs_im, k, m = [msg[n * rows : (n + 1) * rows, lanes] for n in range(4)]
+            real_d = 4.4 * k + 0.3 + gain[b, at] - w * w * m
+            imag_d = 0.2 * w * (k + m)
+            den = real_d * real_d + imag_d * imag_d
+            g, l = real_d / den, imag_d / den
+            stiff[b, at], gain[b, at], lag[b, at] = k, g, l
+            rhs[b, 0, at], rhs[b, 1, at] = rhs_re, rhs_im
+            field[0, b, 0, at] = rhs_re * g + rhs_im * l
+            field[0, b, 1, at] = rhs_im * g - rhs_re * l
+
+    row8 = lax.broadcasted_iota(jnp.int32, (8, LANES), 0)
+    lane_r = lax.broadcasted_iota(jnp.int32, (rows, LANES), 1)
+
+    def sweep(step, carry):
+        now = lax.rem(step, 2)
+        then = 1 - now
+        for b in range(blocks):
+            re_h, re_l = split(field[now, b, 0])
+            im_h, im_l = split(field[now, b, 1])
+            source = jnp.concatenate(
+                [jnp.concatenate([re_h, im_h], axis=1), jnp.concatenate([re_l, im_l], axis=1)], axis=0
+            )
+            got = jnp.dot(take[b], source, preferred_element_type=F32)
+            at_lane, wt = lane_of[b], weights[b]
+            for part, g in enumerate(both(got)):
+                value = jnp.take_along_axis(g, at_lane, axis=1, mode="promise_in_bounds") * wt
+                high, low = split(value)
+                lanes = slice(part * LANES, (part + 1) * LANES)
+                for q in range(blocks):
+                    chunk = slice(q * cap, (q + 1) * cap)
+                    picked[q, b * cap : (b + 1) * cap, lanes] = high[chunk]
+                    picked[q, slots + b * cap : slots + (b + 1) * cap, lanes] = low[chunk]
+        for i in range(n_i):
+            for j in range(n_j):
+                b = i * n_j + j
+                mortar = jnp.dot(put[b], picked[b], preferred_element_type=F32)
+                h = [[None, None], [None, None]]
+                for part in range(2):
+                    whole = field[now, b, part]
+                    v = [whole[:rows], whole[rows:]]
+                    zero = jnp.zeros((rows, LANES), F32)
+                    west = field[now, b - 1, part, rows:] if j > 0 else zero
+                    east = field[now, b + 1, part, :rows] if j < n_j - 1 else zero
+                    for u in range(2):
+                        own = v[u]
+                        left = west if u == 0 else v[0]
+                        right = v[1] if u == 0 else east
+                        around = pltpu.roll(jnp.where(lane_r == LANES - 1, left, own), 1, 1)
+                        around += pltpu.roll(jnp.where(lane_r == 0, right, own), LANES - 1, 1)
+                        top = pltpu.roll(own[rows - 8 :], 1, 0)
+                        bottom = pltpu.roll(own[:8], 7, 0)
+                        above = jnp.zeros((8, LANES), F32)
+                        below = above
+                        if i > 0:
+                            above = pltpu.roll(
+                                field[now, b - n_j, part, (u + 1) * rows - 8 : (u + 1) * rows], 1, 0
+                            )
+                        if i < n_i - 1:
+                            below = pltpu.roll(field[now, b + n_j, part, u * rows : u * rows + 8], 7, 0)
+                        top = jnp.where(row8 == 0, above, top)
+                        bottom = jnp.where(row8 == 7, below, bottom)
+                        around += jnp.concatenate([top, own[:-8]], axis=0)
+                        around += jnp.concatenate([own[8:], bottom], axis=0)
+                        at = slice(u * rows, (u + 1) * rows)
+                        m = mortar[at, part * LANES : (part + 1) * LANES]
+                        h[part][u] = m + rhs[b, part, at] + stiff[b, at] * around
+                for u in range(2):
+                    at = slice(u * rows, (u + 1) * rows)
+                    g, l = gain[b, at], lag[b, at]
+                    field[then, b, 0, at] = h[0][u] * g + h[1][u] * l
+                    field[then, b, 1, at] = h[1][u] * g - h[0][u] * l
+        return carry
+
+    lax.fori_loop(0, ITERS - 1, sweep, 0)
+    last = (ITERS - 1) % 2
+    tiles = rows // 8
+    for s, out in enumerate(outs):
+        b = me_i * n_j + lax.rem(me_j + s, n_j)
+        for part in range(2):
+            for u in range(2):
+                page = pages.at[(s * 4 + part * 2 + u) % 8]
+                for t in range(tiles):
+                    row = u * rows + t * 8
+                    page[pl.ds(t, 8, stride=tiles), :] = field[last, b, part, row : row + 8, :]
+                out[part, :, u * LANES : (u + 1) * LANES] = page[...]
+
+
+def vmem():
+    return pl.BlockSpec(memory_space=pltpu.VMEM)
+
+
+def smem():
+    return pl.BlockSpec(memory_space=pltpu.SMEM)
+
+
+def shifts(n_j, source_limit, target_limit):
+    return [
+        [(a, (a + s) % n_j) for a in range(n_j) if a < source_limit and (a + s) % n_j < target_limit]
+        for s in range(1, n_j)
+    ]
+
+
+def solve(rhs, density, stiffness, mass, omega, send_rows, recv_rows, mortar_weight):
+    rows, cy = density.shape
+    n_i, n_j = lax.axis_size("mx"), lax.axis_size("my")
+    blocks = n_i * n_j
+    slots = send_rows.shape[1]
+    cap = slots // blocks
+    me_i, me_j = lax.axis_index("mx"), lax.axis_index("my")
+    ahead = (me_j + jnp.arange(n_j, dtype=jnp.int32)) % n_j
+    comps = jnp.minimum(ahead, PARTS - 1)
+    height = 4 * rows + 8
+    message = jax.ShapeDtypeStruct((height, cy), F32)
+    own = pl.pallas_call(
+        pack_kernel,
+        out_shape=[message] * n_j,
+        in_specs=[smem()] + [vmem()] * 7,
+        out_specs=[vmem()] * n_j,
+        scratch_shapes=[pltpu.VMEM((8, rows, LANES), F32)],
+        name="pack",
+    )(comps, rhs, density, stiffness, mass, send_rows, recv_rows, mortar_weight)
+    msgs = [own[0]]
+    for s, pairs in enumerate(shifts(n_j, n_j, PARTS), 1):
+        msgs.append(lax.ppermute(own[s], "my", pairs))
+    swap = [(a, (a + 1) % n_i) for a in range(n_i)]
+    for other in range(1, n_i):
+        msgs += [lax.ppermute(m, "mx", swap) for m in msgs[-n_j:]]
+    pos = jnp.stack([me_i, me_j]).astype(jnp.int32)
+    block = (blocks, 2 * rows, LANES)
+    outs = pl.pallas_call(
+        functools.partial(sweep_kernel, n_i, n_j, cap),
+        out_shape=[jax.ShapeDtypeStruct((2, rows, cy), F32)] * n_j,
+        in_specs=[smem(), smem()] + [vmem()] * blocks,
+        out_specs=[vmem()] * n_j,
+        scratch_shapes=[
+            pltpu.VMEM((2, blocks, 2, 2 * rows, LANES), F32),
+            pltpu.VMEM((blocks, 2, 2 * rows, LANES), F32),
+            pltpu.VMEM(block, F32),
+            pltpu.VMEM(block, F32),
+            pltpu.VMEM(block, F32),
+            pltpu.VMEM((blocks, 8, cy), F32),
+            pltpu.VMEM((blocks, slots, 4 * rows), BF16),
+            pltpu.VMEM((blocks, slots, LANES), jnp.int32),
+            pltpu.VMEM((blocks, 2 * rows, 2 * slots), BF16),
+            pltpu.VMEM((blocks, slots, LANES), F32),
+            pltpu.VMEM((blocks, 2 * slots, 2 * LANES), BF16),
+            pltpu.VMEM((8, rows, LANES), F32),
+        ],
+        compiler_params=pltpu.CompilerParams(vmem_limit_bytes=40 * 1024 * 1024),
+        name="sweeps",
+    )(pos, omega, *msgs)
+    parts = [outs[0]]
+    for s, pairs in enumerate(shifts(n_j, PARTS, n_j), 1):
+        parts.append(lax.ppermute(outs[s], "my", pairs))
+    stacked = jnp.stack(parts)
+    comps_of = [lax.dynamic_index_in_dim(stacked, (me_j + n_j - c) % n_j, 0, False) for c in range(PARTS)]
+    return jnp.stack(comps_of, axis=1).reshape(2 * PARTS, rows, cy)
+
+
+def solve_split(rhs, density, stiffness, mass, omega, send_rows, recv_rows, mortar_weight):
     rows_x, rows_y = density.shape
     cells = rows_x * rows_y
     w = omega[0]
     stiff = density**3 * stiffness
-    dstiff = 3.0 * density**2 * stiffness
     rmass = density * mass
     sources = send_rows[0]
     targets = recv_rows[0]
@@ -35,7 +285,6 @@
     real_d = 4.4 * stiff + 0.3 + mdiag - w * w * rmass
     imag_d = 0.2 * w * (stiff + rmass)
     den = real_d * real_d + imag_d * imag_d
-    rhs = adjoint_rhs.reshape(6, rows_x, rows_y)
 
     def mortar(field):
         sent = field.reshape(6, cells)[:, sources]
@@ -53,7 +302,21 @@
         new_im = (h[3:] * real_d - h[:3] * imag_d) / den
         return jnp.concatenate([new_re, new_im], axis=0)
 
-    field = lax.fori_loop(0, ITERS, sweep, jnp.zeros((6, rows_x, rows_y), jnp.float32))
+    return lax.fori_loop(0, ITERS, sweep, jnp.zeros((6, rows_x, rows_y), jnp.float32))
+
+
+def on_device(
+    adjoint_rhs, state, density, stiffness, mass, omega, send_rows, recv_rows, mortar_weight
+):
+    rows_x, rows_y = density.shape
+    w = omega[0]
+    dstiff = 3.0 * density**2 * stiffness
+    rhs = adjoint_rhs.reshape(6, rows_x, rows_y)
+    n_i, n_j = lax.axis_size("mx"), lax.axis_size("my")
+    fits = n_i == 2 and PARTS <= n_j <= 4 and rows_x % 64 == 0 and rows_y == 2 * LANES
+    fits = fits and send_rows.shape[1] == rows_y
+    system = (rhs, density, stiffness, mass, omega, send_rows, recv_rows, mortar_weight)
+    field = (solve if fits else solve_split)(*system)
     state_six = state.reshape(6, rows_x, rows_y)
     state_pad = extended(state_six, (("mx", 1), ("my", 2)), 1).astype(jnp.float32)
     u = state_six.astype(jnp.float32)
@@ -68,7 +331,10 @@
     t_re = da * u[:3] - db * u[3:] - dstiff * nb[:3]
     t_im = da * u[3:] + db * u[:3] - dstiff * nb[3:]
     sens = -jnp.sum(field[:3] * t_re - field[3:] * t_im, axis=0)
-    total = lax.psum(sens, "freq")
+    size = lax.axis_size("freq")
+    total = sens
+    for s in range(1, size):
+        total = total + lax.ppermute(sens, "freq", [(a, (a + s) % size) for a in range(size)])
     weighted = extended(density * total, (("mx", 0), ("my", 1)), 1)
     filt = weighted[1:-1, 1:-1]
     filt = filt + 0.5 * (

time: 875 us -> 140 us (0.16)
  local copies, waits for them, and re-layouts: 319 us -> 1.07 us
  starting transfers between devices: 326 us -> 38.9 us
  other arithmetic: 141 us -> 3.3 us
  Pallas kernels: 0 us -> 59.2 us
  waiting for transfers between devices: 64.3 us -> 34.7 us
  between operations: 14.9 us -> 1.67 us
    ppermute x44 -> x4, starting transfers between devices: 141 us -> 9.67 us  [extended(): before = lax.ppermute(last, axis, up)]
    scatter-add x21 -> x0, other arithmetic: 108 us -> none  [the longest x20 106 us: mortar(): added = jnp.zeros((6, cells), jnp.float32).at[:, targets].add(got * weights)]
    reshape x21 -> x0, local copies, waits for them, and re-layouts: 106 us -> none  [the longest x20 106 us: mortar(): return added.reshape(6, rows_x, rows_y)]
    all_to_all x20 -> x0, starting transfers between devices: 102 us -> none  [mortar(): lax.all_to_all(sent, ('mx', 'my'), split_axis=1, concat_axis=1, tiled=True)]
    another operation x20 -> x1, local copies, waits for them, and re-layouts: 94.5 us -> 0.04 us  [solve(): return jnp.stack(comps_of, axis=1).reshape(2 * PARTS, rows, cy)]
    gather x20 -> x0, local copies, waits for them, and re-layouts: 82 us -> none  [mortar(): sent = field.reshape(6, cells)[:, sources]]
    ppermute x44 -> x4, starting transfers between devices: 82.4 us -> 7.03 us  [extended(): after = lax.ppermute(first, axis, down)]
    pallas_call x0 -> x2, Pallas kernels: none -> 59.2 us  [the longest x1 56.9 us: solve(): pl.pallas_call(functools.partial(sweep_kernel, n_i, n_j, cap), out_shape=...]
  transfers between devices with their start and end apart: 109 -> 21, of which waited for: 24 -> 11; matrix products, arithmetic and copies ran while one was open for 29% -> 1% of each run, Pallas kernels for 0% -> 0%
where the time goes in v1:
time: 140 us; the launch traced here: 139 us
  Pallas kernels  59.2 us (42%)
  starting transfers between devices  38.9 us (28%)
  waiting for transfers between devices  34.7 us (25%)
  other arithmetic  3.3 us (2%)
  between operations  1.67 us (1%)
    pallas_call x1, Pallas kernels, solve(): pl.pallas_call(functools.partial(sweep_kernel, n_i, n_j, cap), out_shape=...  56.9 us
    ppermute x3, waiting for transfers between devices, solve(): msgs.append(lax.ppermute(own[s], 'my', pairs))  14 us
    ppermute x4, starting transfers between devices, extended(): before = lax.ppermute(last, axis, up)  9.67 us
    ppermute x4, waiting for transfers between devices, extended(): before = lax.ppermute(last, axis, up)  8.6 us
    ppermute x3, starting transfers between devices, solve(): msgs.append(lax.ppermute(own[s], 'my', pairs))  8.13 us
    ppermute x3, starting transfers between devices, solve(): parts.append(lax.ppermute(outs[s], 'my', pairs))  7.77 us
    ppermute x4, starting transfers between devices, extended(): after = lax.ppermute(first, axis, down)  7.03 us
    ppermute x3, starting transfers between devices, on_device(): lax.ppermute(sens, 'freq', [(a, (a + s) % size) for a in range(size)])  5.06 us
  transfers between devices with their start and end apart: 21, of which 11 were waited for; matrix products, arithmetic and copies ran while one was open for 1% of the time, Pallas kernels for 0%

profile of v1, /device:TPU:8, one launch (start us, length us, event | category | flops | bytes accessed | tf_op | source)
XLA Modules:
  0.0 138.7 jit_solution(18129262930037049088)
XLA Ops:
  0.6 0.6 fusion.12.comps
  1.2 2.2 %pack.1 = (f32[264,256]{1,0:T(8,128)}, f32[264,256]{1,0:T(8,128)}, f32[264,256]{1,0:T(8,128)}, f32[264,256]{1,0:T(8,128)}) custom-call(s32[4]{0:T(128)} %fusion.12.comps, f32[6,64,256]{2,1,0:T(8,128)} %bitcast.31, f32[64,256]{1,0:T(8,128)} %density.1, f32[64,256]{1,0:T(8,128)} %stiffness.1, f32[64,256]{1,0:T(8,128)} %mass.1, s32[1,256]{1,0:T(1,128)} %send.1, ...), custom_call_target="tpu_custom_call" | custom-call | tf_op jit(solution)/shard_map/pack/pallas_call | solution.py:229
  3.4 3.5 %collective-permute-start = (f32[264,256]{1,0:T(8,128)}, f32[264,256]{1,0:T(8,128)S(1)}, u32[]{:S(2)}, u32[]{:S(2)}) collective-permute-start(f32[264,256]{1,0:T(8,128)} %get-tuple-element.11), channel_id=1, source_target_pairs={{0,1},{1,2},{3,0},{4,5},{5,6},{7,4},{8,9},{9,10},{11,8},{12,13},{1... | collective-permute-start | bytes 811016 | tf_op jit(solution)/shard_map/ppermute | solution.py:239
  6.9 1.3 collective-permute-start.1
  8.2 3.4 %collective-permute-start.2 = (f32[264,256]{1,0:T(8,128)}, f32[264,256]{1,0:T(8,128)S(1)}, u32[]{:S(2)}, u32[]{:S(2)}) collective-permute-start(f32[264,256]{1,0:T(8,128)} %get-tuple-element.13), channel_id=1, source_target_pairs={{1,0},{2,1},{3,2},{5,4},{6,5},{7,6},{9,8},{10,9},{11,10},{13,12},{... | collective-permute-start | bytes 811016 | tf_op jit(solution)/shard_map/ppermute | solution.py:239
  11.6 0.0 copy-done.1
  11.6 1.3 collective-permute-start.10
  12.9 0.0 copy-start.2
  12.9 0.0 copy-start.3
  13.0 0.0 copy-start.4
  13.0 1.4 %collective-permute-start.11 = (bf16[6,1,256]{2,1,0:T(2,128)(2,1)S(1)}, bf16[6,1,256]{2,1,0:T(2,128)(2,1)S(1)}, u32[]{:S(2)}, u32[]{:S(2)}) collective-permute-start(bf16[6,1,256]{2,1,0:T(2,128)(2,1)S(1)} %get-tuple-element.28), channel_id=1, source_target_pairs={{4,0},{5,1},{6,2},{7,3},{12,8},{13,9},{14,10},{15,11},{20,16},{21,... | collective-permute-start | bytes 9224 | tf_op jit(solution)/shard_map/ppermute | solution.py:25
  15.1 0.0 copy-done.2
  15.1 0.0 copy-done.3
  15.1 0.0 copy-done.4
  15.1 0.0 copy-start
  15.2 0.1 pad_add_fusion.pos
  15.3 0.0 collective-permute-done.10
  15.3 0.8 copy-done
  16.1 1.1 collective-permute-start.3
  17.2 0.0 collective-permute-done.11
  17.2 0.1 pad_maximum_fusion.2
  17.3 0.0 collective-permute-done.refs_1_
  17.3 0.1 collective-permute-start.4
  17.4 3.3 %collective-permute-done.1.refs_2_ = f32[264,256]{1,0:T(8,128)S(1)} collective-permute-done((f32[264,256]{1,0:T(8,128)}, f32[264,256]{1,0:T(8,128)S(1)}, u32[]{:S(2)}, u32[]{:S(2)}) %collective-permute-start.1) | collective-permute-done | bytes 270368 | tf_op jit(solution)/shard_map/ppermute | solution.py:239
  20.7 0.0 collective-permute-start.5
  20.7 10.7 %collective-permute-done.2.refs_3_ = f32[264,256]{1,0:T(8,128)S(1)} collective-permute-done((f32[264,256]{1,0:T(8,128)}, f32[264,256]{1,0:T(8,128)S(1)}, u32[]{:S(2)}, u32[]{:S(2)}) %collective-permute-start.2) | collective-permute-done | bytes 270368 | tf_op jit(solution)/shard_map/ppermute | solution.py:239
  31.4 0.0 collective-permute-start.6
  31.4 0.1 fusion.15
  31.5 1.9 %collective-permute-start.12 = (bf16[6,66,1]{2,1,0:T(8,128)(2,1)S(1)}, bf16[6,66,1]{2,1,0:T(8,128)(2,1)S(1)}, u32[]{:S(2)}, u32[]{:S(2)}) collective-permute-start(bf16[6,66,1]{2,1,0:T(8,128)(2,1)S(1)} %get-tuple-element.25), channel_id=1, source_target_pairs={{0,1},{1,2},{2,3},{4,5},{5,6},{6,7},{8,9},{9,10},{10,11},{12,13},{... | collective-permute-start | bytes 2384 | tf_op jit(solution)/shard_map/ppermute | solution.py:24
  33.4 5.4 %collective-permute-done.12 = bf16[6,66,1]{2,1,0:T(8,128)(2,1)S(1)} collective-permute-done((bf16[6,66,1]{2,1,0:T(8,128)(2,1)S(1)}, bf16[6,66,1]{2,1,0:T(8,128)(2,1)S(1)}, u32[]{:S(2)}, u32[]{:S(2)}) %collective-permute-start.12) | collective-permute-done | bytes 824 | tf_op jit(solution)/shard_map/ppermute | solution.py:24
  38.8 1.9 %collective-permute-start.13 = (bf16[6,66,1]{2,1,0:T(8,128)(2,1)S(1)}, bf16[6,66,1]{2,1,0:T(8,128)(2,1)S(1)}, u32[]{:S(2)}, u32[]{:S(2)}) collective-permute-start(bf16[6,66,1]{2,1,0:T(8,128)(2,1)S(1)} %get-tuple-element.26), channel_id=1, source_target_pairs={{1,0},{2,1},{3,2},{5,4},{6,5},{7,6},{9,8},{10,9},{11,10},{13,12},{... | collective-permute-start | bytes 2384 | tf_op jit(solution)/shard_map/ppermute | solution.py:25
  40.8 4.7 %collective-permute-done.13 = bf16[6,66,1]{2,1,0:T(8,128)(2,1)S(1)} collective-permute-done((bf16[6,66,1]{2,1,0:T(8,128)(2,1)S(1)}, bf16[6,66,1]{2,1,0:T(8,128)(2,1)S(1)}, u32[]{:S(2)}, u32[]{:S(2)}) %collective-permute-start.13) | collective-permute-done | bytes 824 | tf_op jit(solution)/shard_map/ppermute | solution.py:25
  45.5 0.3 maximum_convert_fusion
  45.7 0.0 collective-permute-done.3.refs_4_
  45.7 0.0 collective-permute-done.4.refs_5_
  45.7 0.0 collective-permute-done.5.refs_6_
  45.8 0.0 collective-permute-done.6.refs_7_
  45.8 56.9 %sweeps.1 = (f32[2,64,256]{2,1,0:T(8,128)S(1)}, f32[2,64,256]{2,1,0:T(8,128)S(1)}, f32[2,64,256]{2,1,0:T(8,128)S(1)}, f32[2,64,256]{2,1,0:T(8,128)S(1)}) custom-call(s32[2]{0:T(128)S(1)} %pad_add_fusion.pos, f32[1]{0:T(128)S(6)} %copy.11.omega, f32[264,256]{1,0:T(8,128)S(1)} %copy-done, f32[264,256]{1,0:T(8,128)S(1)} %collective-permute-done.refs_1_, ...), custom_call_target="tpu_custom_call" | custom-call | tf_op jit(solution)/shard_map/sweeps/pallas_call | solution.py:245
  102.7 2.3 %collective-permute-start.7 = (f32[2,64,256]{2,1,0:T(8,128)S(1)}, f32[2,64,256]{2,1,0:T(8,128)S(1)}, u32[]{:S(2)}, u32[]{:S(2)}) collective-permute-start(f32[2,64,256]{2,1,0:T(8,128)S(1)} %get-tuple-element.15), channel_id=1, source_target_pairs={{0,1},{1,2},{2,3},{4,5},{5,6},{6,7},{8,9},{9,10},{10,11},{12,13},{... | collective-permute-start | bytes 393224 | tf_op jit(solution)/shard_map/ppermute | solution.py:269
  105.0 1.3 collective-permute-start.8
  106.4 4.1 %collective-permute-start.9 = (f32[2,64,256]{2,1,0:T(8,128)S(1)}, f32[2,64,256]{2,1,0:T(8,128)S(1)}, u32[]{:S(2)}, u32[]{:S(2)}) collective-permute-start(f32[2,64,256]{2,1,0:T(8,128)S(1)} %get-tuple-element.17), channel_id=1, source_target_pairs={{0,3},{1,0},{2,1},{4,7},{5,4},{6,5},{8,11},{9,8},{10,9},{12,15},{1... | collective-permute-start | bytes 393224 | tf_op jit(solution)/shard_map/ppermute | solution.py:269
  110.5 0.4 slice_add_fusion
  110.9 0.1 collective-permute-done.7
  111.0 4.5 %collective-permute-done.8 = f32[2,64,256]{2,1,0:T(8,128)S(1)} collective-permute-done((f32[2,64,256]{2,1,0:T(8,128)S(1)}, f32[2,64,256]{2,1,0:T(8,128)S(1)}, u32[]{:S(2)}, u32[]{:S(2)}) %collective-permute-start.8) | collective-permute-done | bytes 131104 | tf_op jit(solution)/shard_map/ppermute | solution.py:269
  115.4 0.0 collective-permute-done.9
  115.5 0.8 pad_maximum_fusion.1
  116.3 0.1 fusion.3
  116.5 2.1 %collective-permute-start.14 = (f32[64,256]{1,0:T(8,128)S(1)}, f32[64,256]{1,0:T(8,128)S(1)}, u32[]{:S(2)}, u32[]{:S(2)}) collective-permute-start(f32[64,256]{1,0:T(8,128)S(1)} %neg.3), channel_id=1, source_target_pairs={{0,8},{8,16},{16,24},{24,0},{1,9},{9,17},{17,25},{25,1},{2,10},{10... | collective-permute-start | bytes 196616 | tf_op jit(solution)/shard_map/ppermute | solution.py:337
  118.6 1.5 %collective-permute-start.15 = (f32[64,256]{1,0:T(8,128)S(1)}, f32[64,256]{1,0:T(8,128)S(1)}, u32[]{:S(2)}, u32[]{:S(2)}) collective-permute-start(f32[64,256]{1,0:T(8,128)S(1)} %neg.3), channel_id=1, source_target_pairs={{0,16},{8,24},{16,0},{24,8},{1,17},{9,25},{17,1},{25,9},{2,18},{10... | collective-permute-start | bytes 196616 | tf_op jit(solution)/shard_map/ppermute | solution.py:337
  120.1 1.4 %collective-permute-start.16 = (f32[64,256]{1,0:T(8,128)S(1)}, f32[64,256]{1,0:T(8,128)S(1)}, u32[]{:S(2)}, u32[]{:S(2)}) collective-permute-start(f32[64,256]{1,0:T(8,128)S(1)} %neg.3), channel_id=1, source_target_pairs={{0,24},{8,0},{16,8},{24,16},{1,25},{9,1},{17,9},{25,17},{2,26},{10... | collective-permute-start | bytes 196616 | tf_op jit(solution)/shard_map/ppermute | solution.py:337
  121.5 0.2 collective-permute-done.14
  121.8 1.1 collective-permute-done.15
  122.8 1.5 %collective-permute-done.16 = f32[64,256]{1,0:T(8,128)S(1)} collective-permute-done((f32[64,256]{1,0:T(8,128)S(1)}, f32[64,256]{1,0:T(8,128)S(1)}, u32[]{:S(2)}, u32[]{:S(2)}) %collective-permute-start.16) | collective-permute-done | bytes 65568 | tf_op jit(solution)/shard_map/ppermute | solution.py:337
  124.4 1.3 collective-permute-start.17
  125.7 3.0 %collective-permute-start.18 = (f32[1,256]{1,0:T(1,128)S(1)}, f32[1,256]{1,0:T(1,128)S(1)}, u32[]{:S(2)}, u32[]{:S(2)}) collective-permute-start(f32[1,256]{1,0:T(1,128)S(1)} %get-tuple-element.33), channel_id=1, source_target_pairs={{0,4},{1,5},{2,6},{3,7},{8,12},{9,13},{10,14},{11,15},{16,20},{17,... | collective-permute-start | bytes 3080 | tf_op jit(solution)/shard_map/ppermute | solution.py:24
  128.7 0.0 collective-permute-done.17
  128.7 0.8 collective-permute-done.18
  129.5 0.1 fusion.17
  129.6 2.4 %collective-permute-start.19 = (f32[66,1]{1,0:T(8,128)S(1)}, f32[66,1]{1,0:T(8,128)S(1)}, u32[]{:S(2)}, u32[]{:S(2)}) collective-permute-start(f32[66,1]{1,0:T(8,128)S(1)} %get-tuple-element.30), channel_id=1, source_target_pairs={{1,0},{2,1},{3,2},{5,4},{6,5},{7,6},{9,8},{10,9},{11,10},{13,12},{... | collective-permute-start | bytes 800 | tf_op jit(solution)/shard_map/ppermute | solution.py:25
  132.0 3.4 %collective-permute-start.20 = (f32[66,1]{1,0:T(8,128)S(1)}, f32[66,1]{1,0:T(8,128)S(1)}, u32[]{:S(2)}, u32[]{:S(2)}) collective-permute-start(f32[66,1]{1,0:T(8,128)S(1)} %get-tuple-element.29), channel_id=1, source_target_pairs={{0,1},{1,2},{2,3},{4,5},{5,6},{6,7},{8,9},{9,10},{10,11},{12,13},{... | collective-permute-start | bytes 800 | tf_op jit(solution)/shard_map/ppermute | solution.py:24
  135.5 0.0 collective-permute-done.19
  135.5 2.4 %collective-permute-done.20 = f32[66,1]{1,0:T(8,128)S(1)} collective-permute-done((f32[66,1]{1,0:T(8,128)S(1)}, f32[66,1]{1,0:T(8,128)S(1)}, u32[]{:S(2)}, u32[]{:S(2)}) %collective-permute-start.20) | collective-permute-done | bytes 296 | tf_op jit(solution)/shard_map/ppermute | solution.py:24
  137.9 0.1 maximum_maximum_fusion
  138.0 0.8 fusion.8
  (11 shorter events, 0.2 us)
Async XLA Ops:
  1.2 10.4 %copy-start.1 = (bf16[1,2,3,64,256]{4,3,2,1,0:T(8,128)(2,1)S(1)}, bf16[1,2,3,64,256]{4,3,2,1,0:T(8,128)(2,1)}, u32[]{:S(2)}) copy-start(bf16[1,2,3,64,256]{4,3,2,1,0:T(8,128)(2,1)} %param.10) | copy-start | bytes 589828
  3.4 13.8 %collective-permute-start = (f32[264,256]{1,0:T(8,128)}, f32[264,256]{1,0:T(8,128)S(1)}, u32[]{:S(2)}, u32[]{:S(2)}) collective-permute-start(f32[264,256]{1,0:T(8,128)} %get-tuple-element.11), channel_id=1, source_target_pairs={{0,1},{1,2},{3,0},{4,5},{5,6},{7,4},{8,9},{9,10},{11,8},{12,13},{1... | collective-permute-start | bytes 811016 | tf_op jit(solution)/shard_map/ppermute | solution.py:239
  6.9 13.7 %collective-permute-start.1 = (f32[264,256]{1,0:T(8,128)}, f32[264,256]{1,0:T(8,128)S(1)}, u32[]{:S(2)}, u32[]{:S(2)}) collective-permute-start(f32[264,256]{1,0:T(8,128)} %get-tuple-element.12), channel_id=1, source_target_pairs={{0,2},{2,0},{3,1},{4,6},{6,4},{7,5},{8,10},{10,8},{11,9},{12,14},{... | collective-permute-start | bytes 811016 | tf_op jit(solution)/shard_map/ppermute | solution.py:239
  8.2 23.1 %collective-permute-start.2 = (f32[264,256]{1,0:T(8,128)}, f32[264,256]{1,0:T(8,128)S(1)}, u32[]{:S(2)}, u32[]{:S(2)}) collective-permute-start(f32[264,256]{1,0:T(8,128)} %get-tuple-element.13), channel_id=1, source_target_pairs={{1,0},{2,1},{3,2},{5,4},{6,5},{7,6},{9,8},{10,9},{11,10},{13,12},{... | collective-permute-start | bytes 811016 | tf_op jit(solution)/shard_map/ppermute | solution.py:239
  11.6 3.6 %collective-permute-start.10 = (bf16[6,1,256]{2,1,0:T(2,128)(2,1)S(1)}, bf16[6,1,256]{2,1,0:T(2,128)(2,1)S(1)}, u32[]{:S(2)}, u32[]{:S(2)}) collective-permute-start(bf16[6,1,256]{2,1,0:T(2,128)(2,1)S(1)} %get-tuple-element.27), channel_id=1, source_target_pairs={{0,4},{1,5},{2,6},{3,7},{8,12},{9,13},{10,14},{11,15},{16,20},{17,... | collective-permute-start | bytes 9224 | tf_op jit(solution)/shard_map/ppermute | solution.py:24
  12.9 2.2 %copy-start.2 = (f32[64,256]{1,0:T(8,128)S(1)}, f32[64,256]{1,0:T(8,128)}, u32[]{:S(2)}) copy-start(f32[64,256]{1,0:T(8,128)} %density.1) | copy-start | bytes 196612
  12.9 2.2 %copy-start.3 = (f32[64,256]{1,0:T(8,128)S(1)}, f32[64,256]{1,0:T(8,128)}, u32[]{:S(2)}) copy-start(f32[64,256]{1,0:T(8,128)} %mass.1) | copy-start | bytes 196612
  13.0 2.2 %copy-start.4 = (f32[64,256]{1,0:T(8,128)S(1)}, f32[64,256]{1,0:T(8,128)}, u32[]{:S(2)}) copy-start(f32[64,256]{1,0:T(8,128)} %stiffness.1) | copy-start | bytes 196612
  13.0 4.2 %collective-permute-start.11 = (bf16[6,1,256]{2,1,0:T(2,128)(2,1)S(1)}, bf16[6,1,256]{2,1,0:T(2,128)(2,1)S(1)}, u32[]{:S(2)}, u32[]{:S(2)}) collective-permute-start(bf16[6,1,256]{2,1,0:T(2,128)(2,1)S(1)} %get-tuple-element.28), channel_id=1, source_target_pairs={{4,0},{5,1},{6,2},{7,3},{12,8},{13,9},{14,10},{15,11},{20,16},{21,... | collective-permute-start | bytes 9224 | tf_op jit(solution)/shard_map/ppermute | solution.py:25
  15.1 1.0 copy-start
  16.1 29.6 %collective-permute-start.3 = (f32[264,256]{1,0:T(8,128)S(1)}, f32[264,256]{1,0:T(8,128)S(1)}, u32[]{:S(2)}, u32[]{:S(2)}) collective-permute-start(f32[264,256]{1,0:T(8,128)S(1)} %copy-done), channel_id=1, source_target_pairs={{0,4},{4,0},{1,5},{5,1},{2,6},{6,2},{3,7},{7,3},{8,12},{12,8},{9,1... | collective-permute-start | bytes 811016 | tf_op jit(solution)/shard_map/ppermute | solution.py:242
  17.3 28.4 %collective-permute-start.4 = (f32[264,256]{1,0:T(8,128)S(1)}, f32[264,256]{1,0:T(8,128)S(1)}, u32[]{:S(2)}, u32[]{:S(2)}) collective-permute-start(f32[264,256]{1,0:T(8,128)S(1)} %collective-permute-done.refs_1_), channel_id=1, source_target_pairs={{0,4},{4,0},{1,5},{5,1},{2,6},{6,2},{3,7},{7,3},{8,12},{12,8},{9,1... | collective-permute-start | bytes 811016 | tf_op jit(solution)/shard_map/ppermute | solution.py:242
  20.7 25.1 %collective-permute-start.5 = (f32[264,256]{1,0:T(8,128)S(1)}, f32[264,256]{1,0:T(8,128)S(1)}, u32[]{:S(2)}, u32[]{:S(2)}) collective-permute-start(f32[264,256]{1,0:T(8,128)S(1)} %collective-permute-done.1.refs_2_), channel_id=1, source_target_pairs={{0,4},{4,0},{1,5},{5,1},{2,6},{6,2},{3,7},{7,3},{8,12},{12,8},{9,1... | collective-permute-start | bytes 811016 | tf_op jit(solution)/shard_map/ppermute | solution.py:242
  31.4 14.4 %collective-permute-start.6 = (f32[264,256]{1,0:T(8,128)S(1)}, f32[264,256]{1,0:T(8,128)S(1)}, u32[]{:S(2)}, u32[]{:S(2)}) collective-permute-start(f32[264,256]{1,0:T(8,128)S(1)} %collective-permute-done.2.refs_3_), channel_id=1, source_target_pairs={{0,4},{4,0},{1,5},{5,1},{2,6},{6,2},{3,7},{7,3},{8,12},{12,8},{9,1... | collective-permute-start | bytes 811016 | tf_op jit(solution)/shard_map/ppermute | solution.py:242
  31.5 7.3 %collective-permute-start.12 = (bf16[6,66,1]{2,1,0:T(8,128)(2,1)S(1)}, bf16[6,66,1]{2,1,0:T(8,128)(2,1)S(1)}, u32[]{:S(2)}, u32[]{:S(2)}) collective-permute-start(bf16[6,66,1]{2,1,0:T(8,128)(2,1)S(1)} %get-tuple-element.25), channel_id=1, source_target_pairs={{0,1},{1,2},{2,3},{4,5},{5,6},{6,7},{8,9},{9,10},{10,11},{12,13},{... | collective-permute-start | bytes 2384 | tf_op jit(solution)/shard_map/ppermute | solution.py:24
  38.8 6.6 %collective-permute-start.13 = (bf16[6,66,1]{2,1,0:T(8,128)(2,1)S(1)}, bf16[6,66,1]{2,1,0:T(8,128)(2,1)S(1)}, u32[]{:S(2)}, u32[]{:S(2)}) collective-permute-start(bf16[6,66,1]{2,1,0:T(8,128)(2,1)S(1)} %get-tuple-element.26), channel_id=1, source_target_pairs={{1,0},{2,1},{3,2},{5,4},{6,5},{7,6},{9,8},{10,9},{11,10},{13,12},{... | collective-permute-start | bytes 2384 | tf_op jit(solution)/shard_map/ppermute | solution.py:25
  102.7 8.3 %collective-permute-start.7 = (f32[2,64,256]{2,1,0:T(8,128)S(1)}, f32[2,64,256]{2,1,0:T(8,128)S(1)}, u32[]{:S(2)}, u32[]{:S(2)}) collective-permute-start(f32[2,64,256]{2,1,0:T(8,128)S(1)} %get-tuple-element.15), channel_id=1, source_target_pairs={{0,1},{1,2},{2,3},{4,5},{5,6},{6,7},{8,9},{9,10},{10,11},{12,13},{... | collective-permute-start | bytes 393224 | tf_op jit(solution)/shard_map/ppermute | solution.py:269
  105.0 10.4 %collective-permute-start.8 = (f32[2,64,256]{2,1,0:T(8,128)S(1)}, f32[2,64,256]{2,1,0:T(8,128)S(1)}, u32[]{:S(2)}, u32[]{:S(2)}) collective-permute-start(f32[2,64,256]{2,1,0:T(8,128)S(1)} %get-tuple-element.16), channel_id=1, source_target_pairs={{0,2},{1,3},{2,0},{4,6},{5,7},{6,4},{8,10},{9,11},{10,8},{12,14},{... | collective-permute-start | bytes 393224 | tf_op jit(solution)/shard_map/ppermute | solution.py:269
  106.4 9.1 %collective-permute-start.9 = (f32[2,64,256]{2,1,0:T(8,128)S(1)}, f32[2,64,256]{2,1,0:T(8,128)S(1)}, u32[]{:S(2)}, u32[]{:S(2)}) collective-permute-start(f32[2,64,256]{2,1,0:T(8,128)S(1)} %get-tuple-element.17), channel_id=1, source_target_pairs={{0,3},{1,0},{2,1},{4,7},{5,4},{6,5},{8,11},{9,8},{10,9},{12,15},{1... | collective-permute-start | bytes 393224 | tf_op jit(solution)/shard_map/ppermute | solution.py:269
  116.5 5.3 %collective-permute-start.14 = (f32[64,256]{1,0:T(8,128)S(1)}, f32[64,256]{1,0:T(8,128)S(1)}, u32[]{:S(2)}, u32[]{:S(2)}) collective-permute-start(f32[64,256]{1,0:T(8,128)S(1)} %neg.3), channel_id=1, source_target_pairs={{0,8},{8,16},{16,24},{24,0},{1,9},{9,17},{17,25},{25,1},{2,10},{10... | collective-permute-start | bytes 196616 | tf_op jit(solution)/shard_map/ppermute | solution.py:337
  118.6 4.3 %collective-permute-start.15 = (f32[64,256]{1,0:T(8,128)S(1)}, f32[64,256]{1,0:T(8,128)S(1)}, u32[]{:S(2)}, u32[]{:S(2)}) collective-permute-start(f32[64,256]{1,0:T(8,128)S(1)} %neg.3), channel_id=1, source_target_pairs={{0,16},{8,24},{16,0},{24,8},{1,17},{9,25},{17,1},{25,9},{2,18},{10... | collective-permute-start | bytes 196616 | tf_op jit(solution)/shard_map/ppermute | solution.py:337
  120.1 4.3 %collective-permute-start.16 = (f32[64,256]{1,0:T(8,128)S(1)}, f32[64,256]{1,0:T(8,128)S(1)}, u32[]{:S(2)}, u32[]{:S(2)}) collective-permute-start(f32[64,256]{1,0:T(8,128)S(1)} %neg.3), channel_id=1, source_target_pairs={{0,24},{8,0},{16,8},{24,16},{1,25},{9,1},{17,9},{25,17},{2,26},{10... | collective-permute-start | bytes 196616 | tf_op jit(solution)/shard_map/ppermute | solution.py:337
  124.4 4.3 %collective-permute-start.17 = (f32[1,256]{1,0:T(1,128)S(1)}, f32[1,256]{1,0:T(1,128)S(1)}, u32[]{:S(2)}, u32[]{:S(2)}) collective-permute-start(f32[1,256]{1,0:T(1,128)S(1)} %get-tuple-element.34), channel_id=1, source_target_pairs={{4,0},{5,1},{6,2},{7,3},{12,8},{13,9},{14,10},{15,11},{20,16},{21,... | collective-permute-start | bytes 3080 | tf_op jit(solution)/shard_map/ppermute | solution.py:25
  125.7 3.8 %collective-permute-start.18 = (f32[1,256]{1,0:T(1,128)S(1)}, f32[1,256]{1,0:T(1,128)S(1)}, u32[]{:S(2)}, u32[]{:S(2)}) collective-permute-start(f32[1,256]{1,0:T(1,128)S(1)} %get-tuple-element.33), channel_id=1, source_target_pairs={{0,4},{1,5},{2,6},{3,7},{8,12},{9,13},{10,14},{11,15},{16,20},{17,... | collective-permute-start | bytes 3080 | tf_op jit(solution)/shard_map/ppermute | solution.py:24
  129.6 5.9 %collective-permute-start.19 = (f32[66,1]{1,0:T(8,128)S(1)}, f32[66,1]{1,0:T(8,128)S(1)}, u32[]{:S(2)}, u32[]{:S(2)}) collective-permute-start(f32[66,1]{1,0:T(8,128)S(1)} %get-tuple-element.30), channel_id=1, source_target_pairs={{1,0},{2,1},{3,2},{5,4},{6,5},{7,6},{9,8},{10,9},{11,10},{13,12},{... | collective-permute-start | bytes 800 | tf_op jit(solution)/shard_map/ppermute | solution.py:25
  132.0 5.9 %collective-permute-start.20 = (f32[66,1]{1,0:T(8,128)S(1)}, f32[66,1]{1,0:T(8,128)S(1)}, u32[]{:S(2)}, u32[]{:S(2)}) collective-permute-start(f32[66,1]{1,0:T(8,128)S(1)} %get-tuple-element.29), channel_id=1, source_target_pairs={{0,1},{1,2},{2,3},{4,5},{5,6},{6,7},{8,9},{9,10},{10,11},{12,13},{... | collective-permute-start | bytes 800 | tf_op jit(solution)/shard_map/ppermute | solution.py:24

commit v2 on v1

--- a/solution.py
+++ b/solution.py
@@ -75,39 +75,37 @@
     blocks = n_i * n_j
     msgs, refs = refs[: blocks], refs[blocks:]
     outs, refs = refs[:n_j], refs[n_j:]
-    field, rhs, stiff, gain, lag, info, take, lane_of, put, weights, picked, pages = refs
+    field, rhs, stiff, gain, lag, info, weights, pick, rowmask, spread, place, group, values, pages = refs
     rows = rhs.shape[2] // 2
     slots = blocks * cap
     me_i, me_j = pos[0], pos[1]
     w = omega[0]
 
-    def both(x):
-        return x[:, :LANES], x[:, LANES:]
-
     order = [(a, s) for a in range(n_i) for s in range(n_j)]
     index = [lax.rem(me_i + a, n_i) * n_j + lax.rem(me_j + n_j - s, n_j) for a, s in order]
     for msg, b in zip(msgs, index):
         info[b] = msg[4 * rows :, :]
-    lines = jnp.concatenate([info[b] for b in range(blocks)], axis=0)
-    columns = jnp.transpose(lines)
-    lane = lax.broadcasted_iota(jnp.int32, (slots, LANES), 1)
-    depth = lax.broadcasted_iota(jnp.int32, (2 * rows, slots), 0)
-
-    def column(b, kind):
-        return jnp.broadcast_to(columns[:, b * 8 + kind : b * 8 + kind + 1], (slots, LANES))
+    depth = lax.broadcasted_iota(jnp.int32, (LANES, slots), 0)
+    chunk = lax.broadcasted_iota(jnp.int32, (blocks, slots), 1) // cap
+    source = lax.broadcasted_iota(jnp.int32, (blocks, slots), 0)
+
+    def one_hot(line):
+        return (jnp.broadcast_to(line.astype(jnp.int32), depth.shape) == depth).astype(F32)
 
     for b in range(blocks):
-        pick = (column(b, 0).astype(jnp.int32) == lane).astype(F32).astype(BF16)
-        take[b] = jnp.concatenate([pick, pick], axis=1)
-        lane_of[b] = column(b, 1).astype(jnp.int32)
-        target = info[b, 2:3, :].astype(jnp.int32)
-        spread = (jnp.broadcast_to(target, depth.shape) == depth).astype(F32).astype(BF16)
-        put[b] = jnp.concatenate([spread, spread], axis=1)
-        weighted = jnp.where(column(b, 3).astype(jnp.int32) == lane, column(b, 4), 0.0)
-        for p in range(blocks):
-            weights[p, b * cap : (b + 1) * cap, :] = weighted[p * cap : (p + 1) * cap, :]
-        high, low = split(weighted)
-        gain[b] = jnp.dot(put[b], jnp.concatenate([high, low], axis=0), preferred_element_type=F32)
+        line = info[b]
+        line = pltpu.roll(line, b * cap, 1) if b else line
+        lane_in = one_hot(line[1:2]).astype(BF16)
+        pick[b] = jnp.concatenate([lane_in, lane_in], axis=0)
+        rowmask[b] = one_hot(line[0:1])
+        row_out = one_hot(line[2:3])
+        spread[b] = row_out.astype(BF16)
+        lane_out = jnp.transpose(one_hot(line[3:4])).astype(BF16)
+        place[b] = jnp.concatenate([lane_out, lane_out], axis=0)
+        group[b] = (chunk == (source + b) % blocks).astype(F32)
+        weights[pl.ds(b, 1), :] = line[4:5]
+        high, low = split(row_out * line[4:5])
+        gain[b] = jnp.dot(jnp.concatenate([high, low], axis=1), place[b], preferred_element_type=F32)
 
     for msg, b in zip(msgs, index):
         for u in range(2):
@@ -130,25 +128,20 @@
         now = lax.rem(step, 2)
         then = 1 - now
         for b in range(blocks):
-            re_h, re_l = split(field[now, b, 0])
-            im_h, im_l = split(field[now, b, 1])
-            source = jnp.concatenate(
-                [jnp.concatenate([re_h, im_h], axis=1), jnp.concatenate([re_l, im_l], axis=1)], axis=0
-            )
-            got = jnp.dot(take[b], source, preferred_element_type=F32)
-            at_lane, wt = lane_of[b], weights[b]
-            for part, g in enumerate(both(got)):
-                value = jnp.take_along_axis(g, at_lane, axis=1, mode="promise_in_bounds") * wt
-                high, low = split(value)
-                lanes = slice(part * LANES, (part + 1) * LANES)
-                for q in range(blocks):
-                    chunk = slice(q * cap, (q + 1) * cap)
-                    picked[q, b * cap : (b + 1) * cap, lanes] = high[chunk]
-                    picked[q, slots + b * cap : slots + (b + 1) * cap, lanes] = low[chunk]
+            whole = jnp.concatenate([field[now, b, 0], field[now, b, 1]], axis=0)
+            got = jnp.dot(jnp.concatenate(split(whole), axis=1), pick[b], preferred_element_type=F32)
+            for part in range(2):
+                mine = got[part * LANES : (part + 1) * LANES] * rowmask[b]
+                values[part, pl.ds(b, 1), :] = jnp.sum(mine, axis=0, keepdims=True)
         for i in range(n_i):
             for j in range(n_j):
                 b = i * n_j + j
-                mortar = jnp.dot(put[b], picked[b], preferred_element_type=F32)
+                left = []
+                for part in range(2):
+                    arrived = jnp.sum(values[part] * group[b], axis=0, keepdims=True)
+                    high, low = split(arrived * weights[b : b + 1, :])
+                    left.append(jnp.concatenate([spread[b] * high, spread[b] * low], axis=1))
+                mortar = jnp.dot(jnp.concatenate(left, axis=0), place[b], preferred_element_type=F32)
                 h = [[None, None], [None, None]]
                 for part in range(2):
                     whole = field[now, b, part]
@@ -177,7 +170,7 @@
                         around += jnp.concatenate([top, own[:-8]], axis=0)
                         around += jnp.concatenate([own[8:], bottom], axis=0)
                         at = slice(u * rows, (u + 1) * rows)
-                        m = mortar[at, part * LANES : (part + 1) * LANES]
+                        m = mortar[part * 2 * rows + u * rows : part * 2 * rows + (u + 1) * rows]
                         h[part][u] = m + rhs[b, part, at] + stiff[b, at] * around
                 for u in range(2):
                     at = slice(u * rows, (u + 1) * rows)
@@ -254,11 +247,13 @@
             pltpu.VMEM(block, F32),
             pltpu.VMEM(block, F32),
             pltpu.VMEM((blocks, 8, cy), F32),
-            pltpu.VMEM((blocks, slots, 4 * rows), BF16),
-            pltpu.VMEM((blocks, slots, LANES), jnp.int32),
-            pltpu.VMEM((blocks, 2 * rows, 2 * slots), BF16),
-            pltpu.VMEM((blocks, slots, LANES), F32),
-            pltpu.VMEM((blocks, 2 * slots, 2 * LANES), BF16),
+            pltpu.VMEM((blocks, slots), F32),
+            pltpu.VMEM((blocks, 2 * LANES, slots), BF16),
+            pltpu.VMEM((blocks, 2 * rows, slots), F32),
+            pltpu.VMEM((blocks, 2 * rows, slots), BF16),
+            pltpu.VMEM((blocks, 2 * slots, LANES), BF16),
+            pltpu.VMEM((blocks, blocks, slots), F32),
+            pltpu.VMEM((2, blocks, slots), F32),
             pltpu.VMEM((8, rows, LANES), F32),
         ],
         compiler_params=pltpu.CompilerParams(vmem_limit_bytes=40 * 1024 * 1024),
@@ -313,7 +308,7 @@
     dstiff = 3.0 * density**2 * stiffness
     rhs = adjoint_rhs.reshape(6, rows_x, rows_y)
     n_i, n_j = lax.axis_size("mx"), lax.axis_size("my")
-    fits = n_i == 2 and PARTS <= n_j <= 4 and rows_x % 64 == 0 and rows_y == 2 * LANES
+    fits = n_i == 2 and PARTS <= n_j <= 4 and 2 * rows_x == LANES and rows_y == 2 * LANES
     fits = fits and send_rows.shape[1] == rows_y
     system = (rhs, density, stiffness, mass, omega, send_rows, recv_rows, mortar_weight)
     field = (solve if fits else solve_split)(*system)

time: 140 us -> 113 us (0.81)
  Pallas kernels: 59.2 us -> 31.9 us
    pallas_call x1, Pallas kernels: 56.9 us -> 29.6 us  [solve(): pl.pallas_call(functools.partial(sweep_kernel, n_i, n_j, cap), out_shape=...]
where the time goes in v2:
time: 113 us; the launch traced here: 111 us
  starting transfers between devices  38.9 us (34%)
  waiting for transfers between devices  34.7 us (31%)
  Pallas kernels  31.9 us (28%)
  other arithmetic  3.3 us (3%)
  between operations  1.67 us (1%)
    pallas_call x1, Pallas kernels, solve(): pl.pallas_call(functools.partial(sweep_kernel, n_i, n_j, cap), out_shape=...  29.6 us
    ppermute x3, waiting for transfers between devices, solve(): msgs.append(lax.ppermute(own[s], 'my', pairs))  14 us
    ppermute x4, starting transfers between devices, extended(): before = lax.ppermute(last, axis, up)  9.65 us
    ppermute x4, waiting for transfers between devices, extended(): before = lax.ppermute(last, axis, up)  8.62 us
    ppermute x3, starting transfers between devices, solve(): msgs.append(lax.ppermute(own[s], 'my', pairs))  8.13 us
    ppermute x3, starting transfers between devices, solve(): parts.append(lax.ppermute(outs[s], 'my', pairs))  7.77 us
    ppermute x4, starting transfers between devices, extended(): after = lax.ppermute(first, axis, down)  7.05 us
    ppermute x3, starting transfers between devices, on_device(): lax.ppermute(sens, 'freq', [(a, (a + s) % size) for a in range(size)])  5.05 us
  transfers between devices with their start and end apart: 21, of which 11 were waited for; matrix products, arithmetic and copies ran while one was open for 1% of the time, Pallas kernels for 0%

profile of v2, /device:TPU:8, one launch (start us, length us, event | category | flops | bytes accessed | tf_op | source)
XLA Modules:
  0.0 111.5 jit_solution(15365927711337099430)
XLA Ops:
  0.6 0.6 fusion.12.comps
  1.2 2.2 %pack.1 = (f32[264,256]{1,0:T(8,128)}, f32[264,256]{1,0:T(8,128)}, f32[264,256]{1,0:T(8,128)}, f32[264,256]{1,0:T(8,128)}) custom-call(s32[4]{0:T(128)} %fusion.12.comps, f32[6,64,256]{2,1,0:T(8,128)} %bitcast.31, f32[64,256]{1,0:T(8,128)} %density.1, f32[64,256]{1,0:T(8,128)} %stiffness.1, f32[64,256]{1,0:T(8,128)} %mass.1, s32[1,256]{1,0:T(1,128)} %send.1, ...), custom_call_target="tpu_custom_call" | custom-call | tf_op jit(solution)/shard_map/pack/pallas_call | solution.py:222
  3.4 3.5 %collective-permute-start = (f32[264,256]{1,0:T(8,128)}, f32[264,256]{1,0:T(8,128)S(1)}, u32[]{:S(2)}, u32[]{:S(2)}) collective-permute-start(f32[264,256]{1,0:T(8,128)} %get-tuple-element.11), channel_id=1, source_target_pairs={{0,1},{1,2},{3,0},{4,5},{5,6},{7,4},{8,9},{9,10},{11,8},{12,13},{1... | collective-permute-start | bytes 811016 | tf_op jit(solution)/shard_map/ppermute | solution.py:232
  6.9 1.3 %collective-permute-start.1 = (f32[264,256]{1,0:T(8,128)}, f32[264,256]{1,0:T(8,128)S(1)}, u32[]{:S(2)}, u32[]{:S(2)}) collective-permute-start(f32[264,256]{1,0:T(8,128)} %get-tuple-element.12), channel_id=1, source_target_pairs={{0,2},{2,0},{3,1},{4,6},{6,4},{7,5},{8,10},{10,8},{11,9},{12,14},{... | collective-permute-start | bytes 811016 | tf_op jit(solution)/shard_map/ppermute | solution.py:232
  8.2 3.4 %collective-permute-start.2 = (f32[264,256]{1,0:T(8,128)}, f32[264,256]{1,0:T(8,128)S(1)}, u32[]{:S(2)}, u32[]{:S(2)}) collective-permute-start(f32[264,256]{1,0:T(8,128)} %get-tuple-element.13), channel_id=1, source_target_pairs={{1,0},{2,1},{3,2},{5,4},{6,5},{7,6},{9,8},{10,9},{11,10},{13,12},{... | collective-permute-start | bytes 811016 | tf_op jit(solution)/shard_map/ppermute | solution.py:232
  11.6 0.0 copy-done.1
  11.6 1.3 %collective-permute-start.10 = (bf16[6,1,256]{2,1,0:T(2,128)(2,1)S(1)}, bf16[6,1,256]{2,1,0:T(2,128)(2,1)S(1)}, u32[]{:S(2)}, u32[]{:S(2)}) collective-permute-start(bf16[6,1,256]{2,1,0:T(2,128)(2,1)S(1)} %get-tuple-element.27), channel_id=1, source_target_pairs={{0,4},{1,5},{2,6},{3,7},{8,12},{9,13},{10,14},{11,15},{16,20},{17,... | collective-permute-start | bytes 9224 | tf_op jit(solution)/shard_map/ppermute | solution.py:24
  12.9 0.0 copy-start.2
  12.9 0.0 copy-start.3
  13.0 0.0 copy-start.4
  13.0 1.4 %collective-permute-start.11 = (bf16[6,1,256]{2,1,0:T(2,128)(2,1)S(1)}, bf16[6,1,256]{2,1,0:T(2,128)(2,1)S(1)}, u32[]{:S(2)}, u32[]{:S(2)}) collective-permute-start(bf16[6,1,256]{2,1,0:T(2,128)(2,1)S(1)} %get-tuple-element.28), channel_id=1, source_target_pairs={{4,0},{5,1},{6,2},{7,3},{12,8},{13,9},{14,10},{15,11},{20,16},{21,... | collective-permute-start | bytes 9224 | tf_op jit(solution)/shard_map/ppermute | solution.py:25
  15.1 0.0 copy-done.2
  15.1 0.0 copy-done.3
  15.1 0.0 copy-done.4
  15.1 0.0 copy-start
  15.2 0.1 pad_add_fusion.pos
  15.3 0.0 collective-permute-done.10
  15.3 0.8 copy-done
  16.1 1.1 %collective-permute-start.3 = (f32[264,256]{1,0:T(8,128)S(1)}, f32[264,256]{1,0:T(8,128)S(1)}, u32[]{:S(2)}, u32[]{:S(2)}) collective-permute-start(f32[264,256]{1,0:T(8,128)S(1)} %copy-done), channel_id=1, source_target_pairs={{0,4},{4,0},{1,5},{5,1},{2,6},{6,2},{3,7},{7,3},{8,12},{12,8},{9,1... | collective-permute-start | bytes 811016 | tf_op jit(solution)/shard_map/ppermute | solution.py:235
  17.2 0.0 collective-permute-done.11
  17.2 0.1 pad_maximum_fusion.2
  17.3 0.0 collective-permute-done.refs_1_
  17.3 0.1 collective-permute-start.4
  17.4 3.3 %collective-permute-done.1.refs_2_ = f32[264,256]{1,0:T(8,128)S(1)} collective-permute-done((f32[264,256]{1,0:T(8,128)}, f32[264,256]{1,0:T(8,128)S(1)}, u32[]{:S(2)}, u32[]{:S(2)}) %collective-permute-start.1) | collective-permute-done | bytes 270368 | tf_op jit(solution)/shard_map/ppermute | solution.py:232
  20.7 0.0 collective-permute-start.5
  20.7 10.7 %collective-permute-done.2.refs_3_ = f32[264,256]{1,0:T(8,128)S(1)} collective-permute-done((f32[264,256]{1,0:T(8,128)}, f32[264,256]{1,0:T(8,128)S(1)}, u32[]{:S(2)}, u32[]{:S(2)}) %collective-permute-start.2) | collective-permute-done | bytes 270368 | tf_op jit(solution)/shard_map/ppermute | solution.py:232
  31.4 0.0 collective-permute-start.6
  31.4 0.1 fusion.15
  31.5 1.9 %collective-permute-start.12 = (bf16[6,66,1]{2,1,0:T(8,128)(2,1)S(1)}, bf16[6,66,1]{2,1,0:T(8,128)(2,1)S(1)}, u32[]{:S(2)}, u32[]{:S(2)}) collective-permute-start(bf16[6,66,1]{2,1,0:T(8,128)(2,1)S(1)} %get-tuple-element.25), channel_id=1, source_target_pairs={{0,1},{1,2},{2,3},{4,5},{5,6},{6,7},{8,9},{9,10},{10,11},{12,13},{... | collective-permute-start | bytes 2384 | tf_op jit(solution)/shard_map/ppermute | solution.py:24
  33.4 5.4 %collective-permute-done.12 = bf16[6,66,1]{2,1,0:T(8,128)(2,1)S(1)} collective-permute-done((bf16[6,66,1]{2,1,0:T(8,128)(2,1)S(1)}, bf16[6,66,1]{2,1,0:T(8,128)(2,1)S(1)}, u32[]{:S(2)}, u32[]{:S(2)}) %collective-permute-start.12) | collective-permute-done | bytes 824 | tf_op jit(solution)/shard_map/ppermute | solution.py:24
  38.8 1.9 %collective-permute-start.13 = (bf16[6,66,1]{2,1,0:T(8,128)(2,1)S(1)}, bf16[6,66,1]{2,1,0:T(8,128)(2,1)S(1)}, u32[]{:S(2)}, u32[]{:S(2)}) collective-permute-start(bf16[6,66,1]{2,1,0:T(8,128)(2,1)S(1)} %get-tuple-element.26), channel_id=1, source_target_pairs={{1,0},{2,1},{3,2},{5,4},{6,5},{7,6},{9,8},{10,9},{11,10},{13,12},{... | collective-permute-start | bytes 2384 | tf_op jit(solution)/shard_map/ppermute | solution.py:25
  40.8 4.7 %collective-permute-done.13 = bf16[6,66,1]{2,1,0:T(8,128)(2,1)S(1)} collective-permute-done((bf16[6,66,1]{2,1,0:T(8,128)(2,1)S(1)}, bf16[6,66,1]{2,1,0:T(8,128)(2,1)S(1)}, u32[]{:S(2)}, u32[]{:S(2)}) %collective-permute-start.13) | collective-permute-done | bytes 824 | tf_op jit(solution)/shard_map/ppermute | solution.py:25
  45.5 0.3 maximum_convert_fusion
  45.7 0.0 collective-permute-done.3.refs_4_
  45.7 0.0 collective-permute-done.4.refs_5_
  45.7 0.0 collective-permute-done.5.refs_6_
  45.8 0.0 collective-permute-done.6.refs_7_
  45.8 29.6 %sweeps.1 = (f32[2,64,256]{2,1,0:T(8,128)S(1)}, f32[2,64,256]{2,1,0:T(8,128)S(1)}, f32[2,64,256]{2,1,0:T(8,128)S(1)}, f32[2,64,256]{2,1,0:T(8,128)S(1)}) custom-call(s32[2]{0:T(128)S(1)} %pad_add_fusion.pos, f32[1]{0:T(128)S(6)} %copy.11.omega, f32[264,256]{1,0:T(8,128)S(1)} %copy-done, f32[264,256]{1,0:T(8,128)S(1)} %collective-permute-done.refs_1_, ...), custom_call_target="tpu_custom_call" | custom-call | tf_op jit(solution)/shard_map/sweeps/pallas_call | solution.py:238
  75.4 2.3 %collective-permute-start.7 = (f32[2,64,256]{2,1,0:T(8,128)S(1)}, f32[2,64,256]{2,1,0:T(8,128)S(1)}, u32[]{:S(2)}, u32[]{:S(2)}) collective-permute-start(f32[2,64,256]{2,1,0:T(8,128)S(1)} %get-tuple-element.15), channel_id=1, source_target_pairs={{0,1},{1,2},{2,3},{4,5},{5,6},{6,7},{8,9},{9,10},{10,11},{12,13},{... | collective-permute-start | bytes 393224 | tf_op jit(solution)/shard_map/ppermute | solution.py:264
  77.8 1.3 %collective-permute-start.8 = (f32[2,64,256]{2,1,0:T(8,128)S(1)}, f32[2,64,256]{2,1,0:T(8,128)S(1)}, u32[]{:S(2)}, u32[]{:S(2)}) collective-permute-start(f32[2,64,256]{2,1,0:T(8,128)S(1)} %get-tuple-element.16), channel_id=1, source_target_pairs={{0,2},{1,3},{2,0},{4,6},{5,7},{6,4},{8,10},{9,11},{10,8},{12,14},{... | collective-permute-start | bytes 393224 | tf_op jit(solution)/shard_map/ppermute | solution.py:264
  79.1 4.1 %collective-permute-start.9 = (f32[2,64,256]{2,1,0:T(8,128)S(1)}, f32[2,64,256]{2,1,0:T(8,128)S(1)}, u32[]{:S(2)}, u32[]{:S(2)}) collective-permute-start(f32[2,64,256]{2,1,0:T(8,128)S(1)} %get-tuple-element.17), channel_id=1, source_target_pairs={{0,3},{1,0},{2,1},{4,7},{5,4},{6,5},{8,11},{9,8},{10,9},{12,15},{1... | collective-permute-start | bytes 393224 | tf_op jit(solution)/shard_map/ppermute | solution.py:264
  83.2 0.4 slice_add_fusion
  83.6 0.1 collective-permute-done.7
  83.7 4.5 %collective-permute-done.8 = f32[2,64,256]{2,1,0:T(8,128)S(1)} collective-permute-done((f32[2,64,256]{2,1,0:T(8,128)S(1)}, f32[2,64,256]{2,1,0:T(8,128)S(1)}, u32[]{:S(2)}, u32[]{:S(2)}) %collective-permute-start.8) | collective-permute-done | bytes 131104 | tf_op jit(solution)/shard_map/ppermute | solution.py:264
  88.1 0.0 collective-permute-done.9
  88.2 0.8 pad_maximum_fusion.1
  89.1 0.1 fusion.3
  89.2 2.1 %collective-permute-start.14 = (f32[64,256]{1,0:T(8,128)S(1)}, f32[64,256]{1,0:T(8,128)S(1)}, u32[]{:S(2)}, u32[]{:S(2)}) collective-permute-start(f32[64,256]{1,0:T(8,128)S(1)} %neg.3), channel_id=1, source_target_pairs={{0,8},{8,16},{16,24},{24,0},{1,9},{9,17},{17,25},{25,1},{2,10},{10... | collective-permute-start | bytes 196616 | tf_op jit(solution)/shard_map/ppermute | solution.py:332
  91.3 1.5 %collective-permute-start.15 = (f32[64,256]{1,0:T(8,128)S(1)}, f32[64,256]{1,0:T(8,128)S(1)}, u32[]{:S(2)}, u32[]{:S(2)}) collective-permute-start(f32[64,256]{1,0:T(8,128)S(1)} %neg.3), channel_id=1, source_target_pairs={{0,16},{8,24},{16,0},{24,8},{1,17},{9,25},{17,1},{25,9},{2,18},{10... | collective-permute-start | bytes 196616 | tf_op jit(solution)/shard_map/ppermute | solution.py:332
  92.8 1.4 %collective-permute-start.16 = (f32[64,256]{1,0:T(8,128)S(1)}, f32[64,256]{1,0:T(8,128)S(1)}, u32[]{:S(2)}, u32[]{:S(2)}) collective-permute-start(f32[64,256]{1,0:T(8,128)S(1)} %neg.3), channel_id=1, source_target_pairs={{0,24},{8,0},{16,8},{24,16},{1,25},{9,1},{17,9},{25,17},{2,26},{10... | collective-permute-start | bytes 196616 | tf_op jit(solution)/shard_map/ppermute | solution.py:332
  94.2 0.2 collective-permute-done.14
  94.5 1.1 collective-permute-done.15
  95.5 1.5 %collective-permute-done.16 = f32[64,256]{1,0:T(8,128)S(1)} collective-permute-done((f32[64,256]{1,0:T(8,128)S(1)}, f32[64,256]{1,0:T(8,128)S(1)}, u32[]{:S(2)}, u32[]{:S(2)}) %collective-permute-start.16) | collective-permute-done | bytes 65568 | tf_op jit(solution)/shard_map/ppermute | solution.py:332
  97.1 1.3 %collective-permute-start.17 = (f32[1,256]{1,0:T(1,128)S(1)}, f32[1,256]{1,0:T(1,128)S(1)}, u32[]{:S(2)}, u32[]{:S(2)}) collective-permute-start(f32[1,256]{1,0:T(1,128)S(1)} %get-tuple-element.34), channel_id=1, source_target_pairs={{4,0},{5,1},{6,2},{7,3},{12,8},{13,9},{14,10},{15,11},{20,16},{21,... | collective-permute-start | bytes 3080 | tf_op jit(solution)/shard_map/ppermute | solution.py:25
  98.4 3.0 %collective-permute-start.18 = (f32[1,256]{1,0:T(1,128)S(1)}, f32[1,256]{1,0:T(1,128)S(1)}, u32[]{:S(2)}, u32[]{:S(2)}) collective-permute-start(f32[1,256]{1,0:T(1,128)S(1)} %get-tuple-element.33), channel_id=1, source_target_pairs={{0,4},{1,5},{2,6},{3,7},{8,12},{9,13},{10,14},{11,15},{16,20},{17,... | collective-permute-start | bytes 3080 | tf_op jit(solution)/shard_map/ppermute | solution.py:24
  101.4 0.0 collective-permute-done.17
  101.4 0.8 collective-permute-done.18
  102.2 0.1 fusion.17
  102.3 2.4 %collective-permute-start.19 = (f32[66,1]{1,0:T(8,128)S(1)}, f32[66,1]{1,0:T(8,128)S(1)}, u32[]{:S(2)}, u32[]{:S(2)}) collective-permute-start(f32[66,1]{1,0:T(8,128)S(1)} %get-tuple-element.30), channel_id=1, source_target_pairs={{1,0},{2,1},{3,2},{5,4},{6,5},{7,6},{9,8},{10,9},{11,10},{13,12},{... | collective-permute-start | bytes 800 | tf_op jit(solution)/shard_map/ppermute | solution.py:25
  104.8 3.4 %collective-permute-start.20 = (f32[66,1]{1,0:T(8,128)S(1)}, f32[66,1]{1,0:T(8,128)S(1)}, u32[]{:S(2)}, u32[]{:S(2)}) collective-permute-start(f32[66,1]{1,0:T(8,128)S(1)} %get-tuple-element.29), channel_id=1, source_target_pairs={{0,1},{1,2},{2,3},{4,5},{5,6},{6,7},{8,9},{9,10},{10,11},{12,13},{... | collective-permute-start | bytes 800 | tf_op jit(solution)/shard_map/ppermute | solution.py:24
  108.2 0.0 collective-permute-done.19
  108.2 2.4 %collective-permute-done.20 = f32[66,1]{1,0:T(8,128)S(1)} collective-permute-done((f32[66,1]{1,0:T(8,128)S(1)}, f32[66,1]{1,0:T(8,128)S(1)}, u32[]{:S(2)}, u32[]{:S(2)}) %collective-permute-start.20) | collective-permute-done | bytes 296 | tf_op jit(solution)/shard_map/ppermute | solution.py:24
  110.6 0.1 maximum_maximum_fusion
  110.7 0.8 fusion.8
  (11 shorter events, 0.2 us)
Async XLA Ops:
  1.2 10.4 %copy-start.1 = (bf16[1,2,3,64,256]{4,3,2,1,0:T(8,128)(2,1)S(1)}, bf16[1,2,3,64,256]{4,3,2,1,0:T(8,128)(2,1)}, u32[]{:S(2)}) copy-start(bf16[1,2,3,64,256]{4,3,2,1,0:T(8,128)(2,1)} %param.10) | copy-start | bytes 589828
  3.4 13.8 %collective-permute-start = (f32[264,256]{1,0:T(8,128)}, f32[264,256]{1,0:T(8,128)S(1)}, u32[]{:S(2)}, u32[]{:S(2)}) collective-permute-start(f32[264,256]{1,0:T(8,128)} %get-tuple-element.11), channel_id=1, source_target_pairs={{0,1},{1,2},{3,0},{4,5},{5,6},{7,4},{8,9},{9,10},{11,8},{12,13},{1... | collective-permute-start | bytes 811016 | tf_op jit(solution)/shard_map/ppermute | solution.py:232
  6.9 13.7 %collective-permute-start.1 = (f32[264,256]{1,0:T(8,128)}, f32[264,256]{1,0:T(8,128)S(1)}, u32[]{:S(2)}, u32[]{:S(2)}) collective-permute-start(f32[264,256]{1,0:T(8,128)} %get-tuple-element.12), channel_id=1, source_target_pairs={{0,2},{2,0},{3,1},{4,6},{6,4},{7,5},{8,10},{10,8},{11,9},{12,14},{... | collective-permute-start | bytes 811016 | tf_op jit(solution)/shard_map/ppermute | solution.py:232
  8.2 23.1 %collective-permute-start.2 = (f32[264,256]{1,0:T(8,128)}, f32[264,256]{1,0:T(8,128)S(1)}, u32[]{:S(2)}, u32[]{:S(2)}) collective-permute-start(f32[264,256]{1,0:T(8,128)} %get-tuple-element.13), channel_id=1, source_target_pairs={{1,0},{2,1},{3,2},{5,4},{6,5},{7,6},{9,8},{10,9},{11,10},{13,12},{... | collective-permute-start | bytes 811016 | tf_op jit(solution)/shard_map/ppermute | solution.py:232
  11.6 3.6 %collective-permute-start.10 = (bf16[6,1,256]{2,1,0:T(2,128)(2,1)S(1)}, bf16[6,1,256]{2,1,0:T(2,128)(2,1)S(1)}, u32[]{:S(2)}, u32[]{:S(2)}) collective-permute-start(bf16[6,1,256]{2,1,0:T(2,128)(2,1)S(1)} %get-tuple-element.27), channel_id=1, source_target_pairs={{0,4},{1,5},{2,6},{3,7},{8,12},{9,13},{10,14},{11,15},{16,20},{17,... | collective-permute-start | bytes 9224 | tf_op jit(solution)/shard_map/ppermute | solution.py:24
  12.9 2.2 %copy-start.2 = (f32[64,256]{1,0:T(8,128)S(1)}, f32[64,256]{1,0:T(8,128)}, u32[]{:S(2)}) copy-start(f32[64,256]{1,0:T(8,128)} %density.1) | copy-start | bytes 196612
  12.9 2.2 %copy-start.3 = (f32[64,256]{1,0:T(8,128)S(1)}, f32[64,256]{1,0:T(8,128)}, u32[]{:S(2)}) copy-start(f32[64,256]{1,0:T(8,128)} %mass.1) | copy-start | bytes 196612
  13.0 2.2 %copy-start.4 = (f32[64,256]{1,0:T(8,128)S(1)}, f32[64,256]{1,0:T(8,128)}, u32[]{:S(2)}) copy-start(f32[64,256]{1,0:T(8,128)} %stiffness.1) | copy-start | bytes 196612
  13.0 4.2 %collective-permute-start.11 = (bf16[6,1,256]{2,1,0:T(2,128)(2,1)S(1)}, bf16[6,1,256]{2,1,0:T(2,128)(2,1)S(1)}, u32[]{:S(2)}, u32[]{:S(2)}) collective-permute-start(bf16[6,1,256]{2,1,0:T(2,128)(2,1)S(1)} %get-tuple-element.28), channel_id=1, source_target_pairs={{4,0},{5,1},{6,2},{7,3},{12,8},{13,9},{14,10},{15,11},{20,16},{21,... | collective-permute-start | bytes 9224 | tf_op jit(solution)/shard_map/ppermute | solution.py:25
  15.1 1.0 copy-start
  16.1 29.6 %collective-permute-start.3 = (f32[264,256]{1,0:T(8,128)S(1)}, f32[264,256]{1,0:T(8,128)S(1)}, u32[]{:S(2)}, u32[]{:S(2)}) collective-permute-start(f32[264,256]{1,0:T(8,128)S(1)} %copy-done), channel_id=1, source_target_pairs={{0,4},{4,0},{1,5},{5,1},{2,6},{6,2},{3,7},{7,3},{8,12},{12,8},{9,1... | collective-permute-start | bytes 811016 | tf_op jit(solution)/shard_map/ppermute | solution.py:235
  17.3 28.4 %collective-permute-start.4 = (f32[264,256]{1,0:T(8,128)S(1)}, f32[264,256]{1,0:T(8,128)S(1)}, u32[]{:S(2)}, u32[]{:S(2)}) collective-permute-start(f32[264,256]{1,0:T(8,128)S(1)} %collective-permute-done.refs_1_), channel_id=1, source_target_pairs={{0,4},{4,0},{1,5},{5,1},{2,6},{6,2},{3,7},{7,3},{8,12},{12,8},{9,1... | collective-permute-start | bytes 811016 | tf_op jit(solution)/shard_map/ppermute | solution.py:235
  20.7 25.1 %collective-permute-start.5 = (f32[264,256]{1,0:T(8,128)S(1)}, f32[264,256]{1,0:T(8,128)S(1)}, u32[]{:S(2)}, u32[]{:S(2)}) collective-permute-start(f32[264,256]{1,0:T(8,128)S(1)} %collective-permute-done.1.refs_2_), channel_id=1, source_target_pairs={{0,4},{4,0},{1,5},{5,1},{2,6},{6,2},{3,7},{7,3},{8,12},{12,8},{9,1... | collective-permute-start | bytes 811016 | tf_op jit(solution)/shard_map/ppermute | solution.py:235
  31.4 14.4 %collective-permute-start.6 = (f32[264,256]{1,0:T(8,128)S(1)}, f32[264,256]{1,0:T(8,128)S(1)}, u32[]{:S(2)}, u32[]{:S(2)}) collective-permute-start(f32[264,256]{1,0:T(8,128)S(1)} %collective-permute-done.2.refs_3_), channel_id=1, source_target_pairs={{0,4},{4,0},{1,5},{5,1},{2,6},{6,2},{3,7},{7,3},{8,12},{12,8},{9,1... | collective-permute-start | bytes 811016 | tf_op jit(solution)/shard_map/ppermute | solution.py:235
  31.5 7.3 %collective-permute-start.12 = (bf16[6,66,1]{2,1,0:T(8,128)(2,1)S(1)}, bf16[6,66,1]{2,1,0:T(8,128)(2,1)S(1)}, u32[]{:S(2)}, u32[]{:S(2)}) collective-permute-start(bf16[6,66,1]{2,1,0:T(8,128)(2,1)S(1)} %get-tuple-element.25), channel_id=1, source_target_pairs={{0,1},{1,2},{2,3},{4,5},{5,6},{6,7},{8,9},{9,10},{10,11},{12,13},{... | collective-permute-start | bytes 2384 | tf_op jit(solution)/shard_map/ppermute | solution.py:24
  38.8 6.6 %collective-permute-start.13 = (bf16[6,66,1]{2,1,0:T(8,128)(2,1)S(1)}, bf16[6,66,1]{2,1,0:T(8,128)(2,1)S(1)}, u32[]{:S(2)}, u32[]{:S(2)}) collective-permute-start(bf16[6,66,1]{2,1,0:T(8,128)(2,1)S(1)} %get-tuple-element.26), channel_id=1, source_target_pairs={{1,0},{2,1},{3,2},{5,4},{6,5},{7,6},{9,8},{10,9},{11,10},{13,12},{... | collective-permute-start | bytes 2384 | tf_op jit(solution)/shard_map/ppermute | solution.py:25
  75.4 8.3 %collective-permute-start.7 = (f32[2,64,256]{2,1,0:T(8,128)S(1)}, f32[2,64,256]{2,1,0:T(8,128)S(1)}, u32[]{:S(2)}, u32[]{:S(2)}) collective-permute-start(f32[2,64,256]{2,1,0:T(8,128)S(1)} %get-tuple-element.15), channel_id=1, source_target_pairs={{0,1},{1,2},{2,3},{4,5},{5,6},{6,7},{8,9},{9,10},{10,11},{12,13},{... | collective-permute-start | bytes 393224 | tf_op jit(solution)/shard_map/ppermute | solution.py:264
  77.8 10.4 %collective-permute-start.8 = (f32[2,64,256]{2,1,0:T(8,128)S(1)}, f32[2,64,256]{2,1,0:T(8,128)S(1)}, u32[]{:S(2)}, u32[]{:S(2)}) collective-permute-start(f32[2,64,256]{2,1,0:T(8,128)S(1)} %get-tuple-element.16), channel_id=1, source_target_pairs={{0,2},{1,3},{2,0},{4,6},{5,7},{6,4},{8,10},{9,11},{10,8},{12,14},{... | collective-permute-start | bytes 393224 | tf_op jit(solution)/shard_map/ppermute | solution.py:264
  79.1 9.1 %collective-permute-start.9 = (f32[2,64,256]{2,1,0:T(8,128)S(1)}, f32[2,64,256]{2,1,0:T(8,128)S(1)}, u32[]{:S(2)}, u32[]{:S(2)}) collective-permute-start(f32[2,64,256]{2,1,0:T(8,128)S(1)} %get-tuple-element.17), channel_id=1, source_target_pairs={{0,3},{1,0},{2,1},{4,7},{5,4},{6,5},{8,11},{9,8},{10,9},{12,15},{1... | collective-permute-start | bytes 393224 | tf_op jit(solution)/shard_map/ppermute | solution.py:264
  89.2 5.3 %collective-permute-start.14 = (f32[64,256]{1,0:T(8,128)S(1)}, f32[64,256]{1,0:T(8,128)S(1)}, u32[]{:S(2)}, u32[]{:S(2)}) collective-permute-start(f32[64,256]{1,0:T(8,128)S(1)} %neg.3), channel_id=1, source_target_pairs={{0,8},{8,16},{16,24},{24,0},{1,9},{9,17},{17,25},{25,1},{2,10},{10... | collective-permute-start | bytes 196616 | tf_op jit(solution)/shard_map/ppermute | solution.py:332
  91.3 4.3 %collective-permute-start.15 = (f32[64,256]{1,0:T(8,128)S(1)}, f32[64,256]{1,0:T(8,128)S(1)}, u32[]{:S(2)}, u32[]{:S(2)}) collective-permute-start(f32[64,256]{1,0:T(8,128)S(1)} %neg.3), channel_id=1, source_target_pairs={{0,16},{8,24},{16,0},{24,8},{1,17},{9,25},{17,1},{25,9},{2,18},{10... | collective-permute-start | bytes 196616 | tf_op jit(solution)/shard_map/ppermute | solution.py:332
  92.8 4.3 %collective-permute-start.16 = (f32[64,256]{1,0:T(8,128)S(1)}, f32[64,256]{1,0:T(8,128)S(1)}, u32[]{:S(2)}, u32[]{:S(2)}) collective-permute-start(f32[64,256]{1,0:T(8,128)S(1)} %neg.3), channel_id=1, source_target_pairs={{0,24},{8,0},{16,8},{24,16},{1,25},{9,1},{17,9},{25,17},{2,26},{10... | collective-permute-start | bytes 196616 | tf_op jit(solution)/shard_map/ppermute | solution.py:332
  97.1 4.3 %collective-permute-start.17 = (f32[1,256]{1,0:T(1,128)S(1)}, f32[1,256]{1,0:T(1,128)S(1)}, u32[]{:S(2)}, u32[]{:S(2)}) collective-permute-start(f32[1,256]{1,0:T(1,128)S(1)} %get-tuple-element.34), channel_id=1, source_target_pairs={{4,0},{5,1},{6,2},{7,3},{12,8},{13,9},{14,10},{15,11},{20,16},{21,... | collective-permute-start | bytes 3080 | tf_op jit(solution)/shard_map/ppermute | solution.py:25
  98.4 3.8 %collective-permute-start.18 = (f32[1,256]{1,0:T(1,128)S(1)}, f32[1,256]{1,0:T(1,128)S(1)}, u32[]{:S(2)}, u32[]{:S(2)}) collective-permute-start(f32[1,256]{1,0:T(1,128)S(1)} %get-tuple-element.33), channel_id=1, source_target_pairs={{0,4},{1,5},{2,6},{3,7},{8,12},{9,13},{10,14},{11,15},{16,20},{17,... | collective-permute-start | bytes 3080 | tf_op jit(solution)/shard_map/ppermute | solution.py:24
  102.3 5.9 %collective-permute-start.19 = (f32[66,1]{1,0:T(8,128)S(1)}, f32[66,1]{1,0:T(8,128)S(1)}, u32[]{:S(2)}, u32[]{:S(2)}) collective-permute-start(f32[66,1]{1,0:T(8,128)S(1)} %get-tuple-element.30), channel_id=1, source_target_pairs={{1,0},{2,1},{3,2},{5,4},{6,5},{7,6},{9,8},{10,9},{11,10},{13,12},{... | collective-permute-start | bytes 800 | tf_op jit(solution)/shard_map/ppermute | solution.py:25
  104.8 5.9 %collective-permute-start.20 = (f32[66,1]{1,0:T(8,128)S(1)}, f32[66,1]{1,0:T(8,128)S(1)}, u32[]{:S(2)}, u32[]{:S(2)}) collective-permute-start(f32[66,1]{1,0:T(8,128)S(1)} %get-tuple-element.29), channel_id=1, source_target_pairs={{0,1},{1,2},{2,3},{4,5},{5,6},{6,7},{8,9},{9,10},{10,11},{12,13},{... | collective-permute-start | bytes 800 | tf_op jit(solution)/shard_map/ppermute | solution.py:24

commit v3 on v0

--- a/solution.py
+++ b/solution.py
@@ -1,9 +1,17 @@
+import functools
+
 import jax
 import jax.numpy as jnp
 from jax import lax
+from jax.experimental import pallas as pl
+from jax.experimental.pallas import tpu as pltpu
 from jax.sharding import PartitionSpec as P
 
 ITERS = 20
+PARTS = 3
+LANES = 128
+F32 = jnp.float32
+BF16 = jnp.bfloat16
 
 
 def extended(x, sides, width):
@@ -19,14 +27,541 @@
     return x
 
 
-def on_device(
+def placed(cell, rows, cy):
+    x, y = cell // cy, cell % cy
+    tiles = rows // 8
+    return (x % tiles) * 8 + x // tiles, (y % 2) * LANES + y // 2
+
+
+def lane_order(cy, inverse):
+    a = lax.broadcasted_iota(jnp.int32, (cy, cy), 0)
+    b = lax.broadcasted_iota(jnp.int32, (cy, cy), 1)
+    natural, kept = (b, a) if inverse else (a, b)
+    return ((natural % 2) * LANES + natural // 2 == kept).astype(F32)
+
+
+STIFF_SCALE, STIFF_POWER = 1.92, 96.0
+MASS_SCALE, MASS_POWER = 1.0, 16.0
+POWER, FLOOR, SHIFT = 30.0, 1.0 / 256.0, 4.0
+
+
+def coded(v, most):
+    size = jnp.exp2(POWER * (jnp.log2(jnp.abs(v) / most + FLOOR) + SHIFT))
+    return jnp.where(v < 0.0, -size, size).astype(BF16)
+
+
+def decoded(v, most):
+    v = v.astype(F32)
+    size = (jnp.exp2(jnp.log2(jnp.abs(v)) * (1.0 / POWER) - SHIFT) - FLOOR) * most
+    return jnp.where(v < 0.0, -size, size)
+
+
+def largest(*arrays):
+    tops = [jnp.max(jnp.abs(v), axis=(0, 1), keepdims=True) for v in arrays]
+    return jnp.maximum(functools.reduce(jnp.maximum, tops), 1e-30)
+
+
+def raised(v, scale, power):
+    return jnp.exp2(power * jnp.log2(v * (1.0 / scale))).astype(BF16)
+
+
+def lowered(v, scale, power):
+    return scale * jnp.exp2(jnp.log2(v.astype(F32)) * (1.0 / power))
+
+
+def pieces(v):
+    out = []
+    for _ in range(3):
+        out.append(v.astype(BF16).astype(F32))
+        v = v - out[-1]
+    return out
+
+
+def permuted(v, order):
+    return jnp.dot(v, order, precision=lax.Precision.HIGHEST, preferred_element_type=F32)
+
+
+def pack_kernel(n_j, rhs, density, stiffness, mass, send, recv, weight, *outs):
+    *outs, pages = outs
+    rows, cy = density.shape
+    tiles = rows // 8
+    info = []
+    for ref in (send, recv):
+        row, column = placed(ref[...], rows, cy)
+        info += [row.astype(F32), column.astype(F32)]
+    info += pieces(weight[...])
+    order = lane_order(cy, False)
+    slot = 0
+
+    def packed(value):
+        nonlocal slot
+        value = permuted(value, order)
+        halves = []
+        for u in range(cy // LANES):
+            page = pages.at[slot % pages.shape[0]]
+            slot += 1
+            page[...] = value[:, u * LANES : (u + 1) * LANES]
+            halves.append(jnp.concatenate([page[pl.ds(t, 8, stride=tiles), :] for t in range(tiles)], axis=0))
+        return jnp.concatenate(halves, axis=1)
+
+    rho = density[...]
+    stiff = raised(packed(rho * rho * rho * stiffness[...]), STIFF_SCALE, STIFF_POWER)
+    rmass = raised(packed(rho * mass[...]), MASS_SCALE, MASS_POWER)
+    for s, out in enumerate(outs):
+        c = jnp.minimum(lax.rem(lax.axis_index("my") + s, n_j), PARTS - 1)
+        re, im = rhs[c], rhs[PARTS + c]
+        most = largest(re, im)
+        out[:rows, :] = coded(packed(re), most)
+        out[rows : 2 * rows, :] = coded(packed(im), most)
+        out[2 * rows : 3 * rows, :] = stiff
+        out[3 * rows : 4 * rows, :] = rmass
+        scale = [jnp.broadcast_to(x, (1, cy)) for x in pieces(most)]
+        out[4 * rows :, :] = jnp.concatenate(info + scale + [jnp.zeros((6, cy), F32)], axis=0).astype(BF16)
+
+
+def split(v):
+    high = v.astype(BF16)
+    return high, (v - high.astype(F32)).astype(BF16)
+
+
+def sweep_kernel(n_i, n_j, cap, omega, *refs):
+    blocks = n_i * n_j
+    msgs, refs = refs[: blocks], refs[blocks:]
+    outs, refs = refs[:n_j], refs[n_j:]
+    field_a, field_b, start, inverse, gain, lag, info, weights, pick, rowmask, spread, place, group, values, pages, plain, ends, rim, frame = refs
+    rows, cy = start.shape[2:]
+    slots = blocks * cap
+    me_i, me_j = lax.axis_index("mx"), lax.axis_index("my")
+    w = omega[0]
+
+    order = [(a, s) for a in range(n_i) for s in range(n_j)]
+    index = [lax.rem(me_i + a, n_i) * n_j + lax.rem(me_j + n_j - s, n_j) for a, s in order]
+    for msg, b in zip(msgs, index):
+        info[b] = msg[4 * rows :, :].astype(F32)
+    chunk = lax.broadcasted_iota(jnp.int32, (blocks, slots), 1) // cap
+    source = lax.broadcasted_iota(jnp.int32, (blocks, slots), 0)
+
+    def one_hot(line, depth):
+        at = lax.broadcasted_iota(jnp.int32, (depth, slots), 0)
+        return (jnp.broadcast_to(line.astype(jnp.int32), at.shape) == at).astype(F32)
+
+    for b in range(blocks):
+        line = info[b]
+        line = pltpu.roll(line, b * cap, 1) if b else line
+        pick[b] = one_hot(line[1:2], cy).astype(BF16)
+        rowmask[b] = one_hot(line[0:1], rows)
+        row_out = one_hot(line[2:3], rows)
+        spread[b] = row_out.astype(BF16)
+        lane_out = jnp.transpose(one_hot(line[3:4], cy)).astype(BF16)
+        place[b] = lane_out
+        group[b] = (chunk == (source + b) % blocks).astype(F32)
+        high, low = split(row_out * (line[4:5] + line[5:6] + line[6:7]))
+        both = jnp.dot(jnp.concatenate([high, low], axis=0), lane_out, preferred_element_type=F32)
+        gain[b] = both[:rows] + both[rows:]
+
+    for msg, b in zip(msgs, index):
+        rhs_re, rhs_im, k, m = [msg[n * rows : (n + 1) * rows, :] for n in range(4)]
+        most = info[b][7:8] + info[b][8:9] + info[b][9:10]
+        rhs_re, rhs_im = decoded(rhs_re, most), decoded(rhs_im, most)
+        k, m = lowered(k, STIFF_SCALE, STIFF_POWER), lowered(m, MASS_SCALE, MASS_POWER)
+        real_d = 4.4 * k + 0.3 + gain[b] - w * w * m
+        imag_d = 0.2 * w * (k + m)
+        scale = 1.0 / (real_d * real_d + imag_d * imag_d)
+        g, l = real_d * scale, imag_d * scale
+        first_re, first_im = rhs_re * g + rhs_im * l, rhs_im * g - rhs_re * l
+        gain[b], lag[b], inverse[b] = k * g, k * l, 1.0 / k
+        start[b, 0], start[b, 1] = first_re, first_im
+        field_a[b, 0], field_a[b, 1] = first_re, first_im
+
+    for b in range(blocks):
+        line = info[b]
+        line = pltpu.roll(line, b * cap, 1) if b else line
+        lane_out = one_hot(line[3:4], cy).astype(BF16)
+        found = jnp.dot(jnp.concatenate(split(inverse[b]), axis=0), lane_out, preferred_element_type=F32)
+        found = (found[:rows] + found[rows:]) * one_hot(line[2:3], rows)
+        found = jnp.sum(found, axis=0, keepdims=True)
+        weights[pl.ds(b, 1), :] = (line[4:5] + line[5:6] + line[6:7]) * found
+
+    row8 = lax.broadcasted_iota(jnp.int32, (8, LANES), 0)
+    lane_r = lax.broadcasted_iota(jnp.int32, (rows, LANES), 1)
+    zero = jnp.zeros((rows, LANES), F32)
+
+    def gather(now, b):
+        high, low = split(jnp.concatenate([now[b, 0], now[b, 1]], axis=0))
+        got = jnp.dot(jnp.concatenate([high, low], axis=0), pick[b], preferred_element_type=F32)
+        for part in range(2):
+            mine = got[part * rows : (part + 1) * rows] + got[(part + 2) * rows : (part + 3) * rows]
+            values[part, pl.ds(b, 1), :] = jnp.sum(mine * rowmask[b], axis=0, keepdims=True)
+
+    def beside(now, then, b):
+        i, j = b // n_j, b % n_j
+        for u in range(2):
+            lanes = slice(u * LANES, (u + 1) * LANES)
+            others = slice((1 - u) * LANES, (2 - u) * LANES)
+            for part in range(2):
+                own, other = now[b, part, :, lanes], now[b, part, :, others]
+                if u == 0:
+                    edge = now[b - 1, part, :, others] if j > 0 else zero
+                    around = pltpu.roll(jnp.where(lane_r == LANES - 1, edge, other), 1, 1)
+                else:
+                    edge = now[b + 1, part, :, others] if j < n_j - 1 else zero
+                    around = pltpu.roll(jnp.where(lane_r == 0, edge, other), LANES - 1, 1)
+                around += other
+                above = now[b - n_j, part, rows - 8 :, lanes] if i > 0 else zero[:8]
+                below = now[b + n_j, part, :8, lanes] if i < n_i - 1 else zero[:8]
+                top = pltpu.roll(jnp.where(row8 == 7, above, own[rows - 8 :]), 1, 0)
+                bottom = pltpu.roll(jnp.where(row8 == 0, below, own[:8]), 7, 0)
+                around += jnp.concatenate([top, own[:-8]], axis=0)
+                around += jnp.concatenate([own[8:], bottom], axis=0)
+                then[b, part, :, lanes] = around
+
+    def scatter(then, b):
+        left = []
+        for part in range(2):
+            arrived = jnp.sum(values[part] * group[b], axis=0, keepdims=True)
+            left += [spread[b] * x for x in split(arrived * weights[b : b + 1, :])]
+        mortar = jnp.dot(jnp.concatenate(left, axis=0), place[b], preferred_element_type=F32)
+        sums = [
+            then[b, part] + mortar[2 * part * rows : (2 * part + 1) * rows]
+            + mortar[(2 * part + 1) * rows : (2 * part + 2) * rows]
+            for part in range(2)
+        ]
+        g, l = gain[b], lag[b]
+        then[b, 0] = start[b, 0] + sums[0] * g + sums[1] * l
+        then[b, 1] = start[b, 1] + sums[1] * g - sums[0] * l
+
+    def sweep(now, then):
+        for b in range(blocks):
+            if b < blocks:
+                gather(now, b)
+            if b >= 0:
+                beside(now, then, b - 0)
+        for b in range(blocks):
+            scatter(then, b)
+
+    def pair(step, carry):
+        sweep(field_a, field_b)
+        sweep(field_b, field_a)
+        return carry
+
+    lax.fori_loop(0, (ITERS - 1) // 2, pair, 0)
+    last = field_a
+    if (ITERS - 1) % 2:
+        sweep(field_a, field_b)
+        last = field_b
+    tiles = rows // 8
+    back = lane_order(cy, True)
+    around_mesh = jnp.zeros((rows, LANES), F32)
+    for part in range(2):
+        for at in (0, LANES + n_j * cy):
+            plain[part, :, at : at + LANES] = around_mesh
+            ends[part, :, at : at + LANES] = around_mesh[:8]
+    end = jnp.where(me_i == 0, 0, rows - 1)
+    rim[...] = jnp.zeros_like(rim)
+    for j in range(n_j):
+        for part in range(2):
+            halves = []
+            for u in range(2):
+                page = pages.at[(j * 4 + part * 2 + u) % 8]
+                lanes = slice(u * LANES, (u + 1) * LANES)
+                for t in range(tiles):
+                    page[pl.ds(t, 8, stride=tiles), :] = last[me_i * n_j + j, part, t * 8 : (t + 1) * 8, lanes]
+                halves.append(page[...])
+            plain[part, :, LANES + j * cy : LANES + (j + 1) * cy] = permuted(jnp.concatenate(halves, axis=1), back)
+            rim[pl.ds(part * 4 + j, 1), :] = last[(1 - me_i) * n_j + j, part, pl.ds(end, 1), :]
+    natural = permuted(rim[...], back)
+    ends[:, :, LANES : LANES + n_j * cy] = jnp.zeros((2, 8, n_j * cy), F32)
+    for j in range(n_j):
+        for part in range(2):
+            for at in (0, 7):
+                ends[part, at : at + 1, LANES + j * cy : LANES + (j + 1) * cy] = natural[
+                    part * 4 + j : part * 4 + j + 1
+                ]
+    for s, out in enumerate(outs):
+        base = pl.multiple_of(LANES + lax.rem(me_j + s, n_j) * cy, LANES)
+        frame[...] = jnp.zeros_like(frame)
+        block = [plain[part, :, pl.ds(base, cy)] for part in range(2)]
+        for part in range(2):
+            frame[pl.ds(part * 8, 1), :] = ends[part, 0:1, pl.ds(base, cy)]
+            for k, (at, lane) in enumerate(((base - LANES, LANES - 1), (base + cy, 0)), 1):
+                at = pl.multiple_of(at, LANES)
+                beyond = [plain[part, :, pl.ds(at, LANES)], ends[part, :, pl.ds(at, LANES)]]
+                beyond = beyond + [jnp.zeros((LANES - rows - 16, LANES), F32), beyond[1]]
+                beyond = jnp.concatenate(beyond, axis=0)
+                frame[pl.ds(part * 8 + k, 1), :LANES] = jnp.transpose(beyond)[lane : lane + 1]
+        block.append(frame[...])
+        if s:
+            most = largest(*block)
+            block = [coded(v, most) for v in block]
+            row = lax.broadcasted_iota(jnp.int32, (16, cy), 0)
+            for k, piece in enumerate(pieces(most)):
+                block[2] = jnp.where(row == 3 + k, piece, block[2].astype(F32)).astype(BF16)
+        for v, at in zip(block, (0, rows, 2 * rows)):
+            out[at : at + v.shape[0], :] = v
+
+
+def planes_of(state, density, stiffness, mass):
+    return [state[n].astype(F32) for n in range(2 * PARTS)] + [density[...], stiffness[...], mass[...]]
+
+
+def edge_kernel(state, density, stiffness, mass, first, last, line):
+    rows, cy = density.shape
+    for out in (first, last, line):
+        out[...] = jnp.zeros_like(out)
+    top = lax.axis_index("mx") == 0
+    lane = lax.broadcasted_iota(jnp.int32, (1, LANES), 1)
+    for n, v in enumerate(planes_of(state, density, stiffness, mass)):
+        turned = jnp.transpose(jnp.concatenate([v[:, :LANES], v[:, cy - LANES :]], axis=0))
+        late = pltpu.roll(turned[LANES - 8 :], rows, 1)
+        for k in range(2):
+            at = pl.ds(16 * k + n, 1)
+            first[at, :] = jnp.where(lane < rows, turned[k : k + 1], 0.0)
+            last[at, :] = jnp.where(lane < rows, late[7 - k : 8 - k], 0.0)
+            line[at, :] = jnp.where(top, v[rows - 1 - k : rows - k], v[k : k + 1])
+
+
+def response_kernel(
+    omega, state, density, stiffness, mass, first, last, west, east, beyond, inner, ring, rho_ring
+):
+    rows, cy = density.shape
+    w = omega[0]
+    top = lax.axis_index("mx") == 0
+    zero = jnp.zeros((1, cy), F32)
+
+    def terms(u_re, u_im, nb_re, nb_im, rho, k, m):
+        dstiff = 3.0 * rho * rho * k
+        da = 4.4 * dstiff - w * w * m
+        db = 0.2 * w * (dstiff + m)
+        return da * u_re - db * u_im - dstiff * nb_re, da * u_im + db * u_re - dstiff * nb_im
+
+    line = beyond[:, :cy]
+    siblings = (beyond[:, cy : cy + LANES], beyond[:, cy + LANES :])
+    side = [x[...] + pltpu.roll(y, rows, 1) for x, y in zip((west, east), siblings)]
+    lane = lax.broadcasted_iota(jnp.int32, (16, LANES), 1)
+    start = jnp.where(top, 0, rows)
+    stop = jnp.where(top, LANES - 1, rows - 1)
+    corner = (lane == rows) | (lane == LANES - 1)
+    around = []
+    lane_cy = lax.broadcasted_iota(jnp.int32, (16, cy), 1)
+    near = line[:16]
+    touch = [jnp.where(top, y[:16, 0:1], y[:16, rows - 1 : rows]) for y in siblings]
+    before = jnp.where(lane_cy == 0, touch[0], pltpu.roll(near, 1, 1))
+    after = jnp.where(lane_cy == cy - 1, touch[1], pltpu.roll(near, cy - 1, 1))
+    adjacent = []
+    planes = planes_of(state, density, stiffness, mass)
+    for v in planes:
+        adjacent.append(jnp.where(top, v[rows - 1 :], v[:1]))
+    adjacent = jnp.concatenate(adjacent + [zero] * 7, axis=0)
+    around.append(line[16:] + adjacent + before + after)
+    for x, own, at in ((side[0], first, 0), (side[1], last, cy - 1)):
+        own = jnp.where(corner, near[:, at : at + 1], own[:16, :])
+        before = jnp.where(lane == start, 0.0, pltpu.roll(x[:16], 1, 1))
+        after = jnp.where(lane == stop, 0.0, pltpu.roll(x[:16], LANES - 1, 1))
+        around.append(x[16:] + own + before + after)
+    for row, (u, nb) in enumerate(zip([near] + [x[:16] for x in side], around)):
+        t = terms(u[:3], u[3:6], nb[:3], nb[3:6], u[6:7], u[7:8], u[8:9])
+        for part in range(2):
+            for c in range(PARTS):
+                ring[part * PARTS + c, row : row + 1, : u.shape[1]] = t[part][c : c + 1]
+        rho_ring[row : row + 1, : u.shape[1]] = u[6:7]
+    for n in range(2 * PARTS):
+        ring[n, 1:, LANES:] = jnp.zeros((7, cy - LANES), F32)
+        ring[n, 3:, :LANES] = jnp.zeros((5, LANES), F32)
+    rho_ring[1:, LANES:] = jnp.zeros((7, cy - LANES), F32)
+    rho_ring[3:, :LANES] = jnp.zeros((5, LANES), F32)
+
+    fill = jnp.zeros((LANES - 16, LANES), F32)
+    columns = [jnp.transpose(jnp.concatenate([x[:16], fill], axis=0)) for x in side]
+    lane = lax.broadcasted_iota(jnp.int32, (rows, cy), 1)
+    row = lax.broadcasted_iota(jnp.int32, (rows, cy), 0)
+
+    def neighbours(n):
+        v = planes[n]
+        total = jnp.where(lane == 0, columns[0][:rows, n : n + 1], pltpu.roll(v, 1, 1))
+        total += jnp.where(lane == cy - 1, columns[1][:rows, n : n + 1], pltpu.roll(v, cy - 1, 1))
+        edge = line[n : n + 1]
+        total += jnp.where(row == 0, jnp.where(top, zero, edge), pltpu.roll(v, 1, 0))
+        return total + jnp.where(row == rows - 1, jnp.where(top, edge, zero), pltpu.roll(v, rows - 1, 0))
+
+    for c in range(PARTS):
+        t = terms(planes[c], planes[PARTS + c], neighbours(c), neighbours(PARTS + c), *planes[6:])
+        inner[c], inner[PARTS + c] = t
+
+
+def sens_kernel(n_j, inner, ring, *refs):
+    msgs, (field, sens) = refs[:n_j], refs[n_j:]
+    rows = inner.shape[1]
+    sens[...] = jnp.zeros_like(sens)
+    for s, msg in enumerate(msgs):
+        c = lax.rem(lax.axis_index("my") + n_j - s, n_j)
+
+        @pl.when(c < PARTS)
+        def _(msg=msg, c=c):
+            planes = msg[...]
+            if msg.dtype == BF16:
+                scale = planes[2 * rows :].astype(F32)
+                planes = decoded(planes, scale[3:4] + scale[4:5] + scale[5:6])
+            re, im = planes[:rows], planes[rows : 2 * rows]
+            field[c] = re
+            field[PARTS + c] = im
+            sens[:rows, :] -= re * inner[c] - im * inner[PARTS + c]
+            re, im = planes[2 * rows : 2 * rows + 8], planes[2 * rows + 8 :]
+            sens[rows:, :] -= re * ring[c] - im * ring[PARTS + c]
+
+
+def filter_kernel(density, ring, *refs):
+    parts, out = refs[:-1], refs[-1]
+    rows, cy = density.shape
+    total = parts[0][...]
+    for part in parts[1:]:
+        total = total + part[...]
+    top = lax.axis_index("mx") == 0
+    rho = density[...]
+    inner, ring = rho * total[:rows], ring[...] * total[rows:]
+    columns = jnp.transpose(jnp.concatenate([ring, jnp.zeros((LANES - 8, cy), F32)], axis=0)[:, :LANES])
+
+    def across(v, before, after):
+        lane = lax.broadcasted_iota(jnp.int32, v.shape, 1)
+        before = jnp.where(lane == 0, before, pltpu.roll(v, 1, 1))
+        after = jnp.where(lane == cy - 1, after, pltpu.roll(v, cy - 1, 1))
+        return v + 0.5 * (before + after)
+
+    mid = across(inner, columns[:rows, 1:2], columns[:rows, 2:3])
+    corner = jnp.where(top, columns[rows : rows + 1], columns[LANES - 1 :])
+    end = across(ring, corner[:, 1:2], corner[:, 2:3])[0:1]
+    row = lax.broadcasted_iota(jnp.int32, mid.shape, 0)
+    empty = jnp.zeros_like(end)
+    above = jnp.where(row == 0, jnp.where(top, empty, end), pltpu.roll(mid, 1, 0))
+    below = jnp.where(row == rows - 1, jnp.where(top, end, empty), pltpu.roll(mid, rows - 1, 0))
+    out[...] = (mid + 0.5 * (above + below)) / (4.0 * rho)
+
+
+def vmem():
+    return pl.BlockSpec(memory_space=pltpu.VMEM)
+
+
+def smem():
+    return pl.BlockSpec(memory_space=pltpu.SMEM)
+
+
+def shifts(n_j, source_limit, target_limit):
+    return [
+        [(a, (a + s) % n_j) for a in range(n_j) if a < source_limit and (a + s) % n_j < target_limit]
+        for s in range(1, n_j)
+    ]
+
+
+def gathered(
     adjoint_rhs, state, density, stiffness, mass, omega, send_rows, recv_rows, mortar_weight
 ):
+    rhs = adjoint_rhs.reshape(2 * PARTS, *density.shape)
+    rows, cy = density.shape
+    n_i, n_j = lax.axis_size("mx"), lax.axis_size("my")
+    blocks = n_i * n_j
+    slots = send_rows.shape[1]
+    cap = slots // blocks
+    up = [(a, a + 1) for a in range(n_j - 1)]
+    edge = jax.ShapeDtypeStruct((32, LANES), F32)
+    planes = (state.reshape(2 * PARTS, rows, cy), density, stiffness, mass)
+    first, last, line = pl.pallas_call(
+        edge_kernel,
+        out_shape=[edge, edge, jax.ShapeDtypeStruct((32, cy), F32)],
+        in_specs=[vmem()] * 4,
+        out_specs=[vmem()] * 3,
+        name="edges",
+    )(*planes)
+    west = lax.ppermute(last, "my", up)
+    east = lax.ppermute(first, "my", [(b, a) for a, b in up])
+    message = jax.ShapeDtypeStruct((4 * rows + 16, cy), BF16)
+    own = pl.pallas_call(
+        functools.partial(pack_kernel, n_j),
+        out_shape=[message] * n_j,
+        in_specs=[vmem()] * 7,
+        out_specs=[vmem()] * n_j,
+        scratch_shapes=[pltpu.VMEM((8, rows, LANES), F32)],
+        name="pack",
+    )(rhs, density, stiffness, mass, send_rows, recv_rows, mortar_weight)
+    msgs = [own[0]]
+    for s, pairs in enumerate(shifts(n_j, n_j, PARTS), 1):
+        msgs.append(lax.ppermute(own[s], "my", pairs))
+    msgs[1], first, last = lax.optimization_barrier((msgs[1], first, last))
+    msgs[-1], west, east = lax.optimization_barrier((msgs[-1], west, east))
+    msgs += [lax.ppermute(m, "mx", [(0, 1), (1, 0)]) for m in msgs]
+    block = (blocks, rows, cy)
+    outs = pl.pallas_call(
+        functools.partial(sweep_kernel, n_i, n_j, cap),
+        out_shape=[jax.ShapeDtypeStruct((2 * rows + 16, cy), BF16 if s else F32) for s in range(n_j)],
+        in_specs=[smem()] + [vmem()] * blocks,
+        out_specs=[vmem()] * n_j,
+        scratch_shapes=[
+            pltpu.VMEM((blocks, 2, rows, cy), F32),
+            pltpu.VMEM((blocks, 2, rows, cy), F32),
+            pltpu.VMEM((blocks, 2, rows, cy), F32),
+            pltpu.VMEM(block, F32),
+            pltpu.VMEM(block, F32),
+            pltpu.VMEM(block, F32),
+            pltpu.VMEM((blocks, 16, cy), F32),
+            pltpu.VMEM((blocks, slots), F32),
+            pltpu.VMEM((blocks, cy, slots), BF16),
+            pltpu.VMEM((blocks, rows, slots), F32),
+            pltpu.VMEM((blocks, rows, slots), BF16),
+            pltpu.VMEM((blocks, slots, cy), BF16),
+            pltpu.VMEM((blocks, blocks, slots), F32),
+            pltpu.VMEM((2, blocks, slots), F32),
+            pltpu.VMEM((8, rows, LANES), F32),
+            pltpu.VMEM((2, rows, n_j * cy + 2 * LANES), F32),
+            pltpu.VMEM((2, 8, n_j * cy + 2 * LANES), F32),
+            pltpu.VMEM((8, cy), F32),
+            pltpu.VMEM((16, cy), F32),
+        ],
+        compiler_params=pltpu.CompilerParams(vmem_limit_bytes=40 * 1024 * 1024),
+        cost_estimate=pl.CostEstimate(flops=30_000_000_000, bytes_accessed=4_000_000, transcendentals=0),
+        name="sweeps",
+    )(omega, *msgs)
+    parts = [outs[0]]
+    for s, pairs in enumerate(shifts(n_j, PARTS, n_j), 1):
+        parts.append(lax.ppermute(outs[s], "my", pairs))
+    beyond = lax.ppermute(jnp.concatenate([line, west, east], axis=1), "mx", [(0, 1), (1, 0)])
+    inner, ring, rho_ring = pl.pallas_call(
+        response_kernel,
+        out_shape=[
+            jax.ShapeDtypeStruct((2 * PARTS, rows, cy), F32),
+            jax.ShapeDtypeStruct((2 * PARTS, 8, cy), F32),
+            jax.ShapeDtypeStruct((8, cy), F32),
+        ],
+        in_specs=[smem()] + [vmem()] * 9,
+        out_specs=[vmem()] * 3,
+        name="response",
+    )(omega, *planes, first, last, west, east, beyond)
+    field, sens = pl.pallas_call(
+        functools.partial(sens_kernel, n_j),
+        out_shape=[
+            jax.ShapeDtypeStruct((2 * PARTS, rows, cy), F32),
+            jax.ShapeDtypeStruct((rows + 8, cy), F32),
+        ],
+        in_specs=[vmem()] * (2 + n_j),
+        out_specs=[vmem()] * 2,
+        name="sensitivity",
+    )(inner, ring, *parts)
+    size = lax.axis_size("freq")
+    all_freqs = [sens]
+    for s in range(1, size):
+        all_freqs.append(lax.ppermute(sens, "freq", [(a, (a + s) % size) for a in range(size)]))
+    filtered = pl.pallas_call(
+        filter_kernel,
+        out_shape=jax.ShapeDtypeStruct((rows, cy), F32),
+        in_specs=[vmem()] * (2 + size),
+        out_specs=vmem(),
+        name="filter",
+    )(density, rho_ring, *all_freqs)
+    return field.reshape(adjoint_rhs.shape), filtered
+
+
+def solve_split(rhs, density, stiffness, mass, omega, send_rows, recv_rows, mortar_weight):
     rows_x, rows_y = density.shape
     cells = rows_x * rows_y
     w = omega[0]
     stiff = density**3 * stiffness
-    dstiff = 3.0 * density**2 * stiffness
     rmass = density * mass
     sources = send_rows[0]
     targets = recv_rows[0]
@@ -35,7 +570,6 @@
     real_d = 4.4 * stiff + 0.3 + mdiag - w * w * rmass
     imag_d = 0.2 * w * (stiff + rmass)
     den = real_d * real_d + imag_d * imag_d
-    rhs = adjoint_rhs.reshape(6, rows_x, rows_y)
 
     def mortar(field):
         sent = field.reshape(6, cells)[:, sources]
@@ -53,7 +587,17 @@
         new_im = (h[3:] * real_d - h[:3] * imag_d) / den
         return jnp.concatenate([new_re, new_im], axis=0)
 
-    field = lax.fori_loop(0, ITERS, sweep, jnp.zeros((6, rows_x, rows_y), jnp.float32))
+    return lax.fori_loop(0, ITERS, sweep, jnp.zeros((6, rows_x, rows_y), jnp.float32))
+
+
+def distributed(
+    adjoint_rhs, state, density, stiffness, mass, omega, send_rows, recv_rows, mortar_weight
+):
+    rows_x, rows_y = density.shape
+    w = omega[0]
+    dstiff = 3.0 * density**2 * stiffness
+    rhs = adjoint_rhs.reshape(6, rows_x, rows_y)
+    field = solve_split(rhs, density, stiffness, mass, omega, send_rows, recv_rows, mortar_weight)
     state_six = state.reshape(6, rows_x, rows_y)
     state_pad = extended(state_six, (("mx", 1), ("my", 2)), 1).astype(jnp.float32)
     u = state_six.astype(jnp.float32)
@@ -68,7 +612,10 @@
     t_re = da * u[:3] - db * u[3:] - dstiff * nb[:3]
     t_im = da * u[3:] + db * u[:3] - dstiff * nb[3:]
     sens = -jnp.sum(field[:3] * t_re - field[3:] * t_im, axis=0)
-    total = lax.psum(sens, "freq")
+    size = lax.axis_size("freq")
+    total = sens
+    for s in range(1, size):
+        total = total + lax.ppermute(sens, "freq", [(a, (a + s) % size) for a in range(size)])
     weighted = extended(density * total, (("mx", 0), ("my", 1)), 1)
     filt = weighted[1:-1, 1:-1]
     filt = filt + 0.5 * (
@@ -78,6 +625,13 @@
         weighted[2:, 2:] + weighted[:-2, :-2] + weighted[2:, :-2] + weighted[:-2, 2:]
     )
     return (field.reshape(1, 2, 3, rows_x, rows_y), filt / (4.0 * density))
+
+
+def on_device(*args):
+    rows, cy = args[2].shape
+    n_i, n_j = lax.axis_size("mx"), lax.axis_size("my")
+    fits = n_i == 2 and PARTS <= n_j <= 4 and rows == 64 and cy == 2 * LANES and args[6].shape[1] == cy
+    return (gathered if fits else distributed)(*args)
 
 
 def solution(mesh):

time: 875 us -> 79.4 us (0.09)
  the two profiles are of different devices: /device:TPU:8 before, /device:TPU:0 now
where the time goes in v3:
time: 79.4 us; the launch traced here: 79 us
  Pallas kernels  36.6 us (46%)
  starting transfers between devices  30.1 us (38%)
  waiting for transfers between devices  8.24 us (10%)
  local copies, waits for them, and re-layouts  2.57 us (3%)
  between operations  1.49 us (2%)
    pallas_call x1, Pallas kernels, gathered(): pl.pallas_call(functools.partial(sweep_kernel, n_i, n_j, cap), out_shape=...  24.9 us
    ppermute x3, starting transfers between devices, gathered(): msgs.append(lax.ppermute(own[s], 'my', pairs))  11.8 us
    ppermute x3, starting transfers between devices, gathered(): parts.append(lax.ppermute(outs[s], 'my', pairs))  8.03 us
    ppermute x3, waiting for transfers between devices, gathered(): lax.ppermute(sens, 'freq', [(a, (a + s) % size) for a in range(size)])  4.86 us
    ppermute x1, starting transfers between devices, gathered(): west = lax.ppermute(last, 'my', up)  4.55 us
    ppermute x3, starting transfers between devices, gathered(): lax.ppermute(sens, 'freq', [(a, (a + s) % size) for a in range(size)])  3.55 us
    pallas_call x1, Pallas kernels, gathered(): pl.pallas_call(functools.partial(pack_kernel, n_j), out_shape=[message] *...  3.34 us
    unnamed x24, local copies, waits for them, and re-layouts  2.57 us
  transfers between devices with their start and end apart: 16, of which 9 were waited for; matrix products, arithmetic and copies ran while one was open for 0% of the time, Pallas kernels for 5%

profile of v3, /device:TPU:0, one launch (start us, length us, event | category | flops | bytes accessed | tf_op | source)
XLA Modules:
  0.0 79.0 jit_solution(10699950930866109608)
XLA Ops:
  0.6 3.3 %pack.1 = (bf16[272,256]{1,0:T(8,128)(2,1)}, bf16[272,256]{1,0:T(8,128)(2,1)}, bf16[272,256]{1,0:T(8,128)(2,1)}, bf16[272,256]{1,0:T(8,128)(2,1)}) custom-call(f32[6,64,256]{2,1,0:T(8,128)} %bitcast.5, f32[64,256]{1,0:T(8,128)} %density.7, f32[64,256]{1,0:T(8,128)} %stiffness.5, f32[64,256]{1,0:T(8,128)} %mass.5, s32[1,256]{1,0:T(1,128)} %send.1, ...), custom_call_target="tpu_custom_call" | custom-call | tf_op jit(solution)/shard_map/pack/pallas_call | solution.py:476
  4.0 4.9 %collective-permute-start = (bf16[272,256]{1,0:T(8,128)(2,1)}, bf16[272,256]{1,0:T(8,128)(2,1)S(1)}, u32[]{:S(2)}, u32[]{:S(2)}) collective-permute-start(bf16[272,256]{1,0:T(8,128)(2,1)} %get-tuple-element.24), channel_id=1, source_target_pairs={{0,1},{1,2},{3,0},{4,5},{5,6},{7,4},{8,9},{9,10},{11,8},{12,13},{1... | collective-permute-start | bytes 417800 | tf_op jit(solution)/shard_map/ppermute | solution.py:486
  8.9 1.3 %collective-permute-start.1 = (bf16[272,256]{1,0:T(8,128)(2,1)}, bf16[272,256]{1,0:T(8,128)(2,1)S(1)}, u32[]{:S(2)}, u32[]{:S(2)}) collective-permute-start(bf16[272,256]{1,0:T(8,128)(2,1)} %get-tuple-element.29), channel_id=1, source_target_pairs={{1,0},{2,1},{3,2},{5,4},{6,5},{7,6},{9,8},{10,9},{11,10},{13,12},{... | collective-permute-start | bytes 417800 | tf_op jit(solution)/shard_map/ppermute | solution.py:486
  10.2 5.6 %collective-permute-start.5 = (bf16[272,256]{1,0:T(8,128)(2,1)}, bf16[272,256]{1,0:T(8,128)(2,1)S(1)}, u32[]{:S(2)}, u32[]{:S(2)}) collective-permute-start(bf16[272,256]{1,0:T(8,128)(2,1)} %get-tuple-element.37), channel_id=1, source_target_pairs={{0,2},{2,0},{3,1},{4,6},{6,4},{7,5},{8,10},{10,8},{11,9},{12,14},{... | collective-permute-start | bytes 417800 | tf_op jit(solution)/shard_map/ppermute | solution.py:486
  15.8 0.0 copy-start.1
  15.8 1.9 %edges.1 = (f32[32,128]{1,0:T(8,128)}, f32[32,128]{1,0:T(8,128)}, f32[32,256]{1,0:T(8,128)}) custom-call(bf16[6,64,256]{2,1,0:T(8,128)(2,1)} %bitcast.3, f32[64,256]{1,0:T(8,128)} %density.7, f32[64,256]{1,0:T(8,128)} %stiffness.5, f32[64,256]{1,0:T(8,128)} %mass.5), custom_call_target="tpu_custom_call" | custom-call | tf_op jit(solution)/shard_map/edges/pallas_call | solution.py:466
  17.7 1.3 %collective-permute-start.3 = (f32[32,128]{1,0:T(8,128)}, f32[32,128]{1,0:T(8,128)S(1)}, u32[]{:S(2)}, u32[]{:S(2)}) collective-permute-start(f32[32,128]{1,0:T(8,128)} %get-tuple-element.27.first), channel_id=1, source_target_pairs={{1,0},{2,1},{3,2},{5,4},{6,5},{7,6},{9,8},{10,9},{11,10},{13,12},{... | collective-permute-start | bytes 49160 | tf_op jit(solution)/shard_map/ppermute | solution.py:474
  19.0 4.5 %collective-permute-start.2 = (f32[32,128]{1,0:T(8,128)}, f32[32,128]{1,0:T(8,128)S(1)}, u32[]{:S(2)}, u32[]{:S(2)}) collective-permute-start(f32[32,128]{1,0:T(8,128)} %get-tuple-element.28.last), channel_id=1, source_target_pairs={{0,1},{1,2},{2,3},{4,5},{5,6},{6,7},{8,9},{9,10},{10,11},{12,13},{... | collective-permute-start | bytes 49160 | tf_op jit(solution)/shard_map/ppermute | solution.py:473
  23.5 0.0 collective-permute-done.refs_1_
  23.5 0.0 copy-done.1
  23.5 0.1 collective-permute-start.6
  23.6 0.3 collective-permute-done.3.east
  23.9 0.0 copy-start.9
  23.9 0.2 collective-permute-start.7
  24.1 1.0 %collective-permute-done.2.west = f32[32,128]{1,0:T(8,128)S(1)} collective-permute-done((f32[32,128]{1,0:T(8,128)}, f32[32,128]{1,0:T(8,128)S(1)}, u32[]{:S(2)}, u32[]{:S(2)}) %collective-permute-start.2) | collective-permute-done | bytes 16416 | tf_op jit(solution)/shard_map/ppermute | solution.py:473
  25.2 0.0 copy-start.10
  25.2 0.0 collective-permute-done.1.refs_3_
  25.2 0.0 collective-permute-start.9
  25.2 0.0 collective-permute-done.5.refs_2_
  25.2 0.5 collective-permute-start.8
  26.3 0.0 copy-start.11
  26.3 0.0 collective-permute-done.6.refs_4_
  26.3 0.0 collective-permute-done.7.refs_5_
  26.4 0.2 collective-permute-done.9.refs_7_
  26.5 0.2 collective-permute-done.8.refs_6_
  26.7 24.9 %sweeps.1 = (f32[144,256]{1,0:T(8,128)S(1)}, bf16[144,256]{1,0:T(8,128)(2,1)S(1)}, bf16[144,256]{1,0:T(8,128)(2,1)S(1)}, bf16[144,256]{1,0:T(8,128)(2,1)S(1)}) custom-call(f32[1]{0:T(128)S(6)} %copy.11.omega, bf16[272,256]{1,0:T(8,128)(2,1)S(1)} %copy-done.1, bf16[272,256]{1,0:T(8,128)(2,1)S(1)} %collective-permute-done.refs_1_, ...), custom_call_target="tpu_custom_call" | custom-call | flops 30000001024 | bytes 4000000 | tf_op jit(solution)/shard_map/sweeps/pallas_call | solution.py:491
  51.6 0.0 copy-start
  51.7 0.6 copy-done
  52.3 4.2 %collective-permute-start.10 = (bf16[144,256]{1,0:T(8,128)(2,1)S(1)}, bf16[144,256]{1,0:T(8,128)(2,1)S(1)}, u32[]{:S(2)}, u32[]{:S(2)}) collective-permute-start(bf16[144,256]{1,0:T(8,128)(2,1)S(1)} %get-tuple-element.40), channel_id=1, source_target_pairs={{0,1},{1,2},{2,3},{4,5},{5,6},{6,7},{8,9},{9,10},{10,11},{12,13},{... | collective-permute-start | bytes 221192 | tf_op jit(solution)/shard_map/ppermute | solution.py:523
  56.5 1.9 %collective-permute-start.11 = (bf16[144,256]{1,0:T(8,128)(2,1)S(1)}, bf16[144,256]{1,0:T(8,128)(2,1)S(1)}, u32[]{:S(2)}, u32[]{:S(2)}) collective-permute-start(bf16[144,256]{1,0:T(8,128)(2,1)S(1)} %get-tuple-element.41), channel_id=1, source_target_pairs={{0,2},{1,3},{2,0},{4,6},{5,7},{6,4},{8,10},{9,11},{10,8},{12,14},{... | collective-permute-start | bytes 221192 | tf_op jit(solution)/shard_map/ppermute | solution.py:523
  58.4 1.9 %collective-permute-start.12 = (bf16[144,256]{1,0:T(8,128)(2,1)S(1)}, bf16[144,256]{1,0:T(8,128)(2,1)S(1)}, u32[]{:S(2)}, u32[]{:S(2)}) collective-permute-start(bf16[144,256]{1,0:T(8,128)(2,1)S(1)} %get-tuple-element.42), channel_id=1, source_target_pairs={{0,3},{1,0},{2,1},{4,7},{5,4},{6,5},{8,11},{9,8},{10,9},{12,15},{1... | collective-permute-start | bytes 221192 | tf_op jit(solution)/shard_map/ppermute | solution.py:523
  60.4 0.0 copy-done.9
  60.4 0.0 copy-done.10
  60.4 0.0 copy-done.11
  60.4 0.1 collective-permute-start.4
  60.5 1.2 %collective-permute-done.4.beyond = f32[32,512]{1,0:T(8,128)S(1)} collective-permute-done((f32[32,512]{1,0:T(8,128)S(1)}, f32[32,512]{1,0:T(8,128)S(1)}, u32[]{:S(2)}, u32[]{:S(2)}) %collective-permute-start.4) | collective-permute-done | bytes 65568 | tf_op jit(solution)/shard_map/ppermute | solution.py:524
  61.7 0.0 copy-start.8
  61.7 0.6 copy-done.8
  62.4 2.4 %response.1 = (f32[6,64,256]{2,1,0:T(8,128)}, f32[6,8,256]{2,1,0:T(8,128)}, f32[8,256]{1,0:T(8,128)}) custom-call(f32[1]{0:T(128)S(6)} %copy.11.omega, bf16[6,64,256]{2,1,0:T(8,128)(2,1)} %bitcast.4, f32[64,256]{1,0:T(8,128)} %density.7, f32[64,256]{1,0:T(8,128)} %stiffness.5, f32[64,256]{1,0:T(8,128)} %mass.5, f32[32,128]{1,0:T(8,128)} %get-tuple-element.27.first, ...), custom_call_target="tpu_custom_call" | custom-call | tf_op jit(solution)/shard_map/response/pallas_call | solution.py:525
  64.7 0.0 collective-permute-done.10.refs_1_
  64.7 0.0 copy-start.2
  64.7 0.0 collective-permute-done.11.refs_2_
  64.7 0.0 copy-start.3
  64.7 0.5 collective-permute-done.12.refs_3_
  65.2 0.0 copy-start.4
  65.2 0.1 copy-done.2
  65.3 0.0 copy-done.3
  65.4 0.5 copy-done.4
  65.9 2.1 %sensitivity.1 = (f32[6,64,256]{2,1,0:T(8,128)}, f32[72,256]{1,0:T(8,128)}) custom-call(f32[6,64,256]{2,1,0:T(8,128)} %get-tuple-element.33.inner, f32[6,8,256]{2,1,0:T(8,128)} %get-tuple-element.34.ring, f32[144,256]{1,0:T(8,128)} %copy-done, bf16[144,256]{1,0:T(8,128)(2,1)} %copy-done.2, bf16[144,256]{1,0:T(8,128)(2,1)} %copy-done.3, ...), custom_call_target="tpu_custom_call" | custom-call | tf_op jit(solution)/shard_map/sensitivity/pallas_call | solution.py:536
  68.0 2.4 %collective-permute-start.15 = (f32[72,256]{1,0:T(8,128)}, f32[72,256]{1,0:T(8,128)S(1)}, u32[]{:S(2)}, u32[]{:S(2)}) collective-permute-start(f32[72,256]{1,0:T(8,128)} %get-tuple-element.45.refs_0_), channel_id=1, source_target_pairs={{0,24},{8,0},{16,8},{24,16},{1,25},{9,1},{17,9},{25,17},{2,26},{10... | collective-permute-start | bytes 221192 | tf_op jit(solution)/shard_map/ppermute | solution.py:549
  70.4 0.5 collective-permute-start.14
  70.9 0.6 collective-permute-start.13
  71.5 1.4 %collective-permute-done.15.refs_3_ = f32[72,256]{1,0:T(8,128)S(1)} collective-permute-done((f32[72,256]{1,0:T(8,128)}, f32[72,256]{1,0:T(8,128)S(1)}, u32[]{:S(2)}, u32[]{:S(2)}) %collective-permute-start.15) | collective-permute-done | bytes 73760 | tf_op jit(solution)/shard_map/ppermute | solution.py:549
  73.0 0.0 copy-start.5
  73.0 2.4 %collective-permute-done.14.refs_2_ = f32[72,256]{1,0:T(8,128)S(1)} collective-permute-done((f32[72,256]{1,0:T(8,128)}, f32[72,256]{1,0:T(8,128)S(1)}, u32[]{:S(2)}, u32[]{:S(2)}) %collective-permute-start.14) | collective-permute-done | bytes 73760 | tf_op jit(solution)/shard_map/ppermute | solution.py:549
  75.4 0.0 copy-start.6
  75.4 1.0 %collective-permute-done.13.refs_1_ = f32[72,256]{1,0:T(8,128)S(1)} collective-permute-done((f32[72,256]{1,0:T(8,128)}, f32[72,256]{1,0:T(8,128)S(1)}, u32[]{:S(2)}, u32[]{:S(2)}) %collective-permute-start.13) | collective-permute-done | bytes 73760 | tf_op jit(solution)/shard_map/ppermute | solution.py:549
  76.4 0.0 copy-start.7
  76.4 0.0 copy-done.5
  76.4 0.0 copy-done.6
  76.4 0.6 copy-done.7
  77.0 1.9 %filter.1 = f32[64,256]{1,0:T(8,128)} custom-call(f32[64,256]{1,0:T(8,128)} %density.7, f32[8,256]{1,0:T(8,128)} %get-tuple-element.44.ring, f32[72,256]{1,0:T(8,128)} %get-tuple-element.45.refs_0_, f32[72,256]{1,0:T(8,128)} %copy-done.7, f32[72,256]{1,0:T(8,128)} %copy-done.6, f32[72,256]{1,0:T(8,128)} %copy-done.5), custom_call_target="tpu_custom_call" | custom-call | tf_op jit(solution)/shard_map/filter/pallas_call | solution.py:550
  (1 shorter events, 0.0 us)
Async XLA Ops:
  4.0 19.6 %collective-permute-start = (bf16[272,256]{1,0:T(8,128)(2,1)}, bf16[272,256]{1,0:T(8,128)(2,1)S(1)}, u32[]{:S(2)}, u32[]{:S(2)}) collective-permute-start(bf16[272,256]{1,0:T(8,128)(2,1)} %get-tuple-element.24), channel_id=1, source_target_pairs={{0,1},{1,2},{3,0},{4,5},{5,6},{7,4},{8,9},{9,10},{11,8},{12,13},{1... | collective-permute-start | bytes 417800 | tf_op jit(solution)/shard_map/ppermute | solution.py:486
  8.9 16.3 %collective-permute-start.1 = (bf16[272,256]{1,0:T(8,128)(2,1)}, bf16[272,256]{1,0:T(8,128)(2,1)S(1)}, u32[]{:S(2)}, u32[]{:S(2)}) collective-permute-start(bf16[272,256]{1,0:T(8,128)(2,1)} %get-tuple-element.29), channel_id=1, source_target_pairs={{1,0},{2,1},{3,2},{5,4},{6,5},{7,6},{9,8},{10,9},{11,10},{13,12},{... | collective-permute-start | bytes 417800 | tf_op jit(solution)/shard_map/ppermute | solution.py:486
  10.2 15.0 %collective-permute-start.5 = (bf16[272,256]{1,0:T(8,128)(2,1)}, bf16[272,256]{1,0:T(8,128)(2,1)S(1)}, u32[]{:S(2)}, u32[]{:S(2)}) collective-permute-start(bf16[272,256]{1,0:T(8,128)(2,1)} %get-tuple-element.37), channel_id=1, source_target_pairs={{0,2},{2,0},{3,1},{4,6},{6,4},{7,5},{8,10},{10,8},{11,9},{12,14},{... | collective-permute-start | bytes 417800 | tf_op jit(solution)/shard_map/ppermute | solution.py:486
  15.8 7.8 %copy-start.1 = (bf16[272,256]{1,0:T(8,128)(2,1)S(1)}, bf16[272,256]{1,0:T(8,128)(2,1)}, u32[]{:S(2)}) copy-start(bf16[272,256]{1,0:T(8,128)(2,1)} %get-tuple-element.35.refs_0_) | copy-start | bytes 417796
  17.7 6.2 %collective-permute-start.3 = (f32[32,128]{1,0:T(8,128)}, f32[32,128]{1,0:T(8,128)S(1)}, u32[]{:S(2)}, u32[]{:S(2)}) collective-permute-start(f32[32,128]{1,0:T(8,128)} %get-tuple-element.27.first), channel_id=1, source_target_pairs={{1,0},{2,1},{3,2},{5,4},{6,5},{7,6},{9,8},{10,9},{11,10},{13,12},{... | collective-permute-start | bytes 49160 | tf_op jit(solution)/shard_map/ppermute | solution.py:474
  19.0 6.2 %collective-permute-start.2 = (f32[32,128]{1,0:T(8,128)}, f32[32,128]{1,0:T(8,128)S(1)}, u32[]{:S(2)}, u32[]{:S(2)}) collective-permute-start(f32[32,128]{1,0:T(8,128)} %get-tuple-element.28.last), channel_id=1, source_target_pairs={{0,1},{1,2},{2,3},{4,5},{5,6},{6,7},{8,9},{9,10},{10,11},{12,13},{... | collective-permute-start | bytes 49160 | tf_op jit(solution)/shard_map/ppermute | solution.py:473
  23.5 2.8 %collective-permute-start.6 = (bf16[272,256]{1,0:T(8,128)(2,1)S(1)}, bf16[272,256]{1,0:T(8,128)(2,1)S(1)}, u32[]{:S(2)}, u32[]{:S(2)}) collective-permute-start(bf16[272,256]{1,0:T(8,128)(2,1)S(1)} %copy-done.1), channel_id=1, source_target_pairs={{0,4},{4,0},{1,5},{5,1},{2,6},{6,2},{3,7},{7,3},{8,12},{12,8},{9,1... | collective-permute-start | bytes 417800 | tf_op jit(solution)/shard_map/ppermute | solution.py:489
  23.9 36.5 %copy-start.9 = (f32[32,128]{1,0:T(8,128)}, f32[32,128]{1,0:T(8,128)S(1)}, u32[]{:S(2)}) copy-start(f32[32,128]{1,0:T(8,128)S(1)} %collective-permute-done.3.east) | copy-start | bytes 49156
  23.9 2.5 %collective-permute-start.7 = (bf16[272,256]{1,0:T(8,128)(2,1)S(1)}, bf16[272,256]{1,0:T(8,128)(2,1)S(1)}, u32[]{:S(2)}, u32[]{:S(2)}) collective-permute-start(bf16[272,256]{1,0:T(8,128)(2,1)S(1)} %collective-permute-done.refs_1_), channel_id=1, source_target_pairs={{0,4},{4,0},{1,5},{5,1},{2,6},{6,2},{3,7},{7,3},{8,12},{12,8},{9,1... | collective-permute-start | bytes 417800 | tf_op jit(solution)/shard_map/ppermute | solution.py:489
  25.2 35.2 %copy-start.10 = (f32[32,128]{1,0:T(8,128)}, f32[32,128]{1,0:T(8,128)S(1)}, u32[]{:S(2)}) copy-start(f32[32,128]{1,0:T(8,128)S(1)} %collective-permute-done.2.west) | copy-start | bytes 49156
  25.2 1.4 %collective-permute-start.9 = (bf16[272,256]{1,0:T(8,128)(2,1)S(1)}, bf16[272,256]{1,0:T(8,128)(2,1)S(1)}, u32[]{:S(2)}, u32[]{:S(2)}) collective-permute-start(bf16[272,256]{1,0:T(8,128)(2,1)S(1)} %collective-permute-done.1.refs_3_), channel_id=1, source_target_pairs={{0,4},{4,0},{1,5},{5,1},{2,6},{6,2},{3,7},{7,3},{8,12},{12,8},{9,1... | collective-permute-start | bytes 417800 | tf_op jit(solution)/shard_map/ppermute | solution.py:489
  25.2 1.6 %collective-permute-start.8 = (bf16[272,256]{1,0:T(8,128)(2,1)S(1)}, bf16[272,256]{1,0:T(8,128)(2,1)S(1)}, u32[]{:S(2)}, u32[]{:S(2)}) collective-permute-start(bf16[272,256]{1,0:T(8,128)(2,1)S(1)} %collective-permute-done.5.refs_2_), channel_id=1, source_target_pairs={{0,4},{4,0},{1,5},{5,1},{2,6},{6,2},{3,7},{7,3},{8,12},{12,8},{9,1... | collective-permute-start | bytes 417800 | tf_op jit(solution)/shard_map/ppermute | solution.py:489
  26.3 34.1 %copy-start.11 = (f32[32,256]{1,0:T(8,128)S(1)}, f32[32,256]{1,0:T(8,128)}, u32[]{:S(2)}) copy-start(f32[32,256]{1,0:T(8,128)} %get-tuple-element.32) | copy-start | bytes 98308
  51.6 0.7 copy-start
  52.3 12.4 %collective-permute-start.10 = (bf16[144,256]{1,0:T(8,128)(2,1)S(1)}, bf16[144,256]{1,0:T(8,128)(2,1)S(1)}, u32[]{:S(2)}, u32[]{:S(2)}) collective-permute-start(bf16[144,256]{1,0:T(8,128)(2,1)S(1)} %get-tuple-element.40), channel_id=1, source_target_pairs={{0,1},{1,2},{2,3},{4,5},{5,6},{6,7},{8,9},{9,10},{10,11},{12,13},{... | collective-permute-start | bytes 221192 | tf_op jit(solution)/shard_map/ppermute | solution.py:523
  56.5 8.2 %collective-permute-start.11 = (bf16[144,256]{1,0:T(8,128)(2,1)S(1)}, bf16[144,256]{1,0:T(8,128)(2,1)S(1)}, u32[]{:S(2)}, u32[]{:S(2)}) collective-permute-start(bf16[144,256]{1,0:T(8,128)(2,1)S(1)} %get-tuple-element.41), channel_id=1, source_target_pairs={{0,2},{1,3},{2,0},{4,6},{5,7},{6,4},{8,10},{9,11},{10,8},{12,14},{... | collective-permute-start | bytes 221192 | tf_op jit(solution)/shard_map/ppermute | solution.py:523
  58.4 6.8 %collective-permute-start.12 = (bf16[144,256]{1,0:T(8,128)(2,1)S(1)}, bf16[144,256]{1,0:T(8,128)(2,1)S(1)}, u32[]{:S(2)}, u32[]{:S(2)}) collective-permute-start(bf16[144,256]{1,0:T(8,128)(2,1)S(1)} %get-tuple-element.42), channel_id=1, source_target_pairs={{0,3},{1,0},{2,1},{4,7},{5,4},{6,5},{8,11},{9,8},{10,9},{12,15},{1... | collective-permute-start | bytes 221192 | tf_op jit(solution)/shard_map/ppermute | solution.py:523
  60.4 1.3 %collective-permute-start.4 = (f32[32,512]{1,0:T(8,128)S(1)}, f32[32,512]{1,0:T(8,128)S(1)}, u32[]{:S(2)}, u32[]{:S(2)}) collective-permute-start(f32[32,512]{1,0:T(8,128)S(1)} %pad_maximum_fusion), channel_id=1, source_target_pairs={{0,4},{4,0},{1,5},{5,1},{2,6},{6,2},{3,7},{7,3},{8,12},{12,8},{9,1... | collective-permute-start | bytes 196616 | tf_op jit(solution)/shard_map/ppermute | solution.py:524
  61.7 0.6 copy-start.8
  64.7 0.6 copy-start.2
  64.7 0.6 copy-start.3
  65.2 0.6 copy-start.4
  68.0 5.0 %collective-permute-start.15 = (f32[72,256]{1,0:T(8,128)}, f32[72,256]{1,0:T(8,128)S(1)}, u32[]{:S(2)}, u32[]{:S(2)}) collective-permute-start(f32[72,256]{1,0:T(8,128)} %get-tuple-element.45.refs_0_), channel_id=1, source_target_pairs={{0,24},{8,0},{16,8},{24,16},{1,25},{9,1},{17,9},{25,17},{2,26},{10... | collective-permute-start | bytes 221192 | tf_op jit(solution)/shard_map/ppermute | solution.py:549
  70.4 5.0 %collective-permute-start.14 = (f32[72,256]{1,0:T(8,128)}, f32[72,256]{1,0:T(8,128)S(1)}, u32[]{:S(2)}, u32[]{:S(2)}) collective-permute-start(f32[72,256]{1,0:T(8,128)} %get-tuple-element.45.refs_0_), channel_id=1, source_target_pairs={{0,16},{8,24},{16,0},{24,8},{1,17},{9,25},{17,1},{25,9},{2,18},{10... | collective-permute-start | bytes 221192 | tf_op jit(solution)/shard_map/ppermute | solution.py:549
  70.9 5.5 %collective-permute-start.13 = (f32[72,256]{1,0:T(8,128)}, f32[72,256]{1,0:T(8,128)S(1)}, u32[]{:S(2)}, u32[]{:S(2)}) collective-permute-start(f32[72,256]{1,0:T(8,128)} %get-tuple-element.45.refs_0_), channel_id=1, source_target_pairs={{0,8},{8,16},{16,24},{24,0},{1,9},{9,17},{17,25},{25,1},{2,10},{10... | collective-permute-start | bytes 221192 | tf_op jit(solution)/shard_map/ppermute | solution.py:549
  73.0 3.4 %copy-start.5 = (f32[72,256]{1,0:T(8,128)}, f32[72,256]{1,0:T(8,128)S(1)}, u32[]{:S(2)}) copy-start(f32[72,256]{1,0:T(8,128)S(1)} %collective-permute-done.15.refs_3_) | copy-start | bytes 221188
  75.4 1.0 %copy-start.6 = (f32[72,256]{1,0:T(8,128)}, f32[72,256]{1,0:T(8,128)S(1)}, u32[]{:S(2)}) copy-start(f32[72,256]{1,0:T(8,128)S(1)} %collective-permute-done.14.refs_2_) | copy-start | bytes 221188
  76.4 0.6 copy-start.7

commit v4 on v3

--- a/solution.py
+++ b/solution.py
@@ -9,6 +9,7 @@
 
 ITERS = 20
 PARTS = 3
+FINE = 2
 LANES = 128
 F32 = jnp.float32
 BF16 = jnp.bfloat16
@@ -81,8 +82,28 @@
     return jnp.dot(v, order, precision=lax.Precision.HIGHEST, preferred_element_type=F32)
 
 
-def pack_kernel(n_j, rhs, density, stiffness, mass, send, recv, weight, *outs):
-    *outs, pages = outs
+def planes_of(state, density, stiffness, mass):
+    return [state[n].astype(F32) for n in range(2 * PARTS)] + [density[...], stiffness[...], mass[...]]
+
+
+def edge_block(near, far):
+    rows = near[: 2 * PARTS] + [x for v in near[2 * PARTS :] for x in pieces(v)]
+    rows = rows + [jnp.zeros((1, LANES), F32)] * (16 - len(rows))
+    inner = far[: 2 * PARTS] + [jnp.zeros((1, LANES), F32)] * (16 - 2 * PARTS)
+    return jnp.concatenate([jnp.concatenate(rows, axis=0), jnp.concatenate(inner, axis=0)], axis=1)
+
+
+def edge_rows(msg, present):
+    block = msg[msg.shape[0] - 16 :, :].astype(F32)
+    block = jnp.where(present, block, 0.0)
+    near, far = block[:, :LANES], block[:, LANES:]
+    n = 2 * PARTS
+    exact = [near[n + 3 * p : n + 3 * p + 1] + near[n + 3 * p + 1 : n + 3 * p + 2] + near[n + 3 * p + 2 : n + 3 * p + 3] for p in range(3)]
+    return jnp.concatenate([near[:n]] + exact + [jnp.zeros((7, LANES), F32), far], axis=0)
+
+
+def pack_kernel(n_j, rhs, density, stiffness, mass, send, recv, weight, state, *outs):
+    *outs, first, last, line, pages = outs
     rows, cy = density.shape
     tiles = rows // 8
     info = []
@@ -90,6 +111,21 @@
         row, column = placed(ref[...], rows, cy)
         info += [row.astype(F32), column.astype(F32)]
     info += pieces(weight[...])
+    top = lax.axis_index("mx") == 0
+    lane = lax.broadcasted_iota(jnp.int32, (1, LANES), 1)
+    sides = [[[], []], [[], []]]
+    for out in (first, last, line):
+        out[...] = jnp.zeros_like(out)
+    for n, v in enumerate(planes_of(state, density, stiffness, mass)):
+        turned = jnp.transpose(jnp.concatenate([v[:, :LANES], v[:, cy - LANES :]], axis=0))
+        late = pltpu.roll(turned[LANES - 8 :], rows, 1)
+        for k in range(2):
+            sides[0][k].append(jnp.where(lane < rows, turned[k : k + 1], 0.0))
+            sides[1][k].append(jnp.where(lane < rows, late[7 - k : 8 - k], 0.0))
+            line[pl.ds(16 * k + n, 1), :] = jnp.where(top, v[rows - 1 - k : rows - k], v[k : k + 1])
+        first[pl.ds(n, 1), :] = sides[0][0][-1]
+        last[pl.ds(n, 1), :] = sides[1][0][-1]
+    edges = [edge_block(*side).astype(BF16) for side in sides]
     order = lane_order(cy, False)
     slot = 0
 
@@ -116,7 +152,9 @@
         out[2 * rows : 3 * rows, :] = stiff
         out[3 * rows : 4 * rows, :] = rmass
         scale = [jnp.broadcast_to(x, (1, cy)) for x in pieces(most)]
-        out[4 * rows :, :] = jnp.concatenate(info + scale + [jnp.zeros((6, cy), F32)], axis=0).astype(BF16)
+        out[4 * rows : 4 * rows + 16, :] = jnp.concatenate(info + scale + [jnp.zeros((6, cy), F32)], axis=0).astype(BF16)
+        beside = edges[1] if s == 1 else edges[0] if s == n_j - 1 else jnp.zeros((16, cy), BF16)
+        out[4 * rows + 16 :, :] = beside
 
 
 def split(v):
@@ -128,7 +166,7 @@
     blocks = n_i * n_j
     msgs, refs = refs[: blocks], refs[blocks:]
     outs, refs = refs[:n_j], refs[n_j:]
-    field_a, field_b, start, inverse, gain, lag, info, weights, pick, rowmask, spread, place, group, values, pages, plain, ends, rim, frame = refs
+    field_a, field_b, start, inverse, gain, lag, info, weights, pick, rowmask, spread, place, group, values, pages, plain, ends, rim, frame, mid, values_b = refs
     rows, cy = start.shape[2:]
     slots = blocks * cap
     me_i, me_j = lax.axis_index("mx"), lax.axis_index("my")
@@ -137,7 +175,7 @@
     order = [(a, s) for a in range(n_i) for s in range(n_j)]
     index = [lax.rem(me_i + a, n_i) * n_j + lax.rem(me_j + n_j - s, n_j) for a, s in order]
     for msg, b in zip(msgs, index):
-        info[b] = msg[4 * rows :, :].astype(F32)
+        info[b] = msg[4 * rows : 4 * rows + 16, :].astype(F32)
     chunk = lax.broadcasted_iota(jnp.int32, (blocks, slots), 1) // cap
     source = lax.broadcasted_iota(jnp.int32, (blocks, slots), 0)
 
@@ -186,68 +224,90 @@
     lane_r = lax.broadcasted_iota(jnp.int32, (rows, LANES), 1)
     zero = jnp.zeros((rows, LANES), F32)
 
-    def gather(now, b):
-        high, low = split(jnp.concatenate([now[b, 0], now[b, 1]], axis=0))
-        got = jnp.dot(jnp.concatenate([high, low], axis=0), pick[b], preferred_element_type=F32)
+    def gather(held, b, re, im, fine):
+        whole = jnp.concatenate(re + im, axis=0)
+        whole = jnp.concatenate(split(whole), axis=0) if fine else whole.astype(BF16)
+        got = jnp.dot(whole, pick[b], preferred_element_type=F32)
+        mask = rowmask[b]
         for part in range(2):
-            mine = got[part * rows : (part + 1) * rows] + got[(part + 2) * rows : (part + 3) * rows]
-            values[part, pl.ds(b, 1), :] = jnp.sum(mine * rowmask[b], axis=0, keepdims=True)
-
-    def beside(now, then, b):
+            mine = got[part * rows : (part + 1) * rows]
+            if fine:
+                mine += got[(part + 2) * rows : (part + 3) * rows]
+            held[part, pl.ds(b, 1), :] = jnp.sum(mine * mask, axis=0, keepdims=True)
+
+    def mortar_at(held, b, fine):
+        arrived = [jnp.sum(held[part] * group[b], axis=0, keepdims=True) * weights[b : b + 1, :] for part in range(2)]
+        left = []
+        for r in range(0, rows, 16):
+            for v in arrived:
+                left += [spread[b, r : r + 16] * x for x in (split(v) if fine else [v.astype(BF16)])]
+        mortar = jnp.dot(jnp.concatenate(left, axis=0), place[b], preferred_element_type=F32)
+        each = 2 if fine else 1
+        parts = []
+        for r in range(rows // 16 * 2):
+            part = mortar[r * each * 16 : r * each * 16 + 16]
+            parts.append(part + mortar[r * each * 16 + 16 : r * each * 16 + 32] if fine else part)
+        return parts
+
+    def around_of(now, b, part, u):
         i, j = b // n_j, b % n_j
+        lanes = slice(u * LANES, (u + 1) * LANES)
+        others = slice((1 - u) * LANES, (2 - u) * LANES)
+        own, other = now[b, part, :, lanes], now[b, part, :, others]
+        if u == 0:
+            edge = now[b - 1, part, :, others] if j > 0 else zero
+            around = pltpu.roll(jnp.where(lane_r == LANES - 1, edge, other), 1, 1)
+        else:
+            edge = now[b + 1, part, :, others] if j < n_j - 1 else zero
+            around = pltpu.roll(jnp.where(lane_r == 0, edge, other), LANES - 1, 1)
+        around += other
+        above = now[b - n_j, part, rows - 8 :, lanes] if i > 0 else zero[:8]
+        below = now[b + n_j, part, :8, lanes] if i < n_i - 1 else zero[:8]
+        top = pltpu.roll(jnp.where(row8 == 7, above, own[rows - 8 :]), 1, 0)
+        bottom = pltpu.roll(jnp.where(row8 == 0, below, own[:8]), 7, 0)
+        around += jnp.concatenate([top, own[:-8]], axis=0)
+        return around + jnp.concatenate([own[8:], bottom], axis=0)
+
+    def beside(now, b):
         for u in range(2):
             lanes = slice(u * LANES, (u + 1) * LANES)
-            others = slice((1 - u) * LANES, (2 - u) * LANES)
             for part in range(2):
-                own, other = now[b, part, :, lanes], now[b, part, :, others]
-                if u == 0:
-                    edge = now[b - 1, part, :, others] if j > 0 else zero
-                    around = pltpu.roll(jnp.where(lane_r == LANES - 1, edge, other), 1, 1)
-                else:
-                    edge = now[b + 1, part, :, others] if j < n_j - 1 else zero
-                    around = pltpu.roll(jnp.where(lane_r == 0, edge, other), LANES - 1, 1)
-                around += other
-                above = now[b - n_j, part, rows - 8 :, lanes] if i > 0 else zero[:8]
-                below = now[b + n_j, part, :8, lanes] if i < n_i - 1 else zero[:8]
-                top = pltpu.roll(jnp.where(row8 == 7, above, own[rows - 8 :]), 1, 0)
-                bottom = pltpu.roll(jnp.where(row8 == 0, below, own[:8]), 7, 0)
-                around += jnp.concatenate([top, own[:-8]], axis=0)
-                around += jnp.concatenate([own[8:], bottom], axis=0)
-                then[b, part, :, lanes] = around
-
-    def scatter(then, b):
-        left = []
-        for part in range(2):
-            arrived = jnp.sum(values[part] * group[b], axis=0, keepdims=True)
-            left += [spread[b] * x for x in split(arrived * weights[b : b + 1, :])]
-        mortar = jnp.dot(jnp.concatenate(left, axis=0), place[b], preferred_element_type=F32)
-        sums = [
-            then[b, part] + mortar[2 * part * rows : (2 * part + 1) * rows]
-            + mortar[(2 * part + 1) * rows : (2 * part + 2) * rows]
-            for part in range(2)
-        ]
-        g, l = gain[b], lag[b]
-        then[b, 0] = start[b, 0] + sums[0] * g + sums[1] * l
-        then[b, 1] = start[b, 1] + sums[1] * g - sums[0] * l
-
-    def sweep(now, then):
+                mid[b, part, :, lanes] = around_of(now, b, part, u)
+
+    def sweep(now, then, fine, fine_next):
+        held, ahead = (values, values_b) if now is field_a else (values_b, values)
+
+        def finish(b):
+            mortar = mortar_at(held, b, fine)
+            new = ([], [])
+            for n in range(rows // 16):
+                at = slice(n * 16, n * 16 + 16)
+                re, im = mid[b, 0, at] + mortar[2 * n], mid[b, 1, at] + mortar[2 * n + 1]
+                g, l = gain[b, at], lag[b, at]
+                new[0].append(start[b, 0, at] + re * g + im * l)
+                new[1].append(start[b, 1, at] + im * g - re * l)
+                then[b, 0, at], then[b, 1, at] = new[0][-1], new[1][-1]
+            if fine_next is not None:
+                gather(ahead, b, *new, fine_next)
+
         for b in range(blocks):
-            if b < blocks:
-                gather(now, b)
-            if b >= 0:
-                beside(now, then, b - 0)
-        for b in range(blocks):
-            scatter(then, b)
-
-    def pair(step, carry):
-        sweep(field_a, field_b)
-        sweep(field_b, field_a)
+            beside(now, b)
+            finish(b)
+
+    def pair(fine, step, carry):
+        sweep(field_a, field_b, fine, fine)
+        sweep(field_b, field_a, fine, fine)
         return carry
 
-    lax.fori_loop(0, (ITERS - 1) // 2, pair, 0)
+    fine_pairs = min(FINE, ITERS - 1) // 2
+    pairs = (ITERS - 1) // 2
+    for b in range(blocks):
+        gather(values, b, [field_a[b, 0]], [field_a[b, 1]], False)
+    lax.fori_loop(0, pairs - fine_pairs, functools.partial(pair, False), 0)
+    lax.fori_loop(0, fine_pairs, functools.partial(pair, True), 0)
     last = field_a
     if (ITERS - 1) % 2:
-        sweep(field_a, field_b)
+        sweep(field_a, field_b, FINE > 0, None)
         last = field_b
     tiles = rows // 8
     back = lane_order(cy, True)
@@ -278,7 +338,7 @@
                     part * 4 + j : part * 4 + j + 1
                 ]
     for s, out in enumerate(outs):
-        base = pl.multiple_of(LANES + lax.rem(me_j + s, n_j) * cy, LANES)
+        base = pl.multiple_of(LANES + (me_j ^ s) * cy, LANES)
         frame[...] = jnp.zeros_like(frame)
         block = [plain[part, :, pl.ds(base, cy)] for part in range(2)]
         for part in range(2):
@@ -300,32 +360,14 @@
             out[at : at + v.shape[0], :] = v
 
 
-def planes_of(state, density, stiffness, mass):
-    return [state[n].astype(F32) for n in range(2 * PARTS)] + [density[...], stiffness[...], mass[...]]
-
-
-def edge_kernel(state, density, stiffness, mass, first, last, line):
-    rows, cy = density.shape
-    for out in (first, last, line):
-        out[...] = jnp.zeros_like(out)
-    top = lax.axis_index("mx") == 0
-    lane = lax.broadcasted_iota(jnp.int32, (1, LANES), 1)
-    for n, v in enumerate(planes_of(state, density, stiffness, mass)):
-        turned = jnp.transpose(jnp.concatenate([v[:, :LANES], v[:, cy - LANES :]], axis=0))
-        late = pltpu.roll(turned[LANES - 8 :], rows, 1)
-        for k in range(2):
-            at = pl.ds(16 * k + n, 1)
-            first[at, :] = jnp.where(lane < rows, turned[k : k + 1], 0.0)
-            last[at, :] = jnp.where(lane < rows, late[7 - k : 8 - k], 0.0)
-            line[at, :] = jnp.where(top, v[rows - 1 - k : rows - k], v[k : k + 1])
-
-
 def response_kernel(
-    omega, state, density, stiffness, mass, first, last, west, east, beyond, inner, ring, rho_ring
+    n_j, omega, state, density, stiffness, mass, first, last, line, west, east, *refs
 ):
+    beyond_west, beyond_east, inner, ring, rho_ring = refs
     rows, cy = density.shape
     w = omega[0]
     top = lax.axis_index("mx") == 0
+    present = (lax.axis_index("my") > 0, lax.axis_index("my") < n_j - 1)
     zero = jnp.zeros((1, cy), F32)
 
     def terms(u_re, u_im, nb_re, nb_im, rho, k, m):
@@ -334,9 +376,9 @@
         db = 0.2 * w * (dstiff + m)
         return da * u_re - db * u_im - dstiff * nb_re, da * u_im + db * u_re - dstiff * nb_im
 
-    line = beyond[:, :cy]
-    siblings = (beyond[:, cy : cy + LANES], beyond[:, cy + LANES :])
-    side = [x[...] + pltpu.roll(y, rows, 1) for x, y in zip((west, east), siblings)]
+    line = line[...]
+    siblings = [edge_rows(m, p) for m, p in zip((beyond_west, beyond_east), present)]
+    side = [edge_rows(m, p) + pltpu.roll(y, rows, 1) for m, p, y in zip((west, east), present, siblings)]
     lane = lax.broadcasted_iota(jnp.int32, (16, LANES), 1)
     start = jnp.where(top, 0, rows)
     stop = jnp.where(top, LANES - 1, rows - 1)
@@ -388,12 +430,12 @@
         inner[c], inner[PARTS + c] = t
 
 
-def sens_kernel(n_j, inner, ring, *refs):
-    msgs, (field, sens) = refs[:n_j], refs[n_j:]
+def sens_kernel(inner, ring, *refs):
+    *msgs, field, sens = refs
     rows = inner.shape[1]
     sens[...] = jnp.zeros_like(sens)
     for s, msg in enumerate(msgs):
-        c = lax.rem(lax.axis_index("my") + n_j - s, n_j)
+        c = lax.axis_index("my") ^ s
 
         @pl.when(c < PARTS)
         def _(msg=msg, c=c):
@@ -444,13 +486,6 @@
     return pl.BlockSpec(memory_space=pltpu.SMEM)
 
 
-def shifts(n_j, source_limit, target_limit):
-    return [
-        [(a, (a + s) % n_j) for a in range(n_j) if a < source_limit and (a + s) % n_j < target_limit]
-        for s in range(1, n_j)
-    ]
-
-
 def gathered(
     adjoint_rhs, state, density, stiffness, mass, omega, send_rows, recv_rows, mortar_weight
 ):
@@ -460,33 +495,25 @@
     blocks = n_i * n_j
     slots = send_rows.shape[1]
     cap = slots // blocks
-    up = [(a, a + 1) for a in range(n_j - 1)]
-    edge = jax.ShapeDtypeStruct((32, LANES), F32)
     planes = (state.reshape(2 * PARTS, rows, cy), density, stiffness, mass)
-    first, last, line = pl.pallas_call(
-        edge_kernel,
-        out_shape=[edge, edge, jax.ShapeDtypeStruct((32, cy), F32)],
-        in_specs=[vmem()] * 4,
-        out_specs=[vmem()] * 3,
-        name="edges",
-    )(*planes)
-    west = lax.ppermute(last, "my", up)
-    east = lax.ppermute(first, "my", [(b, a) for a, b in up])
-    message = jax.ShapeDtypeStruct((4 * rows + 16, cy), BF16)
-    own = pl.pallas_call(
+    edge = jax.ShapeDtypeStruct((16, LANES), F32)
+    message = jax.ShapeDtypeStruct((4 * rows + 32, cy), BF16)
+    *own, first, last, line = pl.pallas_call(
         functools.partial(pack_kernel, n_j),
-        out_shape=[message] * n_j,
-        in_specs=[vmem()] * 7,
-        out_specs=[vmem()] * n_j,
+        out_shape=[message] * n_j + [edge, edge, jax.ShapeDtypeStruct((32, cy), F32)],
+        in_specs=[vmem()] * 8,
+        out_specs=[vmem()] * (n_j + 3),
         scratch_shapes=[pltpu.VMEM((8, rows, LANES), F32)],
         name="pack",
-    )(rhs, density, stiffness, mass, send_rows, recv_rows, mortar_weight)
+    )(rhs, density, stiffness, mass, send_rows, recv_rows, mortar_weight, planes[0])
     msgs = [own[0]]
-    for s, pairs in enumerate(shifts(n_j, n_j, PARTS), 1):
+    for s in range(1, n_j):
+        pairs = [(a, (a + s) % n_j) for a in range(n_j)]
+        pairs = [(a, b) for a, b in pairs if b < PARTS or (s == 1 and b == PARTS)]
         msgs.append(lax.ppermute(own[s], "my", pairs))
-    msgs[1], first, last = lax.optimization_barrier((msgs[1], first, last))
-    msgs[-1], west, east = lax.optimization_barrier((msgs[-1], west, east))
-    msgs += [lax.ppermute(m, "mx", [(0, 1), (1, 0)]) for m in msgs]
+    swap = [(0, 1), (1, 0)]
+    msgs += [lax.ppermute(m, "mx", swap) for m in msgs]
+    line = lax.ppermute(line, "mx", swap)
     block = (blocks, rows, cy)
     outs = pl.pallas_call(
         functools.partial(sweep_kernel, n_i, n_j, cap),
@@ -513,28 +540,30 @@
             pltpu.VMEM((2, 8, n_j * cy + 2 * LANES), F32),
             pltpu.VMEM((8, cy), F32),
             pltpu.VMEM((16, cy), F32),
+            pltpu.VMEM((blocks, 2, rows, cy), F32),
+            pltpu.VMEM((2, blocks, slots), F32),
         ],
         compiler_params=pltpu.CompilerParams(vmem_limit_bytes=40 * 1024 * 1024),
         cost_estimate=pl.CostEstimate(flops=30_000_000_000, bytes_accessed=4_000_000, transcendentals=0),
         name="sweeps",
     )(omega, *msgs)
-    parts = [outs[0]]
-    for s, pairs in enumerate(shifts(n_j, PARTS, n_j), 1):
-        parts.append(lax.ppermute(outs[s], "my", pairs))
-    beyond = lax.ppermute(jnp.concatenate([line, west, east], axis=1), "mx", [(0, 1), (1, 0)])
+    parts = {0: outs[0]}
+    for s in (2, 3, 1):
+        parts[s] = lax.ppermute(outs[s], "my", [(a, a ^ s) for a in range(PARTS)])
+    parts = [parts[s] for s in range(n_j)]
     inner, ring, rho_ring = pl.pallas_call(
-        response_kernel,
+        functools.partial(response_kernel, n_j),
         out_shape=[
             jax.ShapeDtypeStruct((2 * PARTS, rows, cy), F32),
             jax.ShapeDtypeStruct((2 * PARTS, 8, cy), F32),
             jax.ShapeDtypeStruct((8, cy), F32),
         ],
-        in_specs=[smem()] + [vmem()] * 9,
+        in_specs=[smem()] + [vmem()] * 11,
         out_specs=[vmem()] * 3,
         name="response",
-    )(omega, *planes, first, last, west, east, beyond)
+    )(omega, *planes, first, last, line, msgs[1], msgs[n_j - 1], msgs[n_j + 1], msgs[2 * n_j - 1])
     field, sens = pl.pallas_call(
-        functools.partial(sens_kernel, n_j),
+        sens_kernel,
         out_shape=[
             jax.ShapeDtypeStruct((2 * PARTS, rows, cy), F32),
             jax.ShapeDtypeStruct((rows + 8, cy), F32),
@@ -630,7 +659,7 @@
 def on_device(*args):
     rows, cy = args[2].shape
     n_i, n_j = lax.axis_size("mx"), lax.axis_size("my")
-    fits = n_i == 2 and PARTS <= n_j <= 4 and rows == 64 and cy == 2 * LANES and args[6].shape[1] == cy
+    fits = n_i == 2 and n_j == 4 and rows == 64 and cy == 2 * LANES and args[6].shape[1] == cy
     return (gathered if fits else distributed)(*args)
 
 

time: 79.4 us -> 70.6 us (0.89)
  the two profiles are of different devices: /device:TPU:0 before, /device:TPU:8 now
where the time goes in v4:
time: 70.6 us; the launch traced here: 70.2 us
  Pallas kernels  29.9 us (42%)
  starting transfers between devices  20.4 us (29%)
  waiting for transfers between devices  14.9 us (21%)
  local copies, waits for them, and re-layouts  3.51 us (5%)
  between operations  1.48 us (2%)
    pallas_call x1, Pallas kernels, gathered(): pl.pallas_call(functools.partial(sweep_kernel, n_i, n_j, cap), out_shape=...  19.8 us
    ppermute x3, starting transfers between devices, gathered(): parts[s] = lax.ppermute(outs[s], 'my', [(a, a ^ s) for a in range(PARTS)])  11 us
    ppermute x3, waiting for transfers between devices, gathered(): msgs.append(lax.ppermute(own[s], 'my', pairs))  8.29 us
    ppermute x3, starting transfers between devices, gathered(): msgs.append(lax.ppermute(own[s], 'my', pairs))  5.21 us
    ppermute x3, waiting for transfers between devices, gathered(): lax.ppermute(sens, 'freq', [(a, (a + s) % size) for a in range(size)])  5.05 us
    ppermute x3, starting transfers between devices, gathered(): lax.ppermute(sens, 'freq', [(a, (a + s) % size) for a in range(size)])  3.54 us
    unnamed x28, local copies, waits for them, and re-layouts  3.51 us
    pallas_call x1, Pallas kernels, gathered(): pl.pallas_call(functools.partial(pack_kernel, n_j), out_shape=[message] *...  3.48 us
  transfers between devices with their start and end apart: 14, of which 7 were waited for; matrix products, arithmetic and copies ran while one was open for 0% of the time, Pallas kernels for 4%

profile of v4, /device:TPU:8, one launch (start us, length us, event | category | flops | bytes accessed | tf_op | source)
XLA Modules:
  0.0 70.2 jit_solution(9242652934748248218)
XLA Ops:
  0.6 3.5 %pack.1 = (bf16[288,256]{1,0:T(8,128)(2,1)}, bf16[288,256]{1,0:T(8,128)(2,1)}, bf16[288,256]{1,0:T(8,128)(2,1)}, bf16[288,256]{1,0:T(8,128)(2,1)}, f32[16,128]{1...) custom-call(f32[6,64,256]{2,1,0:T(8,128)} %bitcast.5, f32[64,256]{1,0:T(8,128)} %density.5, f32[64,256]{1,0:T(8,128)} %stiffness.3, ...), custom_call_target="tpu_custom_call" | custom-call | tf_op jit(solution)/shard_map/pack/pallas_call | solution.py:501
  4.1 1.6 %collective-permute-start.1 = (bf16[288,256]{1,0:T(8,128)(2,1)}, bf16[288,256]{1,0:T(8,128)(2,1)S(1)}, u32[]{:S(2)}, u32[]{:S(2)}) collective-permute-start(bf16[288,256]{1,0:T(8,128)(2,1)} %get-tuple-element.21), channel_id=1, source_target_pairs={{0,1},{1,2},{2,3},{3,0},{4,5},{5,6},{6,7},{7,4},{8,9},{9,10},{10,1... | collective-permute-start | bytes 442376 | tf_op jit(solution)/shard_map/ppermute | solution.py:513
  5.7 2.3 %collective-permute-start.2 = (bf16[288,256]{1,0:T(8,128)(2,1)}, bf16[288,256]{1,0:T(8,128)(2,1)S(1)}, u32[]{:S(2)}, u32[]{:S(2)}) collective-permute-start(bf16[288,256]{1,0:T(8,128)(2,1)} %get-tuple-element.22), channel_id=1, source_target_pairs={{1,0},{2,1},{3,2},{5,4},{6,5},{7,6},{9,8},{10,9},{11,10},{13,12},{... | collective-permute-start | bytes 442376 | tf_op jit(solution)/shard_map/ppermute | solution.py:513
  8.0 1.3 %collective-permute-start.5 = (bf16[288,256]{1,0:T(8,128)(2,1)}, bf16[288,256]{1,0:T(8,128)(2,1)S(1)}, u32[]{:S(2)}, u32[]{:S(2)}) collective-permute-start(bf16[288,256]{1,0:T(8,128)(2,1)} %get-tuple-element.26), channel_id=1, source_target_pairs={{0,2},{2,0},{3,1},{4,6},{6,4},{7,5},{8,10},{10,8},{11,9},{12,14},{... | collective-permute-start | bytes 442376 | tf_op jit(solution)/shard_map/ppermute | solution.py:513
  9.3 0.1 collective-permute-start.6
  9.4 0.5 collective-permute-done.1.west.refs_1_
  9.9 0.0 copy-start
  9.9 0.0 collective-permute-start.3
  9.9 7.8 %collective-permute-done.2.east.refs_3_ = bf16[288,256]{1,0:T(8,128)(2,1)S(1)} collective-permute-done((bf16[288,256]{1,0:T(8,128)(2,1)}, bf16[288,256]{1,0:T(8,128)(2,1)S(1)}, u32[]{:S(2)}, u32[]{:S(2)}) %collective-permute-start.2) | collective-permute-done | bytes 147488 | tf_op jit(solution)/shard_map/ppermute | solution.py:513
  17.7 0.0 copy-start.1
  17.7 0.0 collective-permute-start.4
  17.7 0.0 collective-permute-done.5.refs_2_
  17.7 0.5 collective-permute-start.7
  18.9 0.0 collective-permute-done.6.refs_4_
  18.9 0.0 collective-permute-done.3.refs_0_.refs_5_
  18.9 0.0 copy-start.2
  18.9 0.2 collective-permute-done.4.refs_1_.refs_7_
  19.1 0.0 copy-start.3
  19.1 0.2 collective-permute-done.7.refs_6_
  19.3 0.0 copy-start.5
  19.3 0.9 %copy-done.5 = bf16[288,256]{1,0:T(8,128)(2,1)S(1)} copy-done((bf16[288,256]{1,0:T(8,128)(2,1)S(1)}, bf16[288,256]{1,0:T(8,128)(2,1)}, u32[]{:S(2)}) %copy-start.5) | copy-done | bytes 147480
  20.2 0.0 copy-start.13
  20.2 19.8 %sweeps.1 = (f32[144,256]{1,0:T(8,128)S(1)}, bf16[144,256]{1,0:T(8,128)(2,1)S(1)}, bf16[144,256]{1,0:T(8,128)(2,1)S(1)}, bf16[144,256]{1,0:T(8,128)(2,1)S(1)}) custom-call(f32[1]{0:T(128)S(6)} %copy.11.omega, bf16[288,256]{1,0:T(8,128)(2,1)S(1)} %copy-done.5, bf16[288,256]{1,0:T(8,128)(2,1)S(1)} %collective-permute-done.1.west.refs_1_, ...), custom_call_target="tpu_custom_call" | custom-call | flops 30000001024 | bytes 4000000 | tf_op jit(solution)/shard_map/sweeps/pallas_call | solution.py:518
  40.0 0.0 copy-done
  40.0 0.0 copy-done.1
  40.0 0.0 copy-done.2
  40.0 0.0 copy-done.3
  40.1 0.0 copy-start.4
  40.1 0.7 copy-done.4
  40.7 5.7 %collective-permute-start.8 = (bf16[144,256]{1,0:T(8,128)(2,1)S(1)}, bf16[144,256]{1,0:T(8,128)(2,1)S(1)}, u32[]{:S(2)}, u32[]{:S(2)}) collective-permute-start(bf16[144,256]{1,0:T(8,128)(2,1)S(1)} %get-tuple-element.28), channel_id=1, source_target_pairs={{0,1},{1,0},{2,3},{4,5},{5,4},{6,7},{8,9},{9,8},{10,11},{12,13},{1... | collective-permute-start | bytes 221192 | tf_op jit(solution)/shard_map/ppermute | solution.py:552
  46.4 1.3 %collective-permute-start.9 = (bf16[144,256]{1,0:T(8,128)(2,1)S(1)}, bf16[144,256]{1,0:T(8,128)(2,1)S(1)}, u32[]{:S(2)}, u32[]{:S(2)}) collective-permute-start(bf16[144,256]{1,0:T(8,128)(2,1)S(1)} %get-tuple-element.29), channel_id=1, source_target_pairs={{0,2},{1,3},{2,0},{4,6},{5,7},{6,4},{8,10},{9,11},{10,8},{12,14},{... | collective-permute-start | bytes 221192 | tf_op jit(solution)/shard_map/ppermute | solution.py:552
  47.7 4.0 %collective-permute-start.10 = (bf16[144,256]{1,0:T(8,128)(2,1)S(1)}, bf16[144,256]{1,0:T(8,128)(2,1)S(1)}, u32[]{:S(2)}, u32[]{:S(2)}) collective-permute-start(bf16[144,256]{1,0:T(8,128)(2,1)S(1)} %get-tuple-element.30), channel_id=1, source_target_pairs={{0,3},{1,2},{2,1},{4,7},{5,6},{6,5},{8,11},{9,10},{10,9},{12,15},{... | collective-permute-start | bytes 221192 | tf_op jit(solution)/shard_map/ppermute | solution.py:552
  51.7 0.0 copy-done.13
  51.7 0.1 collective-permute-start
  51.8 1.2 %collective-permute-done.line = f32[32,256]{1,0:T(8,128)S(1)} collective-permute-done((f32[32,256]{1,0:T(8,128)S(1)}, f32[32,256]{1,0:T(8,128)S(1)}, u32[]{:S(2)}, u32[]{:S(2)}) %collective-permute-start) | collective-permute-done | bytes 32800 | tf_op jit(solution)/shard_map/ppermute | solution.py:516
  53.0 0.0 copy-start.12
  53.0 0.6 copy-done.12
  53.6 2.6 %response.1 = (f32[6,64,256]{2,1,0:T(8,128)}, f32[6,8,256]{2,1,0:T(8,128)}, f32[8,256]{1,0:T(8,128)}) custom-call(f32[1]{0:T(128)S(6)} %copy.11.omega, bf16[6,64,256]{2,1,0:T(8,128)(2,1)} %bitcast.4, f32[64,256]{1,0:T(8,128)} %density.5, f32[64,256]{1,0:T(8,128)} %stiffness.3, f32[64,256]{1,0:T(8,128)} %mass.3, f32[16,128]{1,0:T(8,128)} %get-tuple-element.18.first, ...), custom_call_target="tpu_custom_call" | custom-call | tf_op jit(solution)/shard_map/response/pallas_call | solution.py:554
  56.2 0.0 collective-permute-done.8.refs_1_
  56.2 0.0 copy-start.6
  56.2 0.0 collective-permute-done.9.refs_2_
  56.2 0.0 copy-start.7
  56.2 0.0 collective-permute-done.10.refs_3_
  56.2 0.0 copy-start.8
  56.2 0.6 copy-done.6
  56.8 0.0 copy-done.7
  56.9 0.0 copy-done.8
  56.9 2.1 %sensitivity.1 = (f32[6,64,256]{2,1,0:T(8,128)}, f32[72,256]{1,0:T(8,128)}) custom-call(f32[6,64,256]{2,1,0:T(8,128)} %get-tuple-element.23.inner, f32[6,8,256]{2,1,0:T(8,128)} %get-tuple-element.24.ring, f32[144,256]{1,0:T(8,128)} %copy-done.4, bf16[144,256]{1,0:T(8,128)(2,1)} %copy-done.6, bf16[144,256]{1,0:T(8,128)(2,1)} %copy-done.7, ...), custom_call_target="tpu_custom_call" | custom-call | tf_op jit(solution)/shard_map/sensitivity/pallas_call | solution.py:565
  59.0 2.5 %collective-permute-start.13 = (f32[72,256]{1,0:T(8,128)}, f32[72,256]{1,0:T(8,128)S(1)}, u32[]{:S(2)}, u32[]{:S(2)}) collective-permute-start(f32[72,256]{1,0:T(8,128)} %get-tuple-element.33.refs_0_), channel_id=1, source_target_pairs={{0,24},{8,0},{16,8},{24,16},{1,25},{9,1},{17,9},{25,17},{2,26},{10... | collective-permute-start | bytes 221192 | tf_op jit(solution)/shard_map/ppermute | solution.py:578
  61.4 0.5 collective-permute-start.12
  61.9 0.6 collective-permute-start.11
  62.5 1.9 %collective-permute-done.13.refs_3_ = f32[72,256]{1,0:T(8,128)S(1)} collective-permute-done((f32[72,256]{1,0:T(8,128)}, f32[72,256]{1,0:T(8,128)S(1)}, u32[]{:S(2)}, u32[]{:S(2)}) %collective-permute-start.13) | collective-permute-done | bytes 73760 | tf_op jit(solution)/shard_map/ppermute | solution.py:578
  64.4 0.0 copy-start.9
  64.4 3.2 %collective-permute-done.12.refs_2_ = f32[72,256]{1,0:T(8,128)S(1)} collective-permute-done((f32[72,256]{1,0:T(8,128)}, f32[72,256]{1,0:T(8,128)S(1)}, u32[]{:S(2)}, u32[]{:S(2)}) %collective-permute-start.12) | collective-permute-done | bytes 73760 | tf_op jit(solution)/shard_map/ppermute | solution.py:578
  67.6 0.0 copy-start.10
  67.6 0.0 collective-permute-done.11.refs_1_
  67.6 0.0 copy-start.11
  67.6 0.0 copy-done.9
  67.6 0.6 copy-done.10
  68.2 0.0 copy-done.11
  68.3 1.9 %filter.1 = f32[64,256]{1,0:T(8,128)} custom-call(f32[64,256]{1,0:T(8,128)} %density.5, f32[8,256]{1,0:T(8,128)} %get-tuple-element.32.ring, f32[72,256]{1,0:T(8,128)} %get-tuple-element.33.refs_0_, f32[72,256]{1,0:T(8,128)} %copy-done.11, f32[72,256]{1,0:T(8,128)} %copy-done.10, f32[72,256]{1,0:T(8,128)} %copy-done.9), custom_call_target="tpu_custom_call" | custom-call | tf_op jit(solution)/shard_map/filter/pallas_call | solution.py:579
Async XLA Ops:
  4.1 5.8 %collective-permute-start.1 = (bf16[288,256]{1,0:T(8,128)(2,1)}, bf16[288,256]{1,0:T(8,128)(2,1)S(1)}, u32[]{:S(2)}, u32[]{:S(2)}) collective-permute-start(bf16[288,256]{1,0:T(8,128)(2,1)} %get-tuple-element.21), channel_id=1, source_target_pairs={{0,1},{1,2},{2,3},{3,0},{4,5},{5,6},{6,7},{7,4},{8,9},{9,10},{10,1... | collective-permute-start | bytes 442376 | tf_op jit(solution)/shard_map/ppermute | solution.py:513
  5.7 12.0 %collective-permute-start.2 = (bf16[288,256]{1,0:T(8,128)(2,1)}, bf16[288,256]{1,0:T(8,128)(2,1)S(1)}, u32[]{:S(2)}, u32[]{:S(2)}) collective-permute-start(bf16[288,256]{1,0:T(8,128)(2,1)} %get-tuple-element.22), channel_id=1, source_target_pairs={{1,0},{2,1},{3,2},{5,4},{6,5},{7,6},{9,8},{10,9},{11,10},{13,12},{... | collective-permute-start | bytes 442376 | tf_op jit(solution)/shard_map/ppermute | solution.py:513
  8.0 9.7 %collective-permute-start.5 = (bf16[288,256]{1,0:T(8,128)(2,1)}, bf16[288,256]{1,0:T(8,128)(2,1)S(1)}, u32[]{:S(2)}, u32[]{:S(2)}) collective-permute-start(bf16[288,256]{1,0:T(8,128)(2,1)} %get-tuple-element.26), channel_id=1, source_target_pairs={{0,2},{2,0},{3,1},{4,6},{6,4},{7,5},{8,10},{10,8},{11,9},{12,14},{... | collective-permute-start | bytes 442376 | tf_op jit(solution)/shard_map/ppermute | solution.py:513
  9.3 9.5 %collective-permute-start.6 = (bf16[288,256]{1,0:T(8,128)(2,1)}, bf16[288,256]{1,0:T(8,128)(2,1)S(1)}, u32[]{:S(2)}, u32[]{:S(2)}) collective-permute-start(bf16[288,256]{1,0:T(8,128)(2,1)} %get-tuple-element.25.refs_0_), channel_id=1, source_target_pairs={{0,4},{4,0},{1,5},{5,1},{2,6},{6,2},{3,7},{7,3},{8,12},{12,8},{9,1... | collective-permute-start | bytes 442376 | tf_op jit(solution)/shard_map/ppermute | solution.py:515
  9.9 30.1 %copy-start = (bf16[288,256]{1,0:T(8,128)(2,1)}, bf16[288,256]{1,0:T(8,128)(2,1)S(1)}, u32[]{:S(2)}) copy-start(bf16[288,256]{1,0:T(8,128)(2,1)S(1)} %collective-permute-done.1.west.refs_1_) | copy-start | bytes 442372
  9.9 9.0 %collective-permute-start.3 = (bf16[288,256]{1,0:T(8,128)(2,1)S(1)}, bf16[288,256]{1,0:T(8,128)(2,1)S(1)}, u32[]{:S(2)}, u32[]{:S(2)}) collective-permute-start(bf16[288,256]{1,0:T(8,128)(2,1)S(1)} %collective-permute-done.1.west.refs_1_), channel_id=1, source_target_pairs={{0,4},{4,0},{1,5},{5,1},{2,6},{6,2},{3,7},{7,3},{8,12},{12,8},{9,1... | collective-permute-start | bytes 442376 | tf_op jit(solution)/shard_map/ppermute | solution.py:515
  17.7 22.3 %copy-start.1 = (bf16[288,256]{1,0:T(8,128)(2,1)}, bf16[288,256]{1,0:T(8,128)(2,1)S(1)}, u32[]{:S(2)}) copy-start(bf16[288,256]{1,0:T(8,128)(2,1)S(1)} %collective-permute-done.2.east.refs_3_) | copy-start | bytes 442372
  17.7 1.4 %collective-permute-start.4 = (bf16[288,256]{1,0:T(8,128)(2,1)S(1)}, bf16[288,256]{1,0:T(8,128)(2,1)S(1)}, u32[]{:S(2)}, u32[]{:S(2)}) collective-permute-start(bf16[288,256]{1,0:T(8,128)(2,1)S(1)} %collective-permute-done.2.east.refs_3_), channel_id=1, source_target_pairs={{0,4},{4,0},{1,5},{5,1},{2,6},{6,2},{3,7},{7,3},{8,12},{12,8},{9,1... | collective-permute-start | bytes 442376 | tf_op jit(solution)/shard_map/ppermute | solution.py:515
  17.7 1.6 %collective-permute-start.7 = (bf16[288,256]{1,0:T(8,128)(2,1)S(1)}, bf16[288,256]{1,0:T(8,128)(2,1)S(1)}, u32[]{:S(2)}, u32[]{:S(2)}) collective-permute-start(bf16[288,256]{1,0:T(8,128)(2,1)S(1)} %collective-permute-done.5.refs_2_), channel_id=1, source_target_pairs={{0,4},{4,0},{1,5},{5,1},{2,6},{6,2},{3,7},{7,3},{8,12},{12,8},{9,1... | collective-permute-start | bytes 442376 | tf_op jit(solution)/shard_map/ppermute | solution.py:515
  18.9 21.1 %copy-start.2 = (bf16[288,256]{1,0:T(8,128)(2,1)}, bf16[288,256]{1,0:T(8,128)(2,1)S(1)}, u32[]{:S(2)}) copy-start(bf16[288,256]{1,0:T(8,128)(2,1)S(1)} %collective-permute-done.3.refs_0_.refs_5_) | copy-start | bytes 442372
  19.1 21.0 %copy-start.3 = (bf16[288,256]{1,0:T(8,128)(2,1)}, bf16[288,256]{1,0:T(8,128)(2,1)S(1)}, u32[]{:S(2)}) copy-start(bf16[288,256]{1,0:T(8,128)(2,1)S(1)} %collective-permute-done.4.refs_1_.refs_7_) | copy-start | bytes 442372
  19.3 0.9 %copy-start.5 = (bf16[288,256]{1,0:T(8,128)(2,1)S(1)}, bf16[288,256]{1,0:T(8,128)(2,1)}, u32[]{:S(2)}) copy-start(bf16[288,256]{1,0:T(8,128)(2,1)} %get-tuple-element.25.refs_0_) | copy-start | bytes 442372
  20.2 31.5 %copy-start.13 = (f32[32,256]{1,0:T(8,128)S(1)}, f32[32,256]{1,0:T(8,128)}, u32[]{:S(2)}) copy-start(f32[32,256]{1,0:T(8,128)} %get-tuple-element.20) | copy-start | bytes 98308
  40.1 0.7 copy-start.4
  40.7 15.5 %collective-permute-start.8 = (bf16[144,256]{1,0:T(8,128)(2,1)S(1)}, bf16[144,256]{1,0:T(8,128)(2,1)S(1)}, u32[]{:S(2)}, u32[]{:S(2)}) collective-permute-start(bf16[144,256]{1,0:T(8,128)(2,1)S(1)} %get-tuple-element.28), channel_id=1, source_target_pairs={{0,1},{1,0},{2,3},{4,5},{5,4},{6,7},{8,9},{9,8},{10,11},{12,13},{1... | collective-permute-start | bytes 221192 | tf_op jit(solution)/shard_map/ppermute | solution.py:552
  46.4 9.8 %collective-permute-start.9 = (bf16[144,256]{1,0:T(8,128)(2,1)S(1)}, bf16[144,256]{1,0:T(8,128)(2,1)S(1)}, u32[]{:S(2)}, u32[]{:S(2)}) collective-permute-start(bf16[144,256]{1,0:T(8,128)(2,1)S(1)} %get-tuple-element.29), channel_id=1, source_target_pairs={{0,2},{1,3},{2,0},{4,6},{5,7},{6,4},{8,10},{9,11},{10,8},{12,14},{... | collective-permute-start | bytes 221192 | tf_op jit(solution)/shard_map/ppermute | solution.py:552
  47.7 8.5 %collective-permute-start.10 = (bf16[144,256]{1,0:T(8,128)(2,1)S(1)}, bf16[144,256]{1,0:T(8,128)(2,1)S(1)}, u32[]{:S(2)}, u32[]{:S(2)}) collective-permute-start(bf16[144,256]{1,0:T(8,128)(2,1)S(1)} %get-tuple-element.30), channel_id=1, source_target_pairs={{0,3},{1,2},{2,1},{4,7},{5,6},{6,5},{8,11},{9,10},{10,9},{12,15},{... | collective-permute-start | bytes 221192 | tf_op jit(solution)/shard_map/ppermute | solution.py:552
  51.7 1.3 %collective-permute-start = (f32[32,256]{1,0:T(8,128)S(1)}, f32[32,256]{1,0:T(8,128)S(1)}, u32[]{:S(2)}, u32[]{:S(2)}) collective-permute-start(f32[32,256]{1,0:T(8,128)S(1)} %copy-done.13), channel_id=1, source_target_pairs={{0,4},{4,0},{1,5},{5,1},{2,6},{6,2},{3,7},{7,3},{8,12},{12,8},{9,1... | collective-permute-start | bytes 98312 | tf_op jit(solution)/shard_map/ppermute | solution.py:516
  53.0 0.6 copy-start.12
  56.2 0.6 copy-start.6
  56.2 0.6 copy-start.7
  56.2 0.6 copy-start.8
  59.0 5.4 %collective-permute-start.13 = (f32[72,256]{1,0:T(8,128)}, f32[72,256]{1,0:T(8,128)S(1)}, u32[]{:S(2)}, u32[]{:S(2)}) collective-permute-start(f32[72,256]{1,0:T(8,128)} %get-tuple-element.33.refs_0_), channel_id=1, source_target_pairs={{0,24},{8,0},{16,8},{24,16},{1,25},{9,1},{17,9},{25,17},{2,26},{10... | collective-permute-start | bytes 221192 | tf_op jit(solution)/shard_map/ppermute | solution.py:578
  61.4 6.1 %collective-permute-start.12 = (f32[72,256]{1,0:T(8,128)}, f32[72,256]{1,0:T(8,128)S(1)}, u32[]{:S(2)}, u32[]{:S(2)}) collective-permute-start(f32[72,256]{1,0:T(8,128)} %get-tuple-element.33.refs_0_), channel_id=1, source_target_pairs={{0,16},{8,24},{16,0},{24,8},{1,17},{9,25},{17,1},{25,9},{2,18},{10... | collective-permute-start | bytes 221192 | tf_op jit(solution)/shard_map/ppermute | solution.py:578
  61.9 5.6 %collective-permute-start.11 = (f32[72,256]{1,0:T(8,128)}, f32[72,256]{1,0:T(8,128)S(1)}, u32[]{:S(2)}, u32[]{:S(2)}) collective-permute-start(f32[72,256]{1,0:T(8,128)} %get-tuple-element.33.refs_0_), channel_id=1, source_target_pairs={{0,8},{8,16},{16,24},{24,0},{1,9},{9,17},{17,25},{25,1},{2,10},{10... | collective-permute-start | bytes 221192 | tf_op jit(solution)/shard_map/ppermute | solution.py:578
  64.4 3.2 %copy-start.9 = (f32[72,256]{1,0:T(8,128)}, f32[72,256]{1,0:T(8,128)S(1)}, u32[]{:S(2)}) copy-start(f32[72,256]{1,0:T(8,128)S(1)} %collective-permute-done.13.refs_3_) | copy-start | bytes 221188
  67.6 0.6 copy-start.10
  67.6 0.7 copy-start.11

commit v5 on v4

--- a/solution.py
+++ b/solution.py
@@ -38,7 +38,7 @@
     a = lax.broadcasted_iota(jnp.int32, (cy, cy), 0)
     b = lax.broadcasted_iota(jnp.int32, (cy, cy), 1)
     natural, kept = (b, a) if inverse else (a, b)
-    return ((natural % 2) * LANES + natural // 2 == kept).astype(F32)
+    return ((natural % 2) * LANES + natural // 2 == kept).astype(F32).astype(BF16)
 
 
 STIFF_SCALE, STIFF_POWER = 1.92, 96.0
@@ -78,8 +78,15 @@
     return out
 
 
+def split(v):
+    high = v.astype(BF16)
+    return high, (v - high.astype(F32)).astype(BF16)
+
+
 def permuted(v, order):
-    return jnp.dot(v, order, precision=lax.Precision.HIGHEST, preferred_element_type=F32)
+    n = v.shape[0]
+    moved = jnp.dot(jnp.concatenate(split(v), axis=0), order, preferred_element_type=F32)
+    return moved[:n] + moved[n:]
 
 
 def planes_of(state, density, stiffness, mass):
@@ -155,11 +162,6 @@
         out[4 * rows : 4 * rows + 16, :] = jnp.concatenate(info + scale + [jnp.zeros((6, cy), F32)], axis=0).astype(BF16)
         beside = edges[1] if s == 1 else edges[0] if s == n_j - 1 else jnp.zeros((16, cy), BF16)
         out[4 * rows + 16 :, :] = beside
-
-
-def split(v):
-    high = v.astype(BF16)
-    return high, (v - high.astype(F32)).astype(BF16)
 
 
 def sweep_kernel(n_i, n_j, cap, omega, *refs):

time: 70.6 us -> 68.7 us (0.973)
  Pallas kernels: 29.9 us -> 28 us
    pallas_call x1, Pallas kernels: 3.48 us -> 2.52 us  [gathered(): pl.pallas_call(functools.partial(pack_kernel, n_j), out_shape=[message] *...]
    pallas_call x1, Pallas kernels: 19.8 us -> 18.9 us  [gathered(): pl.pallas_call(functools.partial(sweep_kernel, n_i, n_j, cap), out_shape=...]
where the time goes in v5:
time: 68.7 us; the launch traced here: 68.3 us
  Pallas kernels  28 us (41%)
  starting transfers between devices  20.4 us (30%)
  waiting for transfers between devices  14.9 us (22%)
  local copies, waits for them, and re-layouts  3.51 us (5%)
  between operations  1.48 us (2%)
    pallas_call x1, Pallas kernels, gathered(): pl.pallas_call(functools.partial(sweep_kernel, n_i, n_j, cap), out_shape=...  18.9 us
    ppermute x3, starting transfers between devices, gathered(): parts[s] = lax.ppermute(outs[s], 'my', [(a, a ^ s) for a in range(PARTS)])  11 us
    ppermute x3, waiting for transfers between devices, gathered(): msgs.append(lax.ppermute(own[s], 'my', pairs))  8.29 us
    ppermute x3, starting transfers between devices, gathered(): msgs.append(lax.ppermute(own[s], 'my', pairs))  5.21 us
    ppermute x3, waiting for transfers between devices, gathered(): lax.ppermute(sens, 'freq', [(a, (a + s) % size) for a in range(size)])  5.05 us
    ppermute x3, starting transfers between devices, gathered(): lax.ppermute(sens, 'freq', [(a, (a + s) % size) for a in range(size)])  3.54 us
    unnamed x28, local copies, waits for them, and re-layouts  3.51 us
    pallas_call x1, Pallas kernels, gathered(): pl.pallas_call(functools.partial(response_kernel, n_j), out_shape=[jax.Sh...  2.59 us
  transfers between devices with their start and end apart: 14, of which 7 were waited for; matrix products, arithmetic and copies ran while one was open for 0% of the time, Pallas kernels for 4%

profile of v5, /device:TPU:8, one launch (start us, length us, event | category | flops | bytes accessed | tf_op | source)
XLA Modules:
  0.0 68.3 jit_solution(5306926161478511326)
XLA Ops:
  0.6 2.5 %pack.1 = (bf16[288,256]{1,0:T(8,128)(2,1)}, bf16[288,256]{1,0:T(8,128)(2,1)}, bf16[288,256]{1,0:T(8,128)(2,1)}, bf16[288,256]{1,0:T(8,128)(2,1)}, f32[16,128]{1...) custom-call(f32[6,64,256]{2,1,0:T(8,128)} %bitcast.5, f32[64,256]{1,0:T(8,128)} %density.5, f32[64,256]{1,0:T(8,128)} %stiffness.3, ...), custom_call_target="tpu_custom_call" | custom-call | tf_op jit(solution)/shard_map/pack/pallas_call | solution.py:503
  3.1 1.6 %collective-permute-start.1 = (bf16[288,256]{1,0:T(8,128)(2,1)}, bf16[288,256]{1,0:T(8,128)(2,1)S(1)}, u32[]{:S(2)}, u32[]{:S(2)}) collective-permute-start(bf16[288,256]{1,0:T(8,128)(2,1)} %get-tuple-element.21), channel_id=1, source_target_pairs={{0,1},{1,2},{2,3},{3,0},{4,5},{5,6},{6,7},{7,4},{8,9},{9,10},{10,1... | collective-permute-start | bytes 442376 | tf_op jit(solution)/shard_map/ppermute | solution.py:515
  4.7 2.3 %collective-permute-start.2 = (bf16[288,256]{1,0:T(8,128)(2,1)}, bf16[288,256]{1,0:T(8,128)(2,1)S(1)}, u32[]{:S(2)}, u32[]{:S(2)}) collective-permute-start(bf16[288,256]{1,0:T(8,128)(2,1)} %get-tuple-element.22), channel_id=1, source_target_pairs={{1,0},{2,1},{3,2},{5,4},{6,5},{7,6},{9,8},{10,9},{11,10},{13,12},{... | collective-permute-start | bytes 442376 | tf_op jit(solution)/shard_map/ppermute | solution.py:515
  7.1 1.3 %collective-permute-start.5 = (bf16[288,256]{1,0:T(8,128)(2,1)}, bf16[288,256]{1,0:T(8,128)(2,1)S(1)}, u32[]{:S(2)}, u32[]{:S(2)}) collective-permute-start(bf16[288,256]{1,0:T(8,128)(2,1)} %get-tuple-element.26), channel_id=1, source_target_pairs={{0,2},{2,0},{3,1},{4,6},{6,4},{7,5},{8,10},{10,8},{11,9},{12,14},{... | collective-permute-start | bytes 442376 | tf_op jit(solution)/shard_map/ppermute | solution.py:515
  8.4 0.1 collective-permute-start.6
  8.5 0.5 collective-permute-done.1.west.refs_1_
  8.9 0.0 copy-start
  8.9 0.0 collective-permute-start.3
  9.0 7.8 %collective-permute-done.2.east.refs_3_ = bf16[288,256]{1,0:T(8,128)(2,1)S(1)} collective-permute-done((bf16[288,256]{1,0:T(8,128)(2,1)}, bf16[288,256]{1,0:T(8,128)(2,1)S(1)}, u32[]{:S(2)}, u32[]{:S(2)}) %collective-permute-start.2) | collective-permute-done | bytes 147488 | tf_op jit(solution)/shard_map/ppermute | solution.py:515
  16.8 0.0 copy-start.1
  16.8 0.0 collective-permute-start.4
  16.8 0.0 collective-permute-done.5.refs_2_
  16.8 0.5 collective-permute-start.7
  17.9 0.0 collective-permute-done.6.refs_4_
  17.9 0.0 collective-permute-done.3.refs_0_.refs_5_
  17.9 0.0 copy-start.2
  18.0 0.2 collective-permute-done.4.refs_1_.refs_7_
  18.1 0.0 copy-start.3
  18.1 0.2 collective-permute-done.7.refs_6_
  18.3 0.0 copy-start.5
  18.3 0.9 %copy-done.5 = bf16[288,256]{1,0:T(8,128)(2,1)S(1)} copy-done((bf16[288,256]{1,0:T(8,128)(2,1)S(1)}, bf16[288,256]{1,0:T(8,128)(2,1)}, u32[]{:S(2)}) %copy-start.5) | copy-done | bytes 147480
  19.2 0.0 copy-start.13
  19.3 18.9 %sweeps.1 = (f32[144,256]{1,0:T(8,128)S(1)}, bf16[144,256]{1,0:T(8,128)(2,1)S(1)}, bf16[144,256]{1,0:T(8,128)(2,1)S(1)}, bf16[144,256]{1,0:T(8,128)(2,1)S(1)}) custom-call(f32[1]{0:T(128)S(6)} %copy.11.omega, bf16[288,256]{1,0:T(8,128)(2,1)S(1)} %copy-done.5, bf16[288,256]{1,0:T(8,128)(2,1)S(1)} %collective-permute-done.1.west.refs_1_, ...), custom_call_target="tpu_custom_call" | custom-call | flops 30000001024 | bytes 4000000 | tf_op jit(solution)/shard_map/sweeps/pallas_call | solution.py:520
  38.1 0.0 copy-done
  38.1 0.0 copy-done.1
  38.1 0.0 copy-done.2
  38.2 0.0 copy-done.3
  38.2 0.0 copy-start.4
  38.2 0.7 copy-done.4
  38.8 5.7 %collective-permute-start.8 = (bf16[144,256]{1,0:T(8,128)(2,1)S(1)}, bf16[144,256]{1,0:T(8,128)(2,1)S(1)}, u32[]{:S(2)}, u32[]{:S(2)}) collective-permute-start(bf16[144,256]{1,0:T(8,128)(2,1)S(1)} %get-tuple-element.28), channel_id=1, source_target_pairs={{0,1},{1,0},{2,3},{4,5},{5,4},{6,7},{8,9},{9,8},{10,11},{12,13},{1... | collective-permute-start | bytes 221192 | tf_op jit(solution)/shard_map/ppermute | solution.py:554
  44.5 1.3 %collective-permute-start.9 = (bf16[144,256]{1,0:T(8,128)(2,1)S(1)}, bf16[144,256]{1,0:T(8,128)(2,1)S(1)}, u32[]{:S(2)}, u32[]{:S(2)}) collective-permute-start(bf16[144,256]{1,0:T(8,128)(2,1)S(1)} %get-tuple-element.29), channel_id=1, source_target_pairs={{0,2},{1,3},{2,0},{4,6},{5,7},{6,4},{8,10},{9,11},{10,8},{12,14},{... | collective-permute-start | bytes 221192 | tf_op jit(solution)/shard_map/ppermute | solution.py:554
  45.8 4.0 %collective-permute-start.10 = (bf16[144,256]{1,0:T(8,128)(2,1)S(1)}, bf16[144,256]{1,0:T(8,128)(2,1)S(1)}, u32[]{:S(2)}, u32[]{:S(2)}) collective-permute-start(bf16[144,256]{1,0:T(8,128)(2,1)S(1)} %get-tuple-element.30), channel_id=1, source_target_pairs={{0,3},{1,2},{2,1},{4,7},{5,6},{6,5},{8,11},{9,10},{10,9},{12,15},{... | collective-permute-start | bytes 221192 | tf_op jit(solution)/shard_map/ppermute | solution.py:554
  49.8 0.0 copy-done.13
  49.8 0.1 collective-permute-start
  49.9 1.2 %collective-permute-done.line = f32[32,256]{1,0:T(8,128)S(1)} collective-permute-done((f32[32,256]{1,0:T(8,128)S(1)}, f32[32,256]{1,0:T(8,128)S(1)}, u32[]{:S(2)}, u32[]{:S(2)}) %collective-permute-start) | collective-permute-done | bytes 32800 | tf_op jit(solution)/shard_map/ppermute | solution.py:518
  51.1 0.0 copy-start.12
  51.1 0.6 copy-done.12
  51.7 2.6 %response.1 = (f32[6,64,256]{2,1,0:T(8,128)}, f32[6,8,256]{2,1,0:T(8,128)}, f32[8,256]{1,0:T(8,128)}) custom-call(f32[1]{0:T(128)S(6)} %copy.11.omega, bf16[6,64,256]{2,1,0:T(8,128)(2,1)} %bitcast.4, f32[64,256]{1,0:T(8,128)} %density.5, f32[64,256]{1,0:T(8,128)} %stiffness.3, f32[64,256]{1,0:T(8,128)} %mass.3, f32[16,128]{1,0:T(8,128)} %get-tuple-element.18.first, ...), custom_call_target="tpu_custom_call" | custom-call | tf_op jit(solution)/shard_map/response/pallas_call | solution.py:556
  54.3 0.0 collective-permute-done.8.refs_1_
  54.3 0.0 copy-start.6
  54.3 0.0 collective-permute-done.9.refs_2_
  54.3 0.0 copy-start.7
  54.3 0.0 collective-permute-done.10.refs_3_
  54.3 0.0 copy-start.8
  54.3 0.6 copy-done.6
  54.9 0.0 copy-done.7
  55.0 0.0 copy-done.8
  55.0 2.1 %sensitivity.1 = (f32[6,64,256]{2,1,0:T(8,128)}, f32[72,256]{1,0:T(8,128)}) custom-call(f32[6,64,256]{2,1,0:T(8,128)} %get-tuple-element.23.inner, f32[6,8,256]{2,1,0:T(8,128)} %get-tuple-element.24.ring, f32[144,256]{1,0:T(8,128)} %copy-done.4, bf16[144,256]{1,0:T(8,128)(2,1)} %copy-done.6, bf16[144,256]{1,0:T(8,128)(2,1)} %copy-done.7, ...), custom_call_target="tpu_custom_call" | custom-call | tf_op jit(solution)/shard_map/sensitivity/pallas_call | solution.py:567
  57.1 2.4 %collective-permute-start.13 = (f32[72,256]{1,0:T(8,128)}, f32[72,256]{1,0:T(8,128)S(1)}, u32[]{:S(2)}, u32[]{:S(2)}) collective-permute-start(f32[72,256]{1,0:T(8,128)} %get-tuple-element.33.refs_0_), channel_id=1, source_target_pairs={{0,24},{8,0},{16,8},{24,16},{1,25},{9,1},{17,9},{25,17},{2,26},{10... | collective-permute-start | bytes 221192 | tf_op jit(solution)/shard_map/ppermute | solution.py:580
  59.5 0.5 collective-permute-start.12
  60.1 0.6 collective-permute-start.11
  60.6 1.9 %collective-permute-done.13.refs_3_ = f32[72,256]{1,0:T(8,128)S(1)} collective-permute-done((f32[72,256]{1,0:T(8,128)}, f32[72,256]{1,0:T(8,128)S(1)}, u32[]{:S(2)}, u32[]{:S(2)}) %collective-permute-start.13) | collective-permute-done | bytes 73760 | tf_op jit(solution)/shard_map/ppermute | solution.py:580
  62.5 0.0 copy-start.9
  62.5 3.2 %collective-permute-done.12.refs_2_ = f32[72,256]{1,0:T(8,128)S(1)} collective-permute-done((f32[72,256]{1,0:T(8,128)}, f32[72,256]{1,0:T(8,128)S(1)}, u32[]{:S(2)}, u32[]{:S(2)}) %collective-permute-start.12) | collective-permute-done | bytes 73760 | tf_op jit(solution)/shard_map/ppermute | solution.py:580
  65.7 0.0 copy-start.10
  65.7 0.0 collective-permute-done.11.refs_1_
  65.7 0.0 copy-start.11
  65.7 0.0 copy-done.9
  65.7 0.6 copy-done.10
  66.3 0.0 copy-done.11
  66.4 1.9 %filter.1 = f32[64,256]{1,0:T(8,128)} custom-call(f32[64,256]{1,0:T(8,128)} %density.5, f32[8,256]{1,0:T(8,128)} %get-tuple-element.32.ring, f32[72,256]{1,0:T(8,128)} %get-tuple-element.33.refs_0_, f32[72,256]{1,0:T(8,128)} %copy-done.11, f32[72,256]{1,0:T(8,128)} %copy-done.10, f32[72,256]{1,0:T(8,128)} %copy-done.9), custom_call_target="tpu_custom_call" | custom-call | tf_op jit(solution)/shard_map/filter/pallas_call | solution.py:581
Async XLA Ops:
  3.1 5.8 %collective-permute-start.1 = (bf16[288,256]{1,0:T(8,128)(2,1)}, bf16[288,256]{1,0:T(8,128)(2,1)S(1)}, u32[]{:S(2)}, u32[]{:S(2)}) collective-permute-start(bf16[288,256]{1,0:T(8,128)(2,1)} %get-tuple-element.21), channel_id=1, source_target_pairs={{0,1},{1,2},{2,3},{3,0},{4,5},{5,6},{6,7},{7,4},{8,9},{9,10},{10,1... | collective-permute-start | bytes 442376 | tf_op jit(solution)/shard_map/ppermute | solution.py:515
  4.7 12.0 %collective-permute-start.2 = (bf16[288,256]{1,0:T(8,128)(2,1)}, bf16[288,256]{1,0:T(8,128)(2,1)S(1)}, u32[]{:S(2)}, u32[]{:S(2)}) collective-permute-start(bf16[288,256]{1,0:T(8,128)(2,1)} %get-tuple-element.22), channel_id=1, source_target_pairs={{1,0},{2,1},{3,2},{5,4},{6,5},{7,6},{9,8},{10,9},{11,10},{13,12},{... | collective-permute-start | bytes 442376 | tf_op jit(solution)/shard_map/ppermute | solution.py:515
  7.1 9.7 %collective-permute-start.5 = (bf16[288,256]{1,0:T(8,128)(2,1)}, bf16[288,256]{1,0:T(8,128)(2,1)S(1)}, u32[]{:S(2)}, u32[]{:S(2)}) collective-permute-start(bf16[288,256]{1,0:T(8,128)(2,1)} %get-tuple-element.26), channel_id=1, source_target_pairs={{0,2},{2,0},{3,1},{4,6},{6,4},{7,5},{8,10},{10,8},{11,9},{12,14},{... | collective-permute-start | bytes 442376 | tf_op jit(solution)/shard_map/ppermute | solution.py:515
  8.4 9.5 %collective-permute-start.6 = (bf16[288,256]{1,0:T(8,128)(2,1)}, bf16[288,256]{1,0:T(8,128)(2,1)S(1)}, u32[]{:S(2)}, u32[]{:S(2)}) collective-permute-start(bf16[288,256]{1,0:T(8,128)(2,1)} %get-tuple-element.25.refs_0_), channel_id=1, source_target_pairs={{0,4},{4,0},{1,5},{5,1},{2,6},{6,2},{3,7},{7,3},{8,12},{12,8},{9,1... | collective-permute-start | bytes 442376 | tf_op jit(solution)/shard_map/ppermute | solution.py:517
  8.9 29.2 %copy-start = (bf16[288,256]{1,0:T(8,128)(2,1)}, bf16[288,256]{1,0:T(8,128)(2,1)S(1)}, u32[]{:S(2)}) copy-start(bf16[288,256]{1,0:T(8,128)(2,1)S(1)} %collective-permute-done.1.west.refs_1_) | copy-start | bytes 442372
  8.9 9.0 %collective-permute-start.3 = (bf16[288,256]{1,0:T(8,128)(2,1)S(1)}, bf16[288,256]{1,0:T(8,128)(2,1)S(1)}, u32[]{:S(2)}, u32[]{:S(2)}) collective-permute-start(bf16[288,256]{1,0:T(8,128)(2,1)S(1)} %collective-permute-done.1.west.refs_1_), channel_id=1, source_target_pairs={{0,4},{4,0},{1,5},{5,1},{2,6},{6,2},{3,7},{7,3},{8,12},{12,8},{9,1... | collective-permute-start | bytes 442376 | tf_op jit(solution)/shard_map/ppermute | solution.py:517
  16.8 21.4 %copy-start.1 = (bf16[288,256]{1,0:T(8,128)(2,1)}, bf16[288,256]{1,0:T(8,128)(2,1)S(1)}, u32[]{:S(2)}) copy-start(bf16[288,256]{1,0:T(8,128)(2,1)S(1)} %collective-permute-done.2.east.refs_3_) | copy-start | bytes 442372
  16.8 1.4 %collective-permute-start.4 = (bf16[288,256]{1,0:T(8,128)(2,1)S(1)}, bf16[288,256]{1,0:T(8,128)(2,1)S(1)}, u32[]{:S(2)}, u32[]{:S(2)}) collective-permute-start(bf16[288,256]{1,0:T(8,128)(2,1)S(1)} %collective-permute-done.2.east.refs_3_), channel_id=1, source_target_pairs={{0,4},{4,0},{1,5},{5,1},{2,6},{6,2},{3,7},{7,3},{8,12},{12,8},{9,1... | collective-permute-start | bytes 442376 | tf_op jit(solution)/shard_map/ppermute | solution.py:517
  16.8 1.6 %collective-permute-start.7 = (bf16[288,256]{1,0:T(8,128)(2,1)S(1)}, bf16[288,256]{1,0:T(8,128)(2,1)S(1)}, u32[]{:S(2)}, u32[]{:S(2)}) collective-permute-start(bf16[288,256]{1,0:T(8,128)(2,1)S(1)} %collective-permute-done.5.refs_2_), channel_id=1, source_target_pairs={{0,4},{4,0},{1,5},{5,1},{2,6},{6,2},{3,7},{7,3},{8,12},{12,8},{9,1... | collective-permute-start | bytes 442376 | tf_op jit(solution)/shard_map/ppermute | solution.py:517
  17.9 20.2 %copy-start.2 = (bf16[288,256]{1,0:T(8,128)(2,1)}, bf16[288,256]{1,0:T(8,128)(2,1)S(1)}, u32[]{:S(2)}) copy-start(bf16[288,256]{1,0:T(8,128)(2,1)S(1)} %collective-permute-done.3.refs_0_.refs_5_) | copy-start | bytes 442372
  18.1 20.0 %copy-start.3 = (bf16[288,256]{1,0:T(8,128)(2,1)}, bf16[288,256]{1,0:T(8,128)(2,1)S(1)}, u32[]{:S(2)}) copy-start(bf16[288,256]{1,0:T(8,128)(2,1)S(1)} %collective-permute-done.4.refs_1_.refs_7_) | copy-start | bytes 442372
  18.3 0.9 %copy-start.5 = (bf16[288,256]{1,0:T(8,128)(2,1)S(1)}, bf16[288,256]{1,0:T(8,128)(2,1)}, u32[]{:S(2)}) copy-start(bf16[288,256]{1,0:T(8,128)(2,1)} %get-tuple-element.25.refs_0_) | copy-start | bytes 442372
  19.2 30.6 %copy-start.13 = (f32[32,256]{1,0:T(8,128)S(1)}, f32[32,256]{1,0:T(8,128)}, u32[]{:S(2)}) copy-start(f32[32,256]{1,0:T(8,128)} %get-tuple-element.20) | copy-start | bytes 98308
  38.2 0.7 copy-start.4
  38.8 15.5 %collective-permute-start.8 = (bf16[144,256]{1,0:T(8,128)(2,1)S(1)}, bf16[144,256]{1,0:T(8,128)(2,1)S(1)}, u32[]{:S(2)}, u32[]{:S(2)}) collective-permute-start(bf16[144,256]{1,0:T(8,128)(2,1)S(1)} %get-tuple-element.28), channel_id=1, source_target_pairs={{0,1},{1,0},{2,3},{4,5},{5,4},{6,7},{8,9},{9,8},{10,11},{12,13},{1... | collective-permute-start | bytes 221192 | tf_op jit(solution)/shard_map/ppermute | solution.py:554
  44.5 9.8 %collective-permute-start.9 = (bf16[144,256]{1,0:T(8,128)(2,1)S(1)}, bf16[144,256]{1,0:T(8,128)(2,1)S(1)}, u32[]{:S(2)}, u32[]{:S(2)}) collective-permute-start(bf16[144,256]{1,0:T(8,128)(2,1)S(1)} %get-tuple-element.29), channel_id=1, source_target_pairs={{0,2},{1,3},{2,0},{4,6},{5,7},{6,4},{8,10},{9,11},{10,8},{12,14},{... | collective-permute-start | bytes 221192 | tf_op jit(solution)/shard_map/ppermute | solution.py:554
  45.8 8.5 %collective-permute-start.10 = (bf16[144,256]{1,0:T(8,128)(2,1)S(1)}, bf16[144,256]{1,0:T(8,128)(2,1)S(1)}, u32[]{:S(2)}, u32[]{:S(2)}) collective-permute-start(bf16[144,256]{1,0:T(8,128)(2,1)S(1)} %get-tuple-element.30), channel_id=1, source_target_pairs={{0,3},{1,2},{2,1},{4,7},{5,6},{6,5},{8,11},{9,10},{10,9},{12,15},{... | collective-permute-start | bytes 221192 | tf_op jit(solution)/shard_map/ppermute | solution.py:554
  49.8 1.3 %collective-permute-start = (f32[32,256]{1,0:T(8,128)S(1)}, f32[32,256]{1,0:T(8,128)S(1)}, u32[]{:S(2)}, u32[]{:S(2)}) collective-permute-start(f32[32,256]{1,0:T(8,128)S(1)} %copy-done.13), channel_id=1, source_target_pairs={{0,4},{4,0},{1,5},{5,1},{2,6},{6,2},{3,7},{7,3},{8,12},{12,8},{9,1... | collective-permute-start | bytes 98312 | tf_op jit(solution)/shard_map/ppermute | solution.py:518
  51.1 0.6 copy-start.12
  54.3 0.6 copy-start.6
  54.3 0.6 copy-start.7
  54.3 0.6 copy-start.8
  57.1 5.4 %collective-permute-start.13 = (f32[72,256]{1,0:T(8,128)}, f32[72,256]{1,0:T(8,128)S(1)}, u32[]{:S(2)}, u32[]{:S(2)}) collective-permute-start(f32[72,256]{1,0:T(8,128)} %get-tuple-element.33.refs_0_), channel_id=1, source_target_pairs={{0,24},{8,0},{16,8},{24,16},{1,25},{9,1},{17,9},{25,17},{2,26},{10... | collective-permute-start | bytes 221192 | tf_op jit(solution)/shard_map/ppermute | solution.py:580
  59.5 6.1 %collective-permute-start.12 = (f32[72,256]{1,0:T(8,128)}, f32[72,256]{1,0:T(8,128)S(1)}, u32[]{:S(2)}, u32[]{:S(2)}) collective-permute-start(f32[72,256]{1,0:T(8,128)} %get-tuple-element.33.refs_0_), channel_id=1, source_target_pairs={{0,16},{8,24},{16,0},{24,8},{1,17},{9,25},{17,1},{25,9},{2,18},{10... | collective-permute-start | bytes 221192 | tf_op jit(solution)/shard_map/ppermute | solution.py:580
  60.1 5.6 %collective-permute-start.11 = (f32[72,256]{1,0:T(8,128)}, f32[72,256]{1,0:T(8,128)S(1)}, u32[]{:S(2)}, u32[]{:S(2)}) collective-permute-start(f32[72,256]{1,0:T(8,128)} %get-tuple-element.33.refs_0_), channel_id=1, source_target_pairs={{0,8},{8,16},{16,24},{24,0},{1,9},{9,17},{17,25},{25,1},{2,10},{10... | collective-permute-start | bytes 221192 | tf_op jit(solution)/shard_map/ppermute | solution.py:580
  62.5 3.2 %copy-start.9 = (f32[72,256]{1,0:T(8,128)}, f32[72,256]{1,0:T(8,128)S(1)}, u32[]{:S(2)}) copy-start(f32[72,256]{1,0:T(8,128)S(1)} %collective-permute-done.13.refs_3_) | copy-start | bytes 221188
  65.7 0.6 copy-start.10
  65.7 0.7 copy-start.11

commit v6 on v5

--- a/solution.py
+++ b/solution.py
@@ -9,6 +9,8 @@
 
 ITERS = 20
 PARTS = 3
+SMALL_VMEM = 8 * 1024 * 1024
+SWEEP_VMEM = 16 * 1024 * 1024
 FINE = 2
 LANES = 128
 F32 = jnp.float32
@@ -432,10 +434,7 @@
         inner[c], inner[PARTS + c] = t
 
 
-def sens_kernel(inner, ring, *refs):
-    *msgs, field, sens = refs
-    rows = inner.shape[1]
-    sens[...] = jnp.zeros_like(sens)
+def for_each_part(msgs, rows, use):
     for s, msg in enumerate(msgs):
         c = lax.axis_index("my") ^ s
 
@@ -445,12 +444,31 @@
             if msg.dtype == BF16:
                 scale = planes[2 * rows :].astype(F32)
                 planes = decoded(planes, scale[3:4] + scale[4:5] + scale[5:6])
-            re, im = planes[:rows], planes[rows : 2 * rows]
-            field[c] = re
-            field[PARTS + c] = im
-            sens[:rows, :] -= re * inner[c] - im * inner[PARTS + c]
-            re, im = planes[2 * rows : 2 * rows + 8], planes[2 * rows + 8 :]
-            sens[rows:, :] -= re * ring[c] - im * ring[PARTS + c]
+            use(c, planes)
+
+
+def sens_kernel(inner, ring, *refs):
+    *msgs, sens = refs
+    rows = inner.shape[1]
+    sens[...] = jnp.zeros_like(sens)
+
+    def use(c, planes):
+        re, im = planes[:rows], planes[rows : 2 * rows]
+        sens[:rows, :] -= re * inner[c] - im * inner[PARTS + c]
+        re, im = planes[2 * rows : 2 * rows + 8], planes[2 * rows + 8 :]
+        sens[rows:, :] -= re * ring[c] - im * ring[PARTS + c]
+
+    for_each_part(msgs, rows, use)
+
+
+def field_kernel(*refs):
+    *msgs, field = refs
+    rows = field.shape[1]
+
+    def use(c, planes):
+        field[c], field[PARTS + c] = planes[:rows], planes[rows : 2 * rows]
+
+    for_each_part(msgs, rows, use)
 
 
 def filter_kernel(density, ring, *refs):
@@ -545,7 +563,7 @@
             pltpu.VMEM((blocks, 2, rows, cy), F32),
             pltpu.VMEM((2, blocks, slots), F32),
         ],
-        compiler_params=pltpu.CompilerParams(vmem_limit_bytes=40 * 1024 * 1024),
+        compiler_params=pltpu.CompilerParams(vmem_limit_bytes=SWEEP_VMEM),
         cost_estimate=pl.CostEstimate(flops=30_000_000_000, bytes_accessed=4_000_000, transcendentals=0),
         name="sweeps",
     )(omega, *msgs)
@@ -562,27 +580,35 @@
         ],
         in_specs=[smem()] + [vmem()] * 11,
         out_specs=[vmem()] * 3,
+        compiler_params=pltpu.CompilerParams(vmem_limit_bytes=SMALL_VMEM),
         name="response",
     )(omega, *planes, first, last, line, msgs[1], msgs[n_j - 1], msgs[n_j + 1], msgs[2 * n_j - 1])
-    field, sens = pl.pallas_call(
+    sens = pl.pallas_call(
         sens_kernel,
-        out_shape=[
-            jax.ShapeDtypeStruct((2 * PARTS, rows, cy), F32),
-            jax.ShapeDtypeStruct((rows + 8, cy), F32),
-        ],
+        out_shape=jax.ShapeDtypeStruct((rows + 8, cy), F32),
         in_specs=[vmem()] * (2 + n_j),
-        out_specs=[vmem()] * 2,
+        out_specs=vmem(),
+        compiler_params=pltpu.CompilerParams(vmem_limit_bytes=SMALL_VMEM),
         name="sensitivity",
     )(inner, ring, *parts)
     size = lax.axis_size("freq")
     all_freqs = [sens]
     for s in range(1, size):
         all_freqs.append(lax.ppermute(sens, "freq", [(a, (a + s) % size) for a in range(size)]))
+    field = pl.pallas_call(
+        field_kernel,
+        out_shape=jax.ShapeDtypeStruct((2 * PARTS, rows, cy), F32),
+        in_specs=[vmem()] * n_j,
+        out_specs=vmem(),
+        compiler_params=pltpu.CompilerParams(vmem_limit_bytes=SMALL_VMEM),
+        name="adjoint",
+    )(*parts)
     filtered = pl.pallas_call(
         filter_kernel,
         out_shape=jax.ShapeDtypeStruct((rows, cy), F32),
         in_specs=[vmem()] * (2 + size),
         out_specs=vmem(),
+        compiler_params=pltpu.CompilerParams(vmem_limit_bytes=SMALL_VMEM),
         name="filter",
     )(density, rho_ring, *all_freqs)
     return field.reshape(adjoint_rhs.shape), filtered

time: 68.7 us -> 62.2 us (0.905)
  Pallas kernels: 28 us -> 23.8 us
  local copies, waits for them, and re-layouts: 3.51 us -> 0.95 us
  waiting for transfers between devices: 14.9 us -> 13.2 us
  starting transfers between devices: 20.4 us -> 21.9 us
    ppermute x3, starting transfers between devices: 5.21 us -> 8.42 us  [gathered(): msgs.append(lax.ppermute(own[s], 'my', pairs))]
    unnamed x28 -> x16, local copies, waits for them, and re-layouts: 3.51 us -> 0.95 us
    pallas_call x1, Pallas kernels: 2.59 us -> 0.49 us  [gathered(): pl.pallas_call(functools.partial(response_kernel, n_j), out_shape=[jax.Sh...]
    ppermute x3, starting transfers between devices: 11 us -> 9.21 us  [gathered(): parts[s] = lax.ppermute(outs[s], 'my', [(a, a ^ s) for a in range(PARTS)])]
    ppermute x3, waiting for transfers between devices: 5.05 us -> 3.79 us  [gathered(): lax.ppermute(sens, 'freq', [(a, (a + s) % size) for a in range(size)])]
    ppermute x3, waiting for transfers between devices: 8.29 us -> 7.16 us  [gathered(): msgs.append(lax.ppermute(own[s], 'my', pairs))]
    pallas_call x1 -> x2, Pallas kernels: 2.11 us -> 1.06 us  [the longest x1 0.87 us: gathered(): pl.pallas_call(field_kernel, out_shape=jax.ShapeDtypeStruct((2 * PARTS, r...]
    pallas_call x1, Pallas kernels: 1.93 us -> 0.89 us  [gathered(): pl.pallas_call(filter_kernel, out_shape=jax.ShapeDtypeStruct((rows, cy),...]
  transfers between devices with their start and end apart: 14 -> 14, of which waited for: 7 -> 8; matrix products, arithmetic and copies ran while one was open for 0% -> 0% of each run, Pallas kernels for 4% -> 2%
where the time goes in v6:
time: 62.2 us; the launch traced here: 61.4 us
  Pallas kernels  23.8 us (38%)
  starting transfers between devices  21.9 us (35%)
  waiting for transfers between devices  13.2 us (21%)
  between operations  1.49 us (2%)
  local copies, waits for them, and re-layouts  0.95 us (2%)
    pallas_call x1, Pallas kernels, gathered(): pl.pallas_call(functools.partial(sweep_kernel, n_i, n_j, cap), out_shape=...  18.9 us
    ppermute x3, starting transfers between devices, gathered(): parts[s] = lax.ppermute(outs[s], 'my', [(a, a ^ s) for a in range(PARTS)])  9.21 us
    ppermute x3, starting transfers between devices, gathered(): msgs.append(lax.ppermute(own[s], 'my', pairs))  8.42 us
    ppermute x3, waiting for transfers between devices, gathered(): msgs.append(lax.ppermute(own[s], 'my', pairs))  7.16 us
    ppermute x3, waiting for transfers between devices, gathered(): lax.ppermute(sens, 'freq', [(a, (a + s) % size) for a in range(size)])  3.79 us
    ppermute x3, starting transfers between devices, gathered(): lax.ppermute(sens, 'freq', [(a, (a + s) % size) for a in range(size)])  3.6 us
    pallas_call x1, Pallas kernels, gathered(): pl.pallas_call(functools.partial(pack_kernel, n_j), out_shape=[message] *...  2.51 us
  transfers between devices with their start and end apart: 14, of which 8 were waited for; matrix products, arithmetic and copies ran while one was open for 0% of the time, Pallas kernels for 2%

profile of v6, /device:TPU:8, one launch (start us, length us, event | category | flops | bytes accessed | tf_op | source)
XLA Modules:
  0.0 61.4 jit_solution(14241418554128504573)
XLA Ops:
  0.6 2.5 %pack.1 = (bf16[288,256]{1,0:T(8,128)(2,1)}, bf16[288,256]{1,0:T(8,128)(2,1)}, bf16[288,256]{1,0:T(8,128)(2,1)}, bf16[288,256]{1,0:T(8,128)(2,1)}, f32[16,128]{1...) custom-call(f32[6,64,256]{2,1,0:T(8,128)} %bitcast.5, f32[64,256]{1,0:T(8,128)} %density.5, f32[64,256]{1,0:T(8,128)} %stiffness.3, ...), custom_call_target="tpu_custom_call" | custom-call | tf_op jit(solution)/shard_map/pack/pallas_call | solution.py:521
  3.1 1.6 %collective-permute-start = (bf16[288,256]{1,0:T(8,128)(2,1)}, bf16[288,256]{1,0:T(8,128)(2,1)S(1)}, u32[]{:S(2)}, u32[]{:S(2)}) collective-permute-start(bf16[288,256]{1,0:T(8,128)(2,1)} %get-tuple-element.17), channel_id=1, source_target_pairs={{0,1},{1,2},{2,3},{3,0},{4,5},{5,6},{6,7},{7,4},{8,9},{9,10},{10,1... | collective-permute-start | bytes 442376 | tf_op jit(solution)/shard_map/ppermute | solution.py:533
  4.7 1.3 %collective-permute-start.1 = (bf16[288,256]{1,0:T(8,128)(2,1)}, bf16[288,256]{1,0:T(8,128)(2,1)S(1)}, u32[]{:S(2)}, u32[]{:S(2)}) collective-permute-start(bf16[288,256]{1,0:T(8,128)(2,1)} %get-tuple-element.18), channel_id=1, source_target_pairs={{0,2},{2,0},{3,1},{4,6},{6,4},{7,5},{8,10},{10,8},{11,9},{12,14},{... | collective-permute-start | bytes 442376 | tf_op jit(solution)/shard_map/ppermute | solution.py:533
  6.0 5.6 %collective-permute-start.2 = (bf16[288,256]{1,0:T(8,128)(2,1)}, bf16[288,256]{1,0:T(8,128)(2,1)S(1)}, u32[]{:S(2)}, u32[]{:S(2)}) collective-permute-start(bf16[288,256]{1,0:T(8,128)(2,1)} %get-tuple-element.19), channel_id=1, source_target_pairs={{1,0},{2,1},{3,2},{5,4},{6,5},{7,6},{9,8},{10,9},{11,10},{13,12},{... | collective-permute-start | bytes 442376 | tf_op jit(solution)/shard_map/ppermute | solution.py:533
  11.6 0.1 collective-permute-start.3
  11.7 0.0 collective-permute-done.refs_1_.west
  11.7 0.5 collective-permute-start.4
  12.2 2.0 %collective-permute-done.1.refs_2_ = bf16[288,256]{1,0:T(8,128)(2,1)S(1)} collective-permute-done((bf16[288,256]{1,0:T(8,128)(2,1)}, bf16[288,256]{1,0:T(8,128)(2,1)S(1)}, u32[]{:S(2)}, u32[]{:S(2)}) %collective-permute-start.1) | collective-permute-done | bytes 147488 | tf_op jit(solution)/shard_map/ppermute | solution.py:533
  14.1 0.0 collective-permute-start.5
  14.1 5.2 %collective-permute-done.2.refs_3_.east = bf16[288,256]{1,0:T(8,128)(2,1)S(1)} collective-permute-done((bf16[288,256]{1,0:T(8,128)(2,1)}, bf16[288,256]{1,0:T(8,128)(2,1)S(1)}, u32[]{:S(2)}, u32[]{:S(2)}) %collective-permute-start.2) | collective-permute-done | bytes 147488 | tf_op jit(solution)/shard_map/ppermute | solution.py:533
  19.3 0.0 collective-permute-start.6
  20.0 0.0 copy-start
  20.0 0.0 copy-start.1
  20.0 0.0 copy-start.2
  20.0 0.0 copy-start.3
  20.0 0.0 collective-permute-done.3.refs_4_
  20.0 0.0 collective-permute-done.4.refs_5_.refs_0_
  20.1 0.0 collective-permute-done.5.refs_6_
  20.1 0.6 %collective-permute-done.6.refs_7_.refs_1_ = bf16[288,256]{1,0:T(8,128)(2,1)S(1)} collective-permute-done((bf16[288,256]{1,0:T(8,128)(2,1)S(1)}, bf16[288,256]{1,0:T(8,128)(2,1)S(1)}, u32[]{:S(2)}, u32[]{:S(2)}) %collective-permute-start.6) | collective-permute-done | bytes 147488 | tf_op jit(solution)/shard_map/ppermute | solution.py:535
  20.7 0.0 copy-start.6
  20.7 0.9 %copy-done.6 = bf16[288,256]{1,0:T(8,128)(2,1)S(1)} copy-done((bf16[288,256]{1,0:T(8,128)(2,1)S(1)}, bf16[288,256]{1,0:T(8,128)(2,1)}, u32[]{:S(2)}) %copy-start.6) | copy-done | bytes 147480
  21.6 0.0 copy-start.7
  21.6 0.0 copy-start.5
  21.6 18.9 %sweeps.1 = (f32[144,256]{1,0:T(8,128)S(1)}, bf16[144,256]{1,0:T(8,128)(2,1)S(1)}, bf16[144,256]{1,0:T(8,128)(2,1)S(1)}, bf16[144,256]{1,0:T(8,128)(2,1)S(1)}) custom-call(f32[1]{0:T(128)S(6)} %copy.11.omega, bf16[288,256]{1,0:T(8,128)(2,1)S(1)} %copy-done.6, bf16[288,256]{1,0:T(8,128)(2,1)S(1)} %collective-permute-done.refs_1_.west, ...), custom_call_target="tpu_custom_call" | custom-call | flops 30000001024 | bytes 4000000 | tf_op jit(solution)/shard_map/sweeps/pallas_call | solution.py:538
  40.5 0.0 copy-start.4
  40.5 2.3 %collective-permute-start.7 = (bf16[144,256]{1,0:T(8,128)(2,1)S(1)}, bf16[144,256]{1,0:T(8,128)(2,1)S(1)}, u32[]{:S(2)}, u32[]{:S(2)}) collective-permute-start(bf16[144,256]{1,0:T(8,128)(2,1)S(1)} %get-tuple-element.21), channel_id=1, source_target_pairs={{0,1},{1,0},{2,3},{4,5},{5,4},{6,7},{8,9},{9,8},{10,11},{12,13},{1... | collective-permute-start | bytes 221192 | tf_op jit(solution)/shard_map/ppermute | solution.py:572
  42.8 1.3 %collective-permute-start.8 = (bf16[144,256]{1,0:T(8,128)(2,1)S(1)}, bf16[144,256]{1,0:T(8,128)(2,1)S(1)}, u32[]{:S(2)}, u32[]{:S(2)}) collective-permute-start(bf16[144,256]{1,0:T(8,128)(2,1)S(1)} %get-tuple-element.22), channel_id=1, source_target_pairs={{0,2},{1,3},{2,0},{4,6},{5,7},{6,4},{8,10},{9,11},{10,8},{12,14},{... | collective-permute-start | bytes 221192 | tf_op jit(solution)/shard_map/ppermute | solution.py:572
  44.1 5.6 %collective-permute-start.9 = (bf16[144,256]{1,0:T(8,128)(2,1)S(1)}, bf16[144,256]{1,0:T(8,128)(2,1)S(1)}, u32[]{:S(2)}, u32[]{:S(2)}) collective-permute-start(bf16[144,256]{1,0:T(8,128)(2,1)S(1)} %get-tuple-element.23), channel_id=1, source_target_pairs={{0,3},{1,2},{2,1},{4,7},{5,6},{6,5},{8,11},{9,10},{10,9},{12,15},{... | collective-permute-start | bytes 221192 | tf_op jit(solution)/shard_map/ppermute | solution.py:572
  49.7 0.0 copy-done.7
  49.7 0.1 collective-permute-start.10
  49.8 1.2 %collective-permute-done.10.line = f32[32,256]{1,0:T(8,128)S(1)} collective-permute-done((f32[32,256]{1,0:T(8,128)S(1)}, f32[32,256]{1,0:T(8,128)S(1)}, u32[]{:S(2)}, u32[]{:S(2)}) %collective-permute-start.10) | collective-permute-done | bytes 32800 | tf_op jit(solution)/shard_map/ppermute | solution.py:536
  51.0 0.0 copy-done
  51.0 0.0 copy-done.1
  51.0 0.0 copy-done.2
  51.0 0.0 copy-done.3
  51.0 0.0 copy-done.5
  51.0 0.0 copy-done.4
  51.1 0.5 response.1
  51.6 0.0 collective-permute-done.7.refs_1_
  51.6 0.0 collective-permute-done.8.refs_2_
  51.6 0.5 collective-permute-done.9.refs_3_
  52.0 0.2 sensitivity.1.refs_0_
  52.2 2.5 %collective-permute-start.13 = (f32[72,256]{1,0:T(8,128)S(1)}, f32[72,256]{1,0:T(8,128)S(1)}, u32[]{:S(2)}, u32[]{:S(2)}) collective-permute-start(f32[72,256]{1,0:T(8,128)S(1)} %sensitivity.1.refs_0_), channel_id=1, source_target_pairs={{0,24},{8,0},{16,8},{24,16},{1,25},{9,1},{17,9},{25,17},{2,26},{10... | collective-permute-start | bytes 221192 | tf_op jit(solution)/shard_map/ppermute | solution.py:597
  54.7 0.5 collective-permute-start.12
  55.2 0.6 collective-permute-start.11
  55.8 0.9 %adjoint.1 = f32[6,64,256]{2,1,0:T(8,128)} custom-call(f32[144,256]{1,0:T(8,128)S(1)} %get-tuple-element.20.refs_0_, bf16[144,256]{1,0:T(8,128)(2,1)S(1)} %collective-permute-done.7.refs_1_, bf16[144,256]{1,0:T(8,128)(2,1)S(1)} %collective-permute-done.8.refs_2_, bf16[144,256]{1,0:T(8,128)(2,1)S(1)} %collective-permute-done.9.refs_3_), custom_call_target="tpu_custom_call" | custom-call | tf_op jit(solution)/shard_map/adjoint/pallas_call | solution.py:598
  56.7 0.2 collective-permute-done.13.refs_3_
  56.9 2.5 %collective-permute-done.12.refs_2_ = f32[72,256]{1,0:T(8,128)S(1)} collective-permute-done((f32[72,256]{1,0:T(8,128)S(1)}, f32[72,256]{1,0:T(8,128)S(1)}, u32[]{:S(2)}, u32[]{:S(2)}) %collective-permute-start.12) | collective-permute-done | bytes 73760 | tf_op jit(solution)/shard_map/ppermute | solution.py:597
  59.5 1.0 %collective-permute-done.11.refs_1_ = f32[72,256]{1,0:T(8,128)S(1)} collective-permute-done((f32[72,256]{1,0:T(8,128)S(1)}, f32[72,256]{1,0:T(8,128)S(1)}, u32[]{:S(2)}, u32[]{:S(2)}) %collective-permute-start.11) | collective-permute-done | bytes 73760 | tf_op jit(solution)/shard_map/ppermute | solution.py:597
  60.5 0.9 %filter.1 = f32[64,256]{1,0:T(8,128)} custom-call(f32[64,256]{1,0:T(8,128)S(1)} %copy-done.1, f32[8,256]{1,0:T(8,128)S(1)} %get-tuple-element.27.ring, f32[72,256]{1,0:T(8,128)S(1)} %sensitivity.1.refs_0_, f32[72,256]{1,0:T(8,128)S(1)} %collective-permute-done.11.refs_1_, f32[72,256]{1,0:T(8,128)S(1)} %collective-permute-done.12.refs_2_, ...), custom_call_target="tpu_custom_call" | custom-call | tf_op jit(solution)/shard_map/filter/pallas_call | solution.py:606
Async XLA Ops:
  3.1 8.5 %collective-permute-start = (bf16[288,256]{1,0:T(8,128)(2,1)}, bf16[288,256]{1,0:T(8,128)(2,1)S(1)}, u32[]{:S(2)}, u32[]{:S(2)}) collective-permute-start(bf16[288,256]{1,0:T(8,128)(2,1)} %get-tuple-element.17), channel_id=1, source_target_pairs={{0,1},{1,2},{2,3},{3,0},{4,5},{5,6},{6,7},{7,4},{8,9},{9,10},{10,1... | collective-permute-start | bytes 442376 | tf_op jit(solution)/shard_map/ppermute | solution.py:533
  4.7 9.4 %collective-permute-start.1 = (bf16[288,256]{1,0:T(8,128)(2,1)}, bf16[288,256]{1,0:T(8,128)(2,1)S(1)}, u32[]{:S(2)}, u32[]{:S(2)}) collective-permute-start(bf16[288,256]{1,0:T(8,128)(2,1)} %get-tuple-element.18), channel_id=1, source_target_pairs={{0,2},{2,0},{3,1},{4,6},{6,4},{7,5},{8,10},{10,8},{11,9},{12,14},{... | collective-permute-start | bytes 442376 | tf_op jit(solution)/shard_map/ppermute | solution.py:533
  6.0 13.3 %collective-permute-start.2 = (bf16[288,256]{1,0:T(8,128)(2,1)}, bf16[288,256]{1,0:T(8,128)(2,1)S(1)}, u32[]{:S(2)}, u32[]{:S(2)}) collective-permute-start(bf16[288,256]{1,0:T(8,128)(2,1)} %get-tuple-element.19), channel_id=1, source_target_pairs={{1,0},{2,1},{3,2},{5,4},{6,5},{7,6},{9,8},{10,9},{11,10},{13,12},{... | collective-permute-start | bytes 442376 | tf_op jit(solution)/shard_map/ppermute | solution.py:533
  11.6 8.5 %collective-permute-start.3 = (bf16[288,256]{1,0:T(8,128)(2,1)}, bf16[288,256]{1,0:T(8,128)(2,1)S(1)}, u32[]{:S(2)}, u32[]{:S(2)}) collective-permute-start(bf16[288,256]{1,0:T(8,128)(2,1)} %get-tuple-element.16.refs_0_), channel_id=1, source_target_pairs={{0,4},{4,0},{1,5},{5,1},{2,6},{6,2},{3,7},{7,3},{8,12},{12,8},{9,1... | collective-permute-start | bytes 442376 | tf_op jit(solution)/shard_map/ppermute | solution.py:535
  11.7 8.4 %collective-permute-start.4 = (bf16[288,256]{1,0:T(8,128)(2,1)S(1)}, bf16[288,256]{1,0:T(8,128)(2,1)S(1)}, u32[]{:S(2)}, u32[]{:S(2)}) collective-permute-start(bf16[288,256]{1,0:T(8,128)(2,1)S(1)} %collective-permute-done.refs_1_.west), channel_id=1, source_target_pairs={{0,4},{4,0},{1,5},{5,1},{2,6},{6,2},{3,7},{7,3},{8,12},{12,8},{9,1... | collective-permute-start | bytes 442376 | tf_op jit(solution)/shard_map/ppermute | solution.py:535
  14.1 5.9 %collective-permute-start.5 = (bf16[288,256]{1,0:T(8,128)(2,1)S(1)}, bf16[288,256]{1,0:T(8,128)(2,1)S(1)}, u32[]{:S(2)}, u32[]{:S(2)}) collective-permute-start(bf16[288,256]{1,0:T(8,128)(2,1)S(1)} %collective-permute-done.1.refs_2_), channel_id=1, source_target_pairs={{0,4},{4,0},{1,5},{5,1},{2,6},{6,2},{3,7},{7,3},{8,12},{12,8},{9,1... | collective-permute-start | bytes 442376 | tf_op jit(solution)/shard_map/ppermute | solution.py:535
  19.3 1.4 %collective-permute-start.6 = (bf16[288,256]{1,0:T(8,128)(2,1)S(1)}, bf16[288,256]{1,0:T(8,128)(2,1)S(1)}, u32[]{:S(2)}, u32[]{:S(2)}) collective-permute-start(bf16[288,256]{1,0:T(8,128)(2,1)S(1)} %collective-permute-done.2.refs_3_.east), channel_id=1, source_target_pairs={{0,4},{4,0},{1,5},{5,1},{2,6},{6,2},{3,7},{7,3},{8,12},{12,8},{9,1... | collective-permute-start | bytes 442376 | tf_op jit(solution)/shard_map/ppermute | solution.py:535
  20.0 31.0 %copy-start = (bf16[1,2,3,64,256]{4,3,2,1,0:T(8,128)(2,1)S(1)}, bf16[1,2,3,64,256]{4,3,2,1,0:T(8,128)(2,1)}, u32[]{:S(2)}) copy-start(bf16[1,2,3,64,256]{4,3,2,1,0:T(8,128)(2,1)} %param.10) | copy-start | bytes 589828
  20.0 31.0 %copy-start.1 = (f32[64,256]{1,0:T(8,128)S(1)}, f32[64,256]{1,0:T(8,128)}, u32[]{:S(2)}) copy-start(f32[64,256]{1,0:T(8,128)} %density.5) | copy-start | bytes 196612
  20.0 31.0 %copy-start.2 = (f32[64,256]{1,0:T(8,128)S(1)}, f32[64,256]{1,0:T(8,128)}, u32[]{:S(2)}) copy-start(f32[64,256]{1,0:T(8,128)} %stiffness.3) | copy-start | bytes 196612
  20.0 31.0 %copy-start.3 = (f32[64,256]{1,0:T(8,128)S(1)}, f32[64,256]{1,0:T(8,128)}, u32[]{:S(2)}) copy-start(f32[64,256]{1,0:T(8,128)} %mass.3) | copy-start | bytes 196612
  20.7 0.9 %copy-start.6 = (bf16[288,256]{1,0:T(8,128)(2,1)S(1)}, bf16[288,256]{1,0:T(8,128)(2,1)}, u32[]{:S(2)}) copy-start(bf16[288,256]{1,0:T(8,128)(2,1)} %get-tuple-element.16.refs_0_) | copy-start | bytes 442372
  21.6 28.1 %copy-start.7 = (f32[32,256]{1,0:T(8,128)S(1)}, f32[32,256]{1,0:T(8,128)}, u32[]{:S(2)}) copy-start(f32[32,256]{1,0:T(8,128)} %get-tuple-element.26) | copy-start | bytes 98308
  21.6 29.4 %copy-start.5 = (f32[16,128]{1,0:T(8,128)S(1)}, f32[16,128]{1,0:T(8,128)}, u32[]{:S(2)}) copy-start(f32[16,128]{1,0:T(8,128)} %get-tuple-element.25.last) | copy-start | bytes 24580
  40.5 10.6 %copy-start.4 = (f32[16,128]{1,0:T(8,128)S(1)}, f32[16,128]{1,0:T(8,128)}, u32[]{:S(2)}) copy-start(f32[16,128]{1,0:T(8,128)} %get-tuple-element.24.first) | copy-start | bytes 24580
  40.5 11.1 %collective-permute-start.7 = (bf16[144,256]{1,0:T(8,128)(2,1)S(1)}, bf16[144,256]{1,0:T(8,128)(2,1)S(1)}, u32[]{:S(2)}, u32[]{:S(2)}) collective-permute-start(bf16[144,256]{1,0:T(8,128)(2,1)S(1)} %get-tuple-element.21), channel_id=1, source_target_pairs={{0,1},{1,0},{2,3},{4,5},{5,4},{6,7},{8,9},{9,8},{10,11},{12,13},{1... | collective-permute-start | bytes 221192 | tf_op jit(solution)/shard_map/ppermute | solution.py:572
  42.8 8.7 %collective-permute-start.8 = (bf16[144,256]{1,0:T(8,128)(2,1)S(1)}, bf16[144,256]{1,0:T(8,128)(2,1)S(1)}, u32[]{:S(2)}, u32[]{:S(2)}) collective-permute-start(bf16[144,256]{1,0:T(8,128)(2,1)S(1)} %get-tuple-element.22), channel_id=1, source_target_pairs={{0,2},{1,3},{2,0},{4,6},{5,7},{6,4},{8,10},{9,11},{10,8},{12,14},{... | collective-permute-start | bytes 221192 | tf_op jit(solution)/shard_map/ppermute | solution.py:572
  44.1 7.9 %collective-permute-start.9 = (bf16[144,256]{1,0:T(8,128)(2,1)S(1)}, bf16[144,256]{1,0:T(8,128)(2,1)S(1)}, u32[]{:S(2)}, u32[]{:S(2)}) collective-permute-start(bf16[144,256]{1,0:T(8,128)(2,1)S(1)} %get-tuple-element.23), channel_id=1, source_target_pairs={{0,3},{1,2},{2,1},{4,7},{5,6},{6,5},{8,11},{9,10},{10,9},{12,15},{... | collective-permute-start | bytes 221192 | tf_op jit(solution)/shard_map/ppermute | solution.py:572
  49.7 1.3 %collective-permute-start.10 = (f32[32,256]{1,0:T(8,128)S(1)}, f32[32,256]{1,0:T(8,128)S(1)}, u32[]{:S(2)}, u32[]{:S(2)}) collective-permute-start(f32[32,256]{1,0:T(8,128)S(1)} %copy-done.7), channel_id=1, source_target_pairs={{0,4},{4,0},{1,5},{5,1},{2,6},{6,2},{3,7},{7,3},{8,12},{12,8},{9,1... | collective-permute-start | bytes 98312 | tf_op jit(solution)/shard_map/ppermute | solution.py:536
  52.2 4.7 %collective-permute-start.13 = (f32[72,256]{1,0:T(8,128)S(1)}, f32[72,256]{1,0:T(8,128)S(1)}, u32[]{:S(2)}, u32[]{:S(2)}) collective-permute-start(f32[72,256]{1,0:T(8,128)S(1)} %sensitivity.1.refs_0_), channel_id=1, source_target_pairs={{0,24},{8,0},{16,8},{24,16},{1,25},{9,1},{17,9},{25,17},{2,26},{10... | collective-permute-start | bytes 221192 | tf_op jit(solution)/shard_map/ppermute | solution.py:597
  54.7 4.7 %collective-permute-start.12 = (f32[72,256]{1,0:T(8,128)S(1)}, f32[72,256]{1,0:T(8,128)S(1)}, u32[]{:S(2)}, u32[]{:S(2)}) collective-permute-start(f32[72,256]{1,0:T(8,128)S(1)} %sensitivity.1.refs_0_), channel_id=1, source_target_pairs={{0,16},{8,24},{16,0},{24,8},{1,17},{9,25},{17,1},{25,9},{2,18},{10... | collective-permute-start | bytes 221192 | tf_op jit(solution)/shard_map/ppermute | solution.py:597
  55.2 5.3 %collective-permute-start.11 = (f32[72,256]{1,0:T(8,128)S(1)}, f32[72,256]{1,0:T(8,128)S(1)}, u32[]{:S(2)}, u32[]{:S(2)}) collective-permute-start(f32[72,256]{1,0:T(8,128)S(1)} %sensitivity.1.refs_0_), channel_id=1, source_target_pairs={{0,8},{8,16},{16,24},{24,0},{1,9},{9,17},{17,25},{25,1},{2,10},{10... | collective-permute-start | bytes 221192 | tf_op jit(solution)/shard_map/ppermute | solution.py:597

commit v7 on v6

--- a/solution.py
+++ b/solution.py
@@ -187,18 +187,19 @@
         at = lax.broadcasted_iota(jnp.int32, (depth, slots), 0)
         return (jnp.broadcast_to(line.astype(jnp.int32), at.shape) == at).astype(F32)
 
-    for b in range(blocks):
-        line = info[b]
-        line = pltpu.roll(line, b * cap, 1) if b else line
+    turned = [pltpu.roll(info[b], b * cap, 1) if b else info[b] for b in range(blocks)]
+    columns = [line[3:4] for line in turned] + [jnp.zeros((LANES - blocks, slots), F32)]
+    columns = jnp.transpose(jnp.concatenate(columns, axis=0))
+    lane_cy = lax.broadcasted_iota(jnp.int32, (slots, cy), 1).astype(F32)
+    for b, line in enumerate(turned):
         pick[b] = one_hot(line[1:2], cy).astype(BF16)
         rowmask[b] = one_hot(line[0:1], rows)
         row_out = one_hot(line[2:3], rows)
         spread[b] = row_out.astype(BF16)
-        lane_out = jnp.transpose(one_hot(line[3:4], cy)).astype(BF16)
-        place[b] = lane_out
+        place[b] = (jnp.broadcast_to(columns[:, b : b + 1], (slots, cy)) == lane_cy).astype(F32).astype(BF16)
         group[b] = (chunk == (source + b) % blocks).astype(F32)
         high, low = split(row_out * (line[4:5] + line[5:6] + line[6:7]))
-        both = jnp.dot(jnp.concatenate([high, low], axis=0), lane_out, preferred_element_type=F32)
+        both = jnp.dot(jnp.concatenate([high, low], axis=0), place[b], preferred_element_type=F32)
         gain[b] = both[:rows] + both[rows:]
 
     for msg, b in zip(msgs, index):
@@ -215,13 +216,14 @@
         start[b, 0], start[b, 1] = first_re, first_im
         field_a[b, 0], field_a[b, 1] = first_re, first_im
 
-    for b in range(blocks):
-        line = info[b]
-        line = pltpu.roll(line, b * cap, 1) if b else line
-        lane_out = one_hot(line[3:4], cy).astype(BF16)
-        found = jnp.dot(jnp.concatenate(split(inverse[b]), axis=0), lane_out, preferred_element_type=F32)
-        found = (found[:rows] + found[rows:]) * one_hot(line[2:3], rows)
-        found = jnp.sum(found, axis=0, keepdims=True)
+    for b, line in enumerate(turned):
+        at_target = lax.dot_general(
+            jnp.concatenate(split(inverse[b]), axis=0),
+            place[b],
+            (((1,), (1,)), ((), ())),
+            preferred_element_type=F32,
+        )
+        found = jnp.sum((at_target[:rows] + at_target[rows:]) * one_hot(line[2:3], rows), axis=0, keepdims=True)
         weights[pl.ds(b, 1), :] = (line[4:5] + line[5:6] + line[6:7]) * found
 
     row8 = lax.broadcasted_iota(jnp.int32, (8, LANES), 0)

time: 62.2 us -> 62 us (level)
  no operation moved by 1% of the time
where the time goes in v7:
time: 62 us; the launch traced here: 61.2 us
  Pallas kernels  23.6 us (38%)
  starting transfers between devices  21.9 us (35%)
  waiting for transfers between devices  13.2 us (21%)
  between operations  1.49 us (2%)
  local copies, waits for them, and re-layouts  0.95 us (2%)
    pallas_call x1, Pallas kernels, gathered(): pl.pallas_call(functools.partial(sweep_kernel, n_i, n_j, cap), out_shape=...  18.7 us
    ppermute x3, starting transfers between devices, gathered(): parts[s] = lax.ppermute(outs[s], 'my', [(a, a ^ s) for a in range(PARTS)])  9.21 us
    ppermute x3, starting transfers between devices, gathered(): msgs.append(lax.ppermute(own[s], 'my', pairs))  8.42 us
    ppermute x3, waiting for transfers between devices, gathered(): msgs.append(lax.ppermute(own[s], 'my', pairs))  7.16 us
    ppermute x3, waiting for transfers between devices, gathered(): lax.ppermute(sens, 'freq', [(a, (a + s) % size) for a in range(size)])  3.78 us
    ppermute x3, starting transfers between devices, gathered(): lax.ppermute(sens, 'freq', [(a, (a + s) % size) for a in range(size)])  3.6 us
    pallas_call x1, Pallas kernels, gathered(): pl.pallas_call(functools.partial(pack_kernel, n_j), out_shape=[message] *...  2.51 us
  transfers between devices with their start and end apart: 14, of which 8 were waited for; matrix products, arithmetic and copies ran while one was open for 0% of the time, Pallas kernels for 2%

profile of v7, /device:TPU:8, one launch (start us, length us, event | category | flops | bytes accessed | tf_op | source)
XLA Modules:
  0.0 61.2 jit_solution(4379144141871690955)
XLA Ops:
  0.6 2.5 %pack.1 = (bf16[288,256]{1,0:T(8,128)(2,1)}, bf16[288,256]{1,0:T(8,128)(2,1)}, bf16[288,256]{1,0:T(8,128)(2,1)}, bf16[288,256]{1,0:T(8,128)(2,1)}, f32[16,128]{1...) custom-call(f32[6,64,256]{2,1,0:T(8,128)} %bitcast.5, f32[64,256]{1,0:T(8,128)} %density.5, f32[64,256]{1,0:T(8,128)} %stiffness.3, ...), custom_call_target="tpu_custom_call" | custom-call | tf_op jit(solution)/shard_map/pack/pallas_call | solution.py:523
  3.1 1.6 %collective-permute-start = (bf16[288,256]{1,0:T(8,128)(2,1)}, bf16[288,256]{1,0:T(8,128)(2,1)S(1)}, u32[]{:S(2)}, u32[]{:S(2)}) collective-permute-start(bf16[288,256]{1,0:T(8,128)(2,1)} %get-tuple-element.17), channel_id=1, source_target_pairs={{0,1},{1,2},{2,3},{3,0},{4,5},{5,6},{6,7},{7,4},{8,9},{9,10},{10,1... | collective-permute-start | bytes 442376 | tf_op jit(solution)/shard_map/ppermute | solution.py:535
  4.7 1.3 %collective-permute-start.1 = (bf16[288,256]{1,0:T(8,128)(2,1)}, bf16[288,256]{1,0:T(8,128)(2,1)S(1)}, u32[]{:S(2)}, u32[]{:S(2)}) collective-permute-start(bf16[288,256]{1,0:T(8,128)(2,1)} %get-tuple-element.18), channel_id=1, source_target_pairs={{0,2},{2,0},{3,1},{4,6},{6,4},{7,5},{8,10},{10,8},{11,9},{12,14},{... | collective-permute-start | bytes 442376 | tf_op jit(solution)/shard_map/ppermute | solution.py:535
  6.0 5.6 %collective-permute-start.2 = (bf16[288,256]{1,0:T(8,128)(2,1)}, bf16[288,256]{1,0:T(8,128)(2,1)S(1)}, u32[]{:S(2)}, u32[]{:S(2)}) collective-permute-start(bf16[288,256]{1,0:T(8,128)(2,1)} %get-tuple-element.19), channel_id=1, source_target_pairs={{1,0},{2,1},{3,2},{5,4},{6,5},{7,6},{9,8},{10,9},{11,10},{13,12},{... | collective-permute-start | bytes 442376 | tf_op jit(solution)/shard_map/ppermute | solution.py:535
  11.6 0.1 collective-permute-start.3
  11.7 0.0 collective-permute-done.refs_1_.west
  11.7 0.5 collective-permute-start.4
  12.2 2.0 %collective-permute-done.1.refs_2_ = bf16[288,256]{1,0:T(8,128)(2,1)S(1)} collective-permute-done((bf16[288,256]{1,0:T(8,128)(2,1)}, bf16[288,256]{1,0:T(8,128)(2,1)S(1)}, u32[]{:S(2)}, u32[]{:S(2)}) %collective-permute-start.1) | collective-permute-done | bytes 147488 | tf_op jit(solution)/shard_map/ppermute | solution.py:535
  14.1 0.0 collective-permute-start.5
  14.1 5.2 %collective-permute-done.2.refs_3_.east = bf16[288,256]{1,0:T(8,128)(2,1)S(1)} collective-permute-done((bf16[288,256]{1,0:T(8,128)(2,1)}, bf16[288,256]{1,0:T(8,128)(2,1)S(1)}, u32[]{:S(2)}, u32[]{:S(2)}) %collective-permute-start.2) | collective-permute-done | bytes 147488 | tf_op jit(solution)/shard_map/ppermute | solution.py:535
  19.3 0.0 collective-permute-start.6
  20.0 0.0 copy-start
  20.0 0.0 copy-start.1
  20.0 0.0 copy-start.2
  20.0 0.0 copy-start.3
  20.0 0.0 collective-permute-done.3.refs_4_
  20.0 0.0 collective-permute-done.4.refs_5_.refs_0_
  20.1 0.0 collective-permute-done.5.refs_6_
  20.1 0.6 %collective-permute-done.6.refs_7_.refs_1_ = bf16[288,256]{1,0:T(8,128)(2,1)S(1)} collective-permute-done((bf16[288,256]{1,0:T(8,128)(2,1)S(1)}, bf16[288,256]{1,0:T(8,128)(2,1)S(1)}, u32[]{:S(2)}, u32[]{:S(2)}) %collective-permute-start.6) | collective-permute-done | bytes 147488 | tf_op jit(solution)/shard_map/ppermute | solution.py:537
  20.7 0.0 copy-start.6
  20.7 0.9 %copy-done.6 = bf16[288,256]{1,0:T(8,128)(2,1)S(1)} copy-done((bf16[288,256]{1,0:T(8,128)(2,1)S(1)}, bf16[288,256]{1,0:T(8,128)(2,1)}, u32[]{:S(2)}) %copy-start.6) | copy-done | bytes 147480
  21.6 0.0 copy-start.7
  21.6 0.0 copy-start.5
  21.6 18.7 %sweeps.1 = (f32[144,256]{1,0:T(8,128)S(1)}, bf16[144,256]{1,0:T(8,128)(2,1)S(1)}, bf16[144,256]{1,0:T(8,128)(2,1)S(1)}, bf16[144,256]{1,0:T(8,128)(2,1)S(1)}) custom-call(f32[1]{0:T(128)S(6)} %copy.11.omega, bf16[288,256]{1,0:T(8,128)(2,1)S(1)} %copy-done.6, bf16[288,256]{1,0:T(8,128)(2,1)S(1)} %collective-permute-done.refs_1_.west, ...), custom_call_target="tpu_custom_call" | custom-call | flops 30000001024 | bytes 4000000 | tf_op jit(solution)/shard_map/sweeps/pallas_call | solution.py:540
  40.3 0.0 copy-start.4
  40.3 2.3 %collective-permute-start.7 = (bf16[144,256]{1,0:T(8,128)(2,1)S(1)}, bf16[144,256]{1,0:T(8,128)(2,1)S(1)}, u32[]{:S(2)}, u32[]{:S(2)}) collective-permute-start(bf16[144,256]{1,0:T(8,128)(2,1)S(1)} %get-tuple-element.21), channel_id=1, source_target_pairs={{0,1},{1,0},{2,3},{4,5},{5,4},{6,7},{8,9},{9,8},{10,11},{12,13},{1... | collective-permute-start | bytes 221192 | tf_op jit(solution)/shard_map/ppermute | solution.py:574
  42.6 1.3 %collective-permute-start.8 = (bf16[144,256]{1,0:T(8,128)(2,1)S(1)}, bf16[144,256]{1,0:T(8,128)(2,1)S(1)}, u32[]{:S(2)}, u32[]{:S(2)}) collective-permute-start(bf16[144,256]{1,0:T(8,128)(2,1)S(1)} %get-tuple-element.22), channel_id=1, source_target_pairs={{0,2},{1,3},{2,0},{4,6},{5,7},{6,4},{8,10},{9,11},{10,8},{12,14},{... | collective-permute-start | bytes 221192 | tf_op jit(solution)/shard_map/ppermute | solution.py:574
  43.9 5.6 %collective-permute-start.9 = (bf16[144,256]{1,0:T(8,128)(2,1)S(1)}, bf16[144,256]{1,0:T(8,128)(2,1)S(1)}, u32[]{:S(2)}, u32[]{:S(2)}) collective-permute-start(bf16[144,256]{1,0:T(8,128)(2,1)S(1)} %get-tuple-element.23), channel_id=1, source_target_pairs={{0,3},{1,2},{2,1},{4,7},{5,6},{6,5},{8,11},{9,10},{10,9},{12,15},{... | collective-permute-start | bytes 221192 | tf_op jit(solution)/shard_map/ppermute | solution.py:574
  49.5 0.0 copy-done.7
  49.5 0.1 collective-permute-start.10
  49.6 1.2 %collective-permute-done.10.line = f32[32,256]{1,0:T(8,128)S(1)} collective-permute-done((f32[32,256]{1,0:T(8,128)S(1)}, f32[32,256]{1,0:T(8,128)S(1)}, u32[]{:S(2)}, u32[]{:S(2)}) %collective-permute-start.10) | collective-permute-done | bytes 32800 | tf_op jit(solution)/shard_map/ppermute | solution.py:538
  50.8 0.0 copy-done
  50.8 0.0 copy-done.1
  50.8 0.0 copy-done.2
  50.8 0.0 copy-done.3
  50.8 0.0 copy-done.5
  50.8 0.0 copy-done.4
  50.8 0.5 response.1
  51.3 0.0 collective-permute-done.7.refs_1_
  51.4 0.0 collective-permute-done.8.refs_2_
  51.4 0.5 collective-permute-done.9.refs_3_
  51.8 0.2 sensitivity.1.refs_0_
  52.0 2.5 %collective-permute-start.13 = (f32[72,256]{1,0:T(8,128)S(1)}, f32[72,256]{1,0:T(8,128)S(1)}, u32[]{:S(2)}, u32[]{:S(2)}) collective-permute-start(f32[72,256]{1,0:T(8,128)S(1)} %sensitivity.1.refs_0_), channel_id=1, source_target_pairs={{0,24},{8,0},{16,8},{24,16},{1,25},{9,1},{17,9},{25,17},{2,26},{10... | collective-permute-start | bytes 221192 | tf_op jit(solution)/shard_map/ppermute | solution.py:599
  54.5 0.5 collective-permute-start.12
  55.0 0.6 collective-permute-start.11
  55.6 0.9 %adjoint.1 = f32[6,64,256]{2,1,0:T(8,128)} custom-call(f32[144,256]{1,0:T(8,128)S(1)} %get-tuple-element.20.refs_0_, bf16[144,256]{1,0:T(8,128)(2,1)S(1)} %collective-permute-done.7.refs_1_, bf16[144,256]{1,0:T(8,128)(2,1)S(1)} %collective-permute-done.8.refs_2_, bf16[144,256]{1,0:T(8,128)(2,1)S(1)} %collective-permute-done.9.refs_3_), custom_call_target="tpu_custom_call" | custom-call | tf_op jit(solution)/shard_map/adjoint/pallas_call | solution.py:600
  56.5 0.2 collective-permute-done.13.refs_3_
  56.7 2.5 %collective-permute-done.12.refs_2_ = f32[72,256]{1,0:T(8,128)S(1)} collective-permute-done((f32[72,256]{1,0:T(8,128)S(1)}, f32[72,256]{1,0:T(8,128)S(1)}, u32[]{:S(2)}, u32[]{:S(2)}) %collective-permute-start.12) | collective-permute-done | bytes 73760 | tf_op jit(solution)/shard_map/ppermute | solution.py:599
  59.2 1.0 %collective-permute-done.11.refs_1_ = f32[72,256]{1,0:T(8,128)S(1)} collective-permute-done((f32[72,256]{1,0:T(8,128)S(1)}, f32[72,256]{1,0:T(8,128)S(1)}, u32[]{:S(2)}, u32[]{:S(2)}) %collective-permute-start.11) | collective-permute-done | bytes 73760 | tf_op jit(solution)/shard_map/ppermute | solution.py:599
  60.3 0.9 %filter.1 = f32[64,256]{1,0:T(8,128)} custom-call(f32[64,256]{1,0:T(8,128)S(1)} %copy-done.1, f32[8,256]{1,0:T(8,128)S(1)} %get-tuple-element.27.ring, f32[72,256]{1,0:T(8,128)S(1)} %sensitivity.1.refs_0_, f32[72,256]{1,0:T(8,128)S(1)} %collective-permute-done.11.refs_1_, f32[72,256]{1,0:T(8,128)S(1)} %collective-permute-done.12.refs_2_, ...), custom_call_target="tpu_custom_call" | custom-call | tf_op jit(solution)/shard_map/filter/pallas_call | solution.py:608
Async XLA Ops:
  3.1 8.5 %collective-permute-start = (bf16[288,256]{1,0:T(8,128)(2,1)}, bf16[288,256]{1,0:T(8,128)(2,1)S(1)}, u32[]{:S(2)}, u32[]{:S(2)}) collective-permute-start(bf16[288,256]{1,0:T(8,128)(2,1)} %get-tuple-element.17), channel_id=1, source_target_pairs={{0,1},{1,2},{2,3},{3,0},{4,5},{5,6},{6,7},{7,4},{8,9},{9,10},{10,1... | collective-permute-start | bytes 442376 | tf_op jit(solution)/shard_map/ppermute | solution.py:535
  4.7 9.4 %collective-permute-start.1 = (bf16[288,256]{1,0:T(8,128)(2,1)}, bf16[288,256]{1,0:T(8,128)(2,1)S(1)}, u32[]{:S(2)}, u32[]{:S(2)}) collective-permute-start(bf16[288,256]{1,0:T(8,128)(2,1)} %get-tuple-element.18), channel_id=1, source_target_pairs={{0,2},{2,0},{3,1},{4,6},{6,4},{7,5},{8,10},{10,8},{11,9},{12,14},{... | collective-permute-start | bytes 442376 | tf_op jit(solution)/shard_map/ppermute | solution.py:535
  6.0 13.3 %collective-permute-start.2 = (bf16[288,256]{1,0:T(8,128)(2,1)}, bf16[288,256]{1,0:T(8,128)(2,1)S(1)}, u32[]{:S(2)}, u32[]{:S(2)}) collective-permute-start(bf16[288,256]{1,0:T(8,128)(2,1)} %get-tuple-element.19), channel_id=1, source_target_pairs={{1,0},{2,1},{3,2},{5,4},{6,5},{7,6},{9,8},{10,9},{11,10},{13,12},{... | collective-permute-start | bytes 442376 | tf_op jit(solution)/shard_map/ppermute | solution.py:535
  11.6 8.5 %collective-permute-start.3 = (bf16[288,256]{1,0:T(8,128)(2,1)}, bf16[288,256]{1,0:T(8,128)(2,1)S(1)}, u32[]{:S(2)}, u32[]{:S(2)}) collective-permute-start(bf16[288,256]{1,0:T(8,128)(2,1)} %get-tuple-element.16.refs_0_), channel_id=1, source_target_pairs={{0,4},{4,0},{1,5},{5,1},{2,6},{6,2},{3,7},{7,3},{8,12},{12,8},{9,1... | collective-permute-start | bytes 442376 | tf_op jit(solution)/shard_map/ppermute | solution.py:537
  11.7 8.4 %collective-permute-start.4 = (bf16[288,256]{1,0:T(8,128)(2,1)S(1)}, bf16[288,256]{1,0:T(8,128)(2,1)S(1)}, u32[]{:S(2)}, u32[]{:S(2)}) collective-permute-start(bf16[288,256]{1,0:T(8,128)(2,1)S(1)} %collective-permute-done.refs_1_.west), channel_id=1, source_target_pairs={{0,4},{4,0},{1,5},{5,1},{2,6},{6,2},{3,7},{7,3},{8,12},{12,8},{9,1... | collective-permute-start | bytes 442376 | tf_op jit(solution)/shard_map/ppermute | solution.py:537
  14.1 5.9 %collective-permute-start.5 = (bf16[288,256]{1,0:T(8,128)(2,1)S(1)}, bf16[288,256]{1,0:T(8,128)(2,1)S(1)}, u32[]{:S(2)}, u32[]{:S(2)}) collective-permute-start(bf16[288,256]{1,0:T(8,128)(2,1)S(1)} %collective-permute-done.1.refs_2_), channel_id=1, source_target_pairs={{0,4},{4,0},{1,5},{5,1},{2,6},{6,2},{3,7},{7,3},{8,12},{12,8},{9,1... | collective-permute-start | bytes 442376 | tf_op jit(solution)/shard_map/ppermute | solution.py:537
  19.3 1.4 %collective-permute-start.6 = (bf16[288,256]{1,0:T(8,128)(2,1)S(1)}, bf16[288,256]{1,0:T(8,128)(2,1)S(1)}, u32[]{:S(2)}, u32[]{:S(2)}) collective-permute-start(bf16[288,256]{1,0:T(8,128)(2,1)S(1)} %collective-permute-done.2.refs_3_.east), channel_id=1, source_target_pairs={{0,4},{4,0},{1,5},{5,1},{2,6},{6,2},{3,7},{7,3},{8,12},{12,8},{9,1... | collective-permute-start | bytes 442376 | tf_op jit(solution)/shard_map/ppermute | solution.py:537
  20.0 30.8 %copy-start = (bf16[1,2,3,64,256]{4,3,2,1,0:T(8,128)(2,1)S(1)}, bf16[1,2,3,64,256]{4,3,2,1,0:T(8,128)(2,1)}, u32[]{:S(2)}) copy-start(bf16[1,2,3,64,256]{4,3,2,1,0:T(8,128)(2,1)} %param.10) | copy-start | bytes 589828
  20.0 30.8 %copy-start.1 = (f32[64,256]{1,0:T(8,128)S(1)}, f32[64,256]{1,0:T(8,128)}, u32[]{:S(2)}) copy-start(f32[64,256]{1,0:T(8,128)} %density.5) | copy-start | bytes 196612
  20.0 30.8 %copy-start.2 = (f32[64,256]{1,0:T(8,128)S(1)}, f32[64,256]{1,0:T(8,128)}, u32[]{:S(2)}) copy-start(f32[64,256]{1,0:T(8,128)} %stiffness.3) | copy-start | bytes 196612
  20.0 30.8 %copy-start.3 = (f32[64,256]{1,0:T(8,128)S(1)}, f32[64,256]{1,0:T(8,128)}, u32[]{:S(2)}) copy-start(f32[64,256]{1,0:T(8,128)} %mass.3) | copy-start | bytes 196612
  20.7 0.9 %copy-start.6 = (bf16[288,256]{1,0:T(8,128)(2,1)S(1)}, bf16[288,256]{1,0:T(8,128)(2,1)}, u32[]{:S(2)}) copy-start(bf16[288,256]{1,0:T(8,128)(2,1)} %get-tuple-element.16.refs_0_) | copy-start | bytes 442372
  21.6 27.9 %copy-start.7 = (f32[32,256]{1,0:T(8,128)S(1)}, f32[32,256]{1,0:T(8,128)}, u32[]{:S(2)}) copy-start(f32[32,256]{1,0:T(8,128)} %get-tuple-element.26) | copy-start | bytes 98308
  21.6 29.2 %copy-start.5 = (f32[16,128]{1,0:T(8,128)S(1)}, f32[16,128]{1,0:T(8,128)}, u32[]{:S(2)}) copy-start(f32[16,128]{1,0:T(8,128)} %get-tuple-element.25.last) | copy-start | bytes 24580
  40.3 10.6 %copy-start.4 = (f32[16,128]{1,0:T(8,128)S(1)}, f32[16,128]{1,0:T(8,128)}, u32[]{:S(2)}) copy-start(f32[16,128]{1,0:T(8,128)} %get-tuple-element.24.first) | copy-start | bytes 24580
  40.3 11.1 %collective-permute-start.7 = (bf16[144,256]{1,0:T(8,128)(2,1)S(1)}, bf16[144,256]{1,0:T(8,128)(2,1)S(1)}, u32[]{:S(2)}, u32[]{:S(2)}) collective-permute-start(bf16[144,256]{1,0:T(8,128)(2,1)S(1)} %get-tuple-element.21), channel_id=1, source_target_pairs={{0,1},{1,0},{2,3},{4,5},{5,4},{6,7},{8,9},{9,8},{10,11},{12,13},{1... | collective-permute-start | bytes 221192 | tf_op jit(solution)/shard_map/ppermute | solution.py:574
  42.6 8.7 %collective-permute-start.8 = (bf16[144,256]{1,0:T(8,128)(2,1)S(1)}, bf16[144,256]{1,0:T(8,128)(2,1)S(1)}, u32[]{:S(2)}, u32[]{:S(2)}) collective-permute-start(bf16[144,256]{1,0:T(8,128)(2,1)S(1)} %get-tuple-element.22), channel_id=1, source_target_pairs={{0,2},{1,3},{2,0},{4,6},{5,7},{6,4},{8,10},{9,11},{10,8},{12,14},{... | collective-permute-start | bytes 221192 | tf_op jit(solution)/shard_map/ppermute | solution.py:574
  43.9 7.9 %collective-permute-start.9 = (bf16[144,256]{1,0:T(8,128)(2,1)S(1)}, bf16[144,256]{1,0:T(8,128)(2,1)S(1)}, u32[]{:S(2)}, u32[]{:S(2)}) collective-permute-start(bf16[144,256]{1,0:T(8,128)(2,1)S(1)} %get-tuple-element.23), channel_id=1, source_target_pairs={{0,3},{1,2},{2,1},{4,7},{5,6},{6,5},{8,11},{9,10},{10,9},{12,15},{... | collective-permute-start | bytes 221192 | tf_op jit(solution)/shard_map/ppermute | solution.py:574
  49.5 1.3 %collective-permute-start.10 = (f32[32,256]{1,0:T(8,128)S(1)}, f32[32,256]{1,0:T(8,128)S(1)}, u32[]{:S(2)}, u32[]{:S(2)}) collective-permute-start(f32[32,256]{1,0:T(8,128)S(1)} %copy-done.7), channel_id=1, source_target_pairs={{0,4},{4,0},{1,5},{5,1},{2,6},{6,2},{3,7},{7,3},{8,12},{12,8},{9,1... | collective-permute-start | bytes 98312 | tf_op jit(solution)/shard_map/ppermute | solution.py:538
  52.0 4.7 %collective-permute-start.13 = (f32[72,256]{1,0:T(8,128)S(1)}, f32[72,256]{1,0:T(8,128)S(1)}, u32[]{:S(2)}, u32[]{:S(2)}) collective-permute-start(f32[72,256]{1,0:T(8,128)S(1)} %sensitivity.1.refs_0_), channel_id=1, source_target_pairs={{0,24},{8,0},{16,8},{24,16},{1,25},{9,1},{17,9},{25,17},{2,26},{10... | collective-permute-start | bytes 221192 | tf_op jit(solution)/shard_map/ppermute | solution.py:599
  54.5 4.7 %collective-permute-start.12 = (f32[72,256]{1,0:T(8,128)S(1)}, f32[72,256]{1,0:T(8,128)S(1)}, u32[]{:S(2)}, u32[]{:S(2)}) collective-permute-start(f32[72,256]{1,0:T(8,128)S(1)} %sensitivity.1.refs_0_), channel_id=1, source_target_pairs={{0,16},{8,24},{16,0},{24,8},{1,17},{9,25},{17,1},{25,9},{2,18},{10... | collective-permute-start | bytes 221192 | tf_op jit(solution)/shard_map/ppermute | solution.py:599
  55.0 5.3 %collective-permute-start.11 = (f32[72,256]{1,0:T(8,128)S(1)}, f32[72,256]{1,0:T(8,128)S(1)}, u32[]{:S(2)}, u32[]{:S(2)}) collective-permute-start(f32[72,256]{1,0:T(8,128)S(1)} %sensitivity.1.refs_0_), channel_id=1, source_target_pairs={{0,8},{8,16},{16,24},{24,0},{1,9},{9,17},{17,25},{25,1},{2,10},{10... | collective-permute-start | bytes 221192 | tf_op jit(solution)/shard_map/ppermute | solution.py:599
